TPU v7x, 1024 devices: a whole 8x8x8 slice. The times are simulated.
1024 devices in a mesh: seq: 32 (over y, x_hi, core), mp: 32 (over z, x_lo).
Axes of the slice: x: 8 (x_hi: 2, x_lo: 4; x = x_hi * 4 + x_lo), y: 8, z: 8, core: 2. Of those that a mesh axis runs over, the one named last changes fastest.
Arguments:
- fields: float32 [16, 256, 256, 256], P(None, 'seq', 'mp'), may hold values from -6 to 6
- lagged_source: bfloat16 [13, 256, 256, 256], P(None, 'seq', 'mp'), may hold values from -6 to 6
- embed_weight: bfloat16 [65536, 1024], P('mp'), may hold values from -0.0234375 to 0.0234375
- position: bfloat16 [4096, 1024], P('seq'), may hold values from -6 to 6
- norm_gain: float32 [1024], replicated, may hold values from 0.1 to 1.9
- head_weight: bfloat16 [1024, 45056], P(None, 'mp'), may hold values from -0.1875 to 0.1875
Outputs:
- fields_next: float32 [16, 256, 256, 256], P(None, 'seq', 'mp')
- source_terms: bfloat16 [4096, 45056], P('seq', 'mp')
All inputs are finite; a program needn't handle non-finite values.
Results may differ from a plain program's by a relative error of at most 0.0054.
Values may be sent and summed in bfloat16 or wider, within the bound.
No kernel may reach another device: no remote copies, remote signals or barrier semaphores. Data moves between devices by JAX's collectives and lax.ppermute only.
A program may use at most 64 MiB of HBM per device.

v0:
```python
import jax
import jax.numpy as jnp
from jax import lax
from jax.sharding import PartitionSpec as P

PATCH = 16


time_step = 0.25
diffusivity = 0.2
epsilon = 1e-05


def padded_2(cells, sides, width):
    for axis, dim in sides:
        count = lax.axis_size(axis)
        ends = count - 1
        head = lax.slice_in_dim(cells, 0, width, axis=dim)
        tail = lax.slice_in_dim(cells, cells.shape[dim] - width, cells.shape[dim], axis=dim)
        cells = jnp.concatenate(
            [
                lax.ppermute(tail, axis, [(i, (i + 1) % count) for i in range(ends)]),
                cells,
                lax.ppermute(head, axis, [((i + 1) % count, i) for i in range(ends)]),
            ],
            axis=dim,
        )
    return cells


def tendency(extended):
    padded = jnp.pad(extended, ((0, 0), (0, 0), (0, 0), (1, 1)))
    centre = padded[:, 1:-1, 1:-1, 1:-1]
    x_plus = padded[:, 2:, 1:-1, 1:-1]
    x_minus = padded[:, :-2, 1:-1, 1:-1]
    y_plus = padded[:, 1:-1, 2:, 1:-1]
    y_minus = padded[:, 1:-1, :-2, 1:-1]
    z_plus = padded[:, 1:-1, 1:-1, 2:]
    z_minus = padded[:, 1:-1, 1:-1, :-2]
    laplacian = x_plus + x_minus + y_plus + y_minus + z_plus + z_minus - 6.0 * centre
    advection = (
        centre[0:1] * (x_plus - x_minus)
        + centre[1:2] * (y_plus - y_minus)
        + centre[2:3] * (z_plus - z_minus)
    )
    return diffusivity * laplacian - 0.5 * advection


def shallow_cycle(values):
    return padded_2(values.astype(jnp.bfloat16), (("seq", 1), ("mp", 2)), 1).astype(values.dtype)


def advance(fields, lagged_source):
    section_one = fields + time_step * tendency(shallow_cycle(fields))
    averaged = 0.5 * (fields + section_one + time_step * tendency(shallow_cycle(section_one)))
    source = jnp.concatenate(
        [jnp.zeros((3,) + fields.shape[1:], jnp.float32), lagged_source.astype(jnp.float32)], 0
    )
    return averaged + time_step * source


def row_norm(hidden, norm_gain):
    row_mean = jnp.mean(hidden, -1, keepdims=True)
    row_square = jnp.mean(hidden * hidden, -1, keepdims=True)
    variance = row_square - row_mean * row_mean
    return ((hidden - row_mean) * lax.rsqrt(variance + epsilon) * norm_gain).astype(jnp.bfloat16)


def closure(fields, embed_weight, position, norm_gain, head_weight):
    seq_size = lax.axis_size("seq")
    mp_size = lax.axis_size("mp")
    field_count, half_patch, y_cells, depth = fields.shape
    z_groups = 2 * seq_size // mp_size
    z_rest = depth // z_groups
    groups = field_count * half_patch // mp_size
    patch_x = seq_size // 2
    patch_z = z_rest // PATCH
    width = position.shape[1]
    cells = fields.astype(jnp.bfloat16).reshape(field_count * half_patch, y_cells, z_groups, z_rest)
    arranged = cells.transpose(2, 0, 1, 3).reshape(z_groups, mp_size, groups, y_cells, z_rest)
    by_column = lax.all_to_all(arranged, "mp", split_axis=1, concat_axis=1, tiled=True)
    by_column = by_column.reshape(seq_size, 2, groups, y_cells, z_rest)
    by_token = lax.all_to_all(by_column, "seq", split_axis=0, concat_axis=0, tiled=True)
    patch_grid = by_token.reshape(patch_x, 2, 2, groups, y_cells, patch_z, PATCH)
    weight_grid = embed_weight.reshape(2, 2, groups, y_cells, PATCH, width)
    partial_value = lax.dot_general(
        patch_grid,
        weight_grid,
        (((1, 2, 3, 4, 6), (0, 1, 2, 3, 4)), ((), ())),
        preferred_element_type=jnp.float32,
    )
    partial_value = partial_value.reshape(patch_x * patch_z, width)
    summed = lax.psum(partial_value, "mp")
    normed = row_norm(summed + position.astype(jnp.float32), norm_gain)
    return jnp.dot(normed, head_weight, preferred_element_type=jnp.float32).astype(jnp.bfloat16)


def on_device(fields, lagged_source, embed_weight, position, norm_gain, head_weight):
    source_terms = closure(fields, embed_weight, position, norm_gain, head_weight)
    fields_next = advance(fields, lagged_source)
    return (fields_next, source_terms)


def solution(mesh):
    placed = (
        P(None, "seq", "mp", None),
        P(None, "seq", "mp", None),
        P("mp", None),
        P("seq", None),
        P(),
        P(None, "mp"),
    )
    return jax.shard_map(
        on_device,
        mesh=mesh,
        in_specs=placed,
        out_specs=(P(None, "seq", "mp", None), P("seq", "mp")),
        check_vma=False,
    )
```

profile of v0, /device:TPU:2, one launch (start us, length us, event | category | flops | bytes accessed | tf_op | source)
XLA Modules:
  0.0 456.3 jit_solution(5348112929637690329)
XLA Ops:
  7.2 1.4 convert_element_type.26
  8.6 0.9 copy.28
  9.5 20.2 %all-to-all-start = ((bf16[2,32,4,8,128]{4,3,2,0,1:T(8,128)(2,1)}), bf16[2,32,4,8,128]{4,3,2,0,1:T(8,128)(2,1)}, u32[]{:S(2)}, u32[]{:S(2)}) async-start(bf16[2,32,4,8,128]{4,3,2,0,1:T(8,128)(2,1)} %copy.28), calls=%async_computation | async-start | bytes 1048576 | tf_op jit(solution)/shard_map/all_to_all | solution.py:81
  29.7 1.3 collective-permute-start
  31.0 1.3 collective-permute-start.1
  32.4 4.9 %collective-permute-done.1 = bf16[16,1,8,256]{3,2,1,0:T(8,128)(2,1)S(1)} collective-permute-done((bf16[16,1,8,256]{3,2,1,0:T(8,128)(2,1)S(1)}, bf16[16,1,8,256]{3,2,1,0:T(8,128)(2,1)S(1)}, u32[]{:S(2)}, u32[]{:S(2)}) %collective-permute-start.1) | collective-permute-done | bytes 65568 | tf_op jit(solution)/shard_map/ppermute | solution.py:24
  37.5 2.2 collective-permute-start.3
  39.7 3.6 collective-permute-start.2
  43.3 2.2 collective-permute-done.3
  45.7 0.7 collective-permute-done.2
  46.5 0.7 maximum_convert_fusion
  47.2 1.5 copy-done.1
  48.7 0.7 slice_bitcast_fusion.5
  49.4 1.9 copy.29
  51.3 17.7 %all-to-all-start.1 = ((bf16[32,2,4,8,128]{4,3,2,1,0:T(8,128)(2,1)}), bf16[32,2,4,8,128]{4,3,2,1,0:T(8,128)(2,1)}, u32[]{:S(2)}, u32[]{:S(2)}) async-start(bf16[32,2,4,8,128]{4,3,2,1,0:T(8,128)(2,1)} %bitcast.9), calls=%async_computation.1 | async-start | bytes 1048576 | tf_op jit(solution)/shard_map/all_to_all | solution.py:83
  69.0 8.3 %fusion.21 = (bf16[16,8,8,256]{3,2,1,0:T(8,128)(2,1)S(1)}, f32[16,8,8,256]{3,2,1,0:T(8,128)}) fusion(f32[16,8,8,256]{3,2,1,0:T(8,128)} %param.6, f32[8,8,256]{2,1,0:T(8,128)} %get-tuple-element.13, f32[8,8,256]{2,1,0:T(8,128)S(1)} %get-tuple-element.12, f32[8,8,256]{2,1,0:T(8,128)S(1)} %get-tuple-element.11, f32[16,10,10,256]{3,2,1,0:T(8,128)} %copy-done.1), kind=kLoop, calls=%fused_computation.45 | loop fusion | flops 5505024 | bytes 10682368 | tf_op jit(solution)/shard_map/convert_element_type | solution.py:50
  77.3 2.1 collective-permute-start.4
  79.4 1.3 collective-permute-start.5
  80.7 6.9 %collective-permute-done.5 = bf16[16,1,8,256]{3,2,1,0:T(8,128)(2,1)S(1)} collective-permute-done((bf16[16,1,8,256]{3,2,1,0:T(8,128)(2,1)S(1)}, bf16[16,1,8,256]{3,2,1,0:T(8,128)(2,1)S(1)}, u32[]{:S(2)}, u32[]{:S(2)}) %collective-permute-start.5) | collective-permute-done | bytes 65568 | tf_op jit(solution)/shard_map/ppermute | solution.py:24
  87.9 1.9 collective-permute-start.7
  89.8 3.9 collective-permute-start.6
  93.7 1.2 collective-permute-done.7
  95.0 1.1 collective-permute-done.6
  96.3 2.2 maximum_convert_fusion.1
  98.5 5.4 %reshape.43 = bf16[16,2,2,4,8,8,16]{6,5,4,3,2,1,0:T(8,128)(2,1)} reshape(bf16[32,2,4,8,128]{4,3,2,1,0:T(8,128)(2,1)} %all-to-all-done.1) | data formatting | bytes 1048576 | tf_op jit(solution)/shard_map/reshape | solution.py:84
  103.9 3.6 copy.30
  107.5 8.3 %fusion.2 = f32[128,1024]{1,0:T(8,128)} fusion(bf16[2,2,4,8,16,1024]{5,4,3,2,1,0:T(8,128)(2,1)S(1)} %bitcast.32, bf16[128,2,2,4,8,16]{5,4,3,2,1,0:T(8,128)(2,1)S(1)} %bitcast.31), kind=kOutput, calls=%fused_computation.9 | convolution fusion | flops 536870912 | bytes 5242880 | tf_op jit(solution)/shard_map/dot_general | solution.py:86
  115.8 1.1 slice_bitcast_fusion.2
  116.9 8.7 %fusion.11 = f32[16,8,8,256]{3,2,1,0:T(8,128)} fusion(f32[16,10,10,256]{3,2,1,0:T(8,128)} %maximum_convert_fusion.1, f32[16,8,8,256]{3,2,1,0:T(8,128)} %param.6, f32[16,8,8,256]{3,2,1,0:T(8,128)} %get-tuple-element.7, bf16[13,8,8,256]{3,2,1,0:T(8,128)(2,1)} %param.7, f32[8,8,256]{2,1,0:T(8,128)S(1)} %get-tuple-element.10, ...), kind=kLoop, calls=%fused_computation.17 | loop fusion | flops 6553600 | bytes 11632640 | tf_op jit(solution)/shard_map/add | solution.py:59
  125.6 320.1 %all-reduce.5.cloned.1.call-done = f32[128,1024]{1,0:T(8,128)} async-done(((f32[128,1024]{1,0:T(8,128)}), f32[128,1024]{1,0:T(8,128)}) %all-reduce.5.cloned.1.call-update) | async-done | bytes 524304 | tf_op jit(solution)/shard_map/psum | solution.py:93
  445.8 1.2 fusion.20
  447.0 2.4 convolution_convert_fusion
  (28 shorter events, 1.1 us)
Async XLA Ops:
  7.2 439.8 %copy-start = (bf16[1024,1408]{1,0:T(8,128)(2,1)S(1)}, bf16[1024,1408]{1,0:T(8,128)(2,1)}, u32[]{:S(2)}) copy-start(bf16[1024,1408]{1,0:T(8,128)(2,1)} %param.11) | copy-start | bytes 8650756
  9.5 39.9 %all-to-all-start = ((bf16[2,32,4,8,128]{4,3,2,0,1:T(8,128)(2,1)}), bf16[2,32,4,8,128]{4,3,2,0,1:T(8,128)(2,1)}, u32[]{:S(2)}, u32[]{:S(2)}) async-start(bf16[2,32,4,8,128]{4,3,2,0,1:T(8,128)(2,1)} %copy.28), calls=%async_computation | async-start | bytes 1048576 | tf_op jit(solution)/shard_map/all_to_all | solution.py:81
  29.7 2.6 collective-permute-start
  31.0 6.2 %collective-permute-start.1 = (bf16[16,1,8,256]{3,2,1,0:T(8,128)(2,1)S(1)}, bf16[16,1,8,256]{3,2,1,0:T(8,128)(2,1)S(1)}, u32[]{:S(2)}, u32[]{:S(2)}) collective-permute-start(bf16[16,1,8,256]{3,2,1,0:T(8,128)(2,1)S(1)} %get-tuple-element.21), channel_id=1, source_target_pairs={{32,0},{64,32},{96,64},{128,96},{160,128},{192,160},{224,192},{256... | collective-permute-start | bytes 196616 | tf_op jit(solution)/shard_map/ppermute | solution.py:24
  37.5 8.1 %collective-permute-start.3 = (bf16[16,10,1,256]{3,0,2,1:T(8,128)(2,1)S(1)}, bf16[16,10,1,256]{3,0,2,1:T(8,128)(2,1)S(1)}, u32[]{:S(2)}, u32[]{:S(2)}) collective-permute-start(bf16[16,10,1,256]{3,0,2,1:T(8,128)(2,1)S(1)} %copy.20), channel_id=1, source_target_pairs={{1,0},{2,1},{3,2},{4,3},{5,4},{6,5},{7,6},{8,7},{9,8},{10,9},{11,1... | collective-permute-start | bytes 245768 | tf_op jit(solution)/shard_map/ppermute | solution.py:24
  39.7 6.7 %collective-permute-start.2 = (bf16[16,10,1,256]{3,0,2,1:T(8,128)(2,1)S(1)}, bf16[16,10,1,256]{3,0,2,1:T(8,128)(2,1)S(1)}, u32[]{:S(2)}, u32[]{:S(2)}) collective-permute-start(bf16[16,10,1,256]{3,0,2,1:T(8,128)(2,1)S(1)} %copy.19), channel_id=1, source_target_pairs={{0,1},{1,2},{2,3},{3,4},{4,5},{5,6},{6,7},{7,8},{8,9},{9,10},{10,1... | collective-permute-start | bytes 245768 | tf_op jit(solution)/shard_map/ppermute | solution.py:22
  47.2 1.5 copy-start.1
  51.3 47.3 %all-to-all-start.1 = ((bf16[32,2,4,8,128]{4,3,2,1,0:T(8,128)(2,1)}), bf16[32,2,4,8,128]{4,3,2,1,0:T(8,128)(2,1)}, u32[]{:S(2)}, u32[]{:S(2)}) async-start(bf16[32,2,4,8,128]{4,3,2,1,0:T(8,128)(2,1)} %bitcast.9), calls=%async_computation.1 | async-start | bytes 1048576 | tf_op jit(solution)/shard_map/all_to_all | solution.py:83
  68.9 376.9 %all-reduce.5.cloned.1.call-start = ((), (), s32[]{:S(2)}) async-start(), calls=%async_computation.2 | async-start | bytes 1048576 | tf_op jit(solution)/shard_map/psum | solution.py:93
  77.3 3.4 collective-permute-start.4
  79.4 8.2 %collective-permute-start.5 = (bf16[16,1,8,256]{3,2,1,0:T(8,128)(2,1)S(1)}, bf16[16,1,8,256]{3,2,1,0:T(8,128)(2,1)S(1)}, u32[]{:S(2)}, u32[]{:S(2)}) collective-permute-start(bf16[16,1,8,256]{3,2,1,0:T(8,128)(2,1)S(1)} %get-tuple-element.19), channel_id=1, source_target_pairs={{32,0},{64,32},{96,64},{128,96},{160,128},{192,160},{224,192},{256... | collective-permute-start | bytes 196616 | tf_op jit(solution)/shard_map/ppermute | solution.py:24
  87.9 7.0 %collective-permute-start.7 = (bf16[16,10,1,256]{3,0,2,1:T(8,128)(2,1)S(1)}, bf16[16,10,1,256]{3,0,2,1:T(8,128)(2,1)S(1)}, u32[]{:S(2)}, u32[]{:S(2)}) collective-permute-start(bf16[16,10,1,256]{3,0,2,1:T(8,128)(2,1)S(1)} %copy.24), channel_id=1, source_target_pairs={{1,0},{2,1},{3,2},{4,3},{5,4},{6,5},{7,6},{8,7},{9,8},{10,9},{11,1... | collective-permute-start | bytes 245768 | tf_op jit(solution)/shard_map/ppermute | solution.py:24
  89.8 6.3 %collective-permute-start.6 = (bf16[16,10,1,256]{3,0,2,1:T(8,128)(2,1)S(1)}, bf16[16,10,1,256]{3,0,2,1:T(8,128)(2,1)S(1)}, u32[]{:S(2)}, u32[]{:S(2)}) collective-permute-start(bf16[16,10,1,256]{3,0,2,1:T(8,128)(2,1)S(1)} %copy.23), channel_id=1, source_target_pairs={{0,1},{1,2},{2,3},{3,4},{4,5},{5,6},{6,7},{7,8},{8,9},{9,10},{10,1... | collective-permute-start | bytes 245768 | tf_op jit(solution)/shard_map/ppermute | solution.py:22
  103.9 3.6 copy-start.4
  116.9 328.9 %copy-start.2 = (bf16[128,1024]{1,0:T(8,128)(2,1)S(1)}, bf16[128,1024]{1,0:T(8,128)(2,1)}, u32[]{:S(2)}) copy-start(bf16[128,1024]{1,0:T(8,128)(2,1)} %param.9) | copy-start | bytes 786436
  116.9 330.1 %copy-start.3 = (f32[1024]{0:T(1024)S(1)}, f32[1024]{0:T(1024)}, u32[]{:S(2)}) copy-start(f32[1024]{0:T(1024)} %param.10) | copy-start | bytes 12292
Sparse Core Ops, SparseCore 0:
  115.9 329.7 all-reduce.4
where the time goes:
time: 457 us; the launch traced here: 456 us
  waiting for transfers between devices  337 us (74%)
  starting transfers between devices  55.6 us (12%)
  other arithmetic  23.2 us (5%)
  local copies, waits for them, and re-layouts  15.5 us (3%)
  between operations  14.3 us (3%)
  matrix products  10.7 us (2%)
    psum x1, waiting for transfers between devices, closure(): summed = lax.psum(partial_value, 'mp')  320 us
    all_to_all x1, starting transfers between devices, closure(): lax.all_to_all(arranged, 'mp', split_axis=1, concat_axis=1, tiled=True)  20.2 us
    all_to_all x1, starting transfers between devices, closure(): lax.all_to_all(by_column, 'seq', split_axis=0, concat_axis=0, tiled=True)  17.7 us
    ppermute x4, waiting for transfers between devices, padded_2(): lax.ppermute(head, axis, [((i + 1) % count, i) for i in range(ends)])  15.1 us
    ppermute x4, starting transfers between devices, padded_2(): lax.ppermute(tail, axis, [(i, (i + 1) % count) for i in range(ends)])  10.9 us
    convert_element_type x2, other arithmetic, shallow_cycle(): values.astype(jnp.bfloat16)  9.78 us
  transfers between devices with their start and end apart: 11, of which 7 were waited for; matrix products, arithmetic and copies ran while one was open for 5% of the time, Pallas kernels for 0%

commit v1 on v0

v1 whole, which is shorter than its diff:
```python
import jax
import jax.numpy as jnp
from jax import lax
from jax.experimental import pallas as pl
from jax.experimental.pallas import tpu as pltpu
from jax.sharding import Mesh
from jax.sharding import PartitionSpec as P

PATCH = 16
time_step = 0.25
diffusivity = 0.2
epsilon = 1e-05

F32 = jnp.float32
BF16 = jnp.bfloat16
ALL = ("sq", "core", "mp")


def block_transpose(tile):
    row = lax.broadcasted_iota(jnp.int32, (8, 128), 0)
    lane_block = lax.broadcasted_iota(jnp.int32, (8, 128), 1) // PATCH
    skewed = pltpu.roll(tile, 0, 1, stride=PATCH, stride_axis=0)
    source_row = (lane_block + row) & 7
    turned = jnp.take_along_axis(skewed, source_row, axis=0)
    unskewed = pltpu.roll(turned, 0, 1, stride=PATCH, stride_axis=0)
    return jnp.take_along_axis(unskewed, (8 - row) & 7, axis=0)


def pack_kernel(fields_ref, packed_ref, y_low_ref, y_high_ref):
    for half in range(2):
        for g in range(4):
            tiles = []
            for c in range(2):
                tile = fields_ref[0, half * 4 + g, :, c * 128 : (c + 1) * 128]
                tiles.append(block_transpose(tile))
            both = jnp.concatenate(tiles, axis=0)
            packed_ref[half, :, g * 128 : (g + 1) * 128] = both.astype(BF16)
    for k in range(2):
        y_low_ref[k, 0] = fields_ref[0, :, k, :].astype(BF16)
        y_high_ref[k, 0] = fields_ref[0, :, 6 + k, :].astype(BF16)


def pack(fields):
    return pl.pallas_call(
        pack_kernel,
        grid=(16,),
        in_specs=[pl.BlockSpec((1, 8, 8, 256), lambda f: (f, 0, 0, 0))],
        out_specs=[
            pl.BlockSpec((2, 16, 512), lambda f: (f, 0, 0)),
            pl.BlockSpec((2, 1, 8, 256), lambda f: (0, f, 0, 0)),
            pl.BlockSpec((2, 1, 8, 256), lambda f: (0, f, 0, 0)),
        ],
        out_shape=[
            jax.ShapeDtypeStruct((32, 16, 512), BF16),
            jax.ShapeDtypeStruct((2, 16, 8, 256), BF16),
            jax.ShapeDtypeStruct((2, 16, 8, 256), BF16),
        ],
        cost_estimate=pl.CostEstimate(flops=1000000, bytes_accessed=2 << 20, transcendentals=0),
    )(fields)


def embed_kernel(core_ref, patches_ref, weight_ref, out_ref):
    columns = weight_ref.shape[-1]
    total = jnp.zeros((256, columns), F32)
    for b in range(2):
        left = patches_ref[:, b].reshape(256, 512)
        total = total + jnp.dot(left, weight_ref[0, b], preferred_element_type=F32)
    total = total.reshape(16, 2, 2, 4, columns)
    for a in range(2):
        for c in range(2):
            out_ref[a, c] = total[:, c, a].astype(BF16)


def embed(patches, weight, core):
    steps = 4
    columns = 1024 // steps
    return pl.pallas_call(
        embed_kernel,
        grid_spec=pltpu.PrefetchScalarGridSpec(
            num_scalar_prefetch=1,
            grid=(steps,),
            in_specs=[
                pl.BlockSpec((16, 2, 16, 512), lambda n, core: (0, 0, 0, 0)),
                pl.BlockSpec((1, 2, 512, columns), lambda n, core: (core[0], 0, 0, n)),
            ],
            out_specs=pl.BlockSpec((2, 2, 16, 4, columns), lambda n, core: (0, 0, 0, 0, n)),
        ),
        out_shape=jax.ShapeDtypeStruct((2, 2, 16, 4, 1024), BF16),
        compiler_params=pltpu.CompilerParams(vmem_limit_bytes=32 << 20),
        cost_estimate=pl.CostEstimate(flops=540000000, bytes_accessed=3 << 20, transcendentals=0),
    )(core, patches, weight)


def advance_kernel(
    edge_ref, fields_ref, source_ref, yl_ref, yh_ref, xl_ref, xh_ref, cl_ref, ch_ref,
    out_ref, ylo, yhi, xlo, xhi, clo, chi, one_ref, face_ref,
):
    ylo[...] = yl_ref[...].astype(F32)
    yhi[...] = yh_ref[...].astype(F32)
    xlo[...] = xl_ref[...].astype(F32)
    xhi[...] = xh_ref[...].astype(F32)
    clo[...] = cl_ref[...].astype(F32)
    chi[...] = ch_ref[...].astype(F32)
    row = lax.broadcasted_iota(jnp.int32, (8, 256), 0)
    lane = lax.broadcasted_iota(jnp.int32, (8, 256), 1)
    first_row, last_row = row == 0, row == 7
    first_lane, last_lane = lane == 0, lane == 255

    def shifted(tile, low, high):
        before = jnp.where(first_row, low, pltpu.roll(tile, 1, 0))
        after = jnp.where(last_row, high, pltpu.roll(tile, 7, 0))
        return before, after

    def tendency(centre, velocity, xm, xp, ym, yp):
        zm = jnp.where(first_lane, 0.0, pltpu.roll(centre, 1, 1))
        zp = jnp.where(last_lane, 0.0, pltpu.roll(centre, 255, 1))
        laplacian = xp + xm + yp + ym + zp + zm - 6.0 * centre
        advection = velocity[0] * (xp - xm) + velocity[1] * (yp - ym) + velocity[2] * (zp - zm)
        return diffusivity * laplacian - 0.5 * advection

    def at8(f):
        return pl.ds(pl.multiple_of(f * 8, 8), 8)

    def first_stage(f, carry):
        mine = at8(f)
        for i in range(8):
            centre = fields_ref[f, i]
            xm = fields_ref[f, i - 1] if i > 0 else xlo[1, mine]
            xp = fields_ref[f, i + 1] if i < 7 else xhi[0, mine]
            low = ylo[1, pl.ds(f * 8 + i, 1)]
            high = yhi[0, pl.ds(f * 8 + i, 1)]
            ym, yp = shifted(centre, low, high)
            velocity = [fields_ref[k, i] for k in range(3)]
            one_ref[f, i] = centre + time_step * tendency(centre, velocity, xm, xp, ym, yp)
        for side in range(2):
            halo = xlo if side == 0 else xhi
            corner = clo if side == 0 else chi
            near = 1 if side == 0 else 0
            centre = halo[near, mine]
            outer = halo[1 - near, mine]
            inner = fields_ref[f, 0 if side == 0 else 7]
            xm, xp = (outer, inner) if side == 0 else (inner, outer)
            ym, yp = shifted(centre, corner[0, pl.ds(f, 1)], corner[1, pl.ds(f, 1)])
            velocity = [halo[near, k * 8 : k * 8 + 8] for k in range(3)]
            value = centre + time_step * tendency(centre, velocity, xm, xp, ym, yp)
            face_ref[side, mine] = value * edge_ref[side]
        for side in range(2):
            halo = ylo if side == 0 else yhi
            near = 1 if side == 0 else 0
            centre = halo[near, mine]
            outer = halo[1 - near, mine]
            inner = fields_ref[f, :, 0 if side == 0 else 7, :]
            ym, yp = (outer, inner) if side == 0 else (inner, outer)
            xm, xp = shifted(centre, clo[side, pl.ds(f, 1)], chi[side, pl.ds(f, 1)])
            velocity = [halo[near, k * 8 : k * 8 + 8] for k in range(3)]
            value = centre + time_step * tendency(centre, velocity, xm, xp, ym, yp)
            face_ref[2 + side, mine] = value * edge_ref[2 + side]
        return carry

    lax.fori_loop(0, 16, first_stage, 0)

    def second_stage(f, with_source):
        mine = at8(f)
        for i in range(8):
            centre = one_ref[f, i]
            xm = one_ref[f, i - 1] if i > 0 else face_ref[0, mine]
            xp = one_ref[f, i + 1] if i < 7 else face_ref[1, mine]
            low = face_ref[2, pl.ds(f * 8 + i, 1)]
            high = face_ref[3, pl.ds(f * 8 + i, 1)]
            ym, yp = shifted(centre, low, high)
            velocity = [one_ref[k, i] for k in range(3)]
            value = 0.5 * (fields_ref[f, i] + centre + time_step * tendency(centre, velocity, xm, xp, ym, yp))
            if with_source:
                value = value + time_step * source_ref[f - 3, i].astype(F32)
            out_ref[f, i] = value

    for f in range(3):
        second_stage(f, False)

    def species(f, carry):
        second_stage(f, True)
        return carry

    lax.fori_loop(3, 16, species, 0)


def advance(edges, fields, lagged_source, y_low, y_high, x_low, x_high, corner_low, corner_high):
    vmem = pl.BlockSpec(memory_space=pltpu.VMEM)
    return pl.pallas_call(
        advance_kernel,
        in_specs=[pl.BlockSpec(memory_space=pltpu.SMEM)] + [vmem] * 8,
        out_specs=vmem,
        out_shape=jax.ShapeDtypeStruct((16, 8, 8, 256), F32),
        scratch_shapes=[pltpu.VMEM((2, 128, 256), F32)] * 4
        + [pltpu.VMEM((2, 16, 256), F32)] * 2
        + [pltpu.VMEM((16, 8, 8, 256), F32), pltpu.VMEM((4, 128, 256), F32)],
        compiler_params=pltpu.CompilerParams(vmem_limit_bytes=32 << 20),
        cost_estimate=pl.CostEstimate(flops=100000000, bytes_accessed=4 << 20, transcendentals=0),
    )(edges, fields, lagged_source, y_low, y_high, x_low, x_high, corner_low, corner_high)


def along(value, axes, step):
    count = 1
    for axis in axes:
        count *= lax.axis_size(axis)
    pairs = [(i, i + step) for i in range(count) if 0 <= i + step < count]
    return lax.ppermute(value, axes, pairs)


def row_norm(hidden, norm_gain):
    row_mean = jnp.mean(hidden, -1, keepdims=True)
    row_square = jnp.mean(hidden * hidden, -1, keepdims=True)
    variance = row_square - row_mean * row_mean
    return ((hidden - row_mean) * lax.rsqrt(variance + epsilon) * norm_gain).astype(BF16)


def on_device(fields, lagged_source, embed_weight, position, norm_gain, head_weight):
    core = lax.axis_index("core")
    mp = lax.axis_index("mp")
    seq = lax.axis_index("sq") * 2 + core
    x_axes = ("sq", "core")

    packed, y_first, y_last = pack(fields)
    patches = lax.all_to_all(packed, "mp", 0, 0, tiled=True)

    y_low = along(y_last.reshape(2, 128, 256), ("mp",), 1)
    y_high = along(y_first.reshape(2, 128, 256), ("mp",), -1)

    weight = embed_weight.reshape(2, 2, 512, 1024)
    partial_sums = embed(
        patches.reshape(16, 2, 16, 512), weight, core.astype(jnp.int32).reshape(1)
    )
    pieces = lax.all_to_all(partial_sums.reshape(64, 4, 1024), ("core", "mp"), 0, 0, tiled=True)

    def x_edge(rows, which):
        cells = rows.astype(BF16).transpose(1, 0, 2, 3).reshape(2, 128, 256)
        corners = jnp.stack([side[k].reshape(16, 8, 256)[:, which] for side, k in ((y_low, 1), (y_high, 0))])
        return jnp.concatenate([cells.reshape(256, 256), corners.reshape(32, 256)], 0)

    (x_source, y_low, y_high, _) = lax.optimization_barrier((fields, y_low, y_high, partial_sums))
    x_low = along(x_edge(x_source[:, 6:8], 7), x_axes, 1)
    x_high = along(x_edge(x_source[:, 0:2], 0), x_axes, -1)

    edges = jnp.stack([seq > 0, seq < 31, mp > 0, mp < 31]).astype(F32)
    fields_next = advance(
        edges, fields, lagged_source, y_low, y_high,
        x_low[:256].reshape(2, 128, 256), x_high[:256].reshape(2, 128, 256),
        x_low[256:].reshape(2, 16, 256), x_high[256:].reshape(2, 16, 256),
    )

    rows = jnp.sum(pieces.astype(F32), 0)
    swap = [(s * 32 + m, m * 32 + s) for s in range(32) for m in range(32)]
    rows = lax.ppermute(rows, ALL, swap)
    own_position = lax.dynamic_slice_in_dim(position, mp * 4, 4, 0).astype(F32)
    normed = row_norm(rows + own_position, norm_gain)
    everyone = jnp.broadcast_to(normed[None], (32, 4, 1024))
    normed = lax.all_to_all(everyone, "mp", 0, 0, tiled=True).reshape(128, 1024)
    source_terms = jnp.dot(normed, head_weight, preferred_element_type=F32).astype(BF16)
    return fields_next, source_terms


def solution(mesh):
    split = Mesh(mesh.devices.reshape(16, 2, 32), ALL)
    seq = ("sq", "core")
    placed = (
        P(None, seq, "mp", None),
        P(None, seq, "mp", None),
        P("mp", None),
        P(seq, None),
        P(),
        P(None, "mp"),
    )
    return jax.shard_map(
        on_device,
        mesh=split,
        in_specs=placed,
        out_specs=(P(None, seq, "mp", None), P(seq, "mp")),
        check_vma=False,
    )
```

time: 457 us -> 144 us (0.32)
  the two profiles are of different devices: /device:TPU:2 before, /device:TPU:15 now
where the time goes in v1:
time: 144 us; the launch traced here: 142 us
  starting transfers between devices  70.4 us (49%)
  waiting for transfers between devices  34.1 us (24%)
  Pallas kernels  18.2 us (13%)
  local copies, waits for them, and re-layouts  11.2 us (8%)
  other arithmetic  6.21 us (4%)
    all_to_all x1, starting transfers between devices, on_device(): normed = lax.all_to_all(everyone, 'mp', 0, 0, tiled=True).reshape(128, 1024)  24.9 us
    all_to_all x1, starting transfers between devices, on_device(): patches = lax.all_to_all(packed, 'mp', 0, 0, tiled=True)  19.5 us
    ppermute x4, starting transfers between devices, along(): return lax.ppermute(value, axes, pairs)  17.3 us
    all_to_all x1, waiting for transfers between devices, on_device(): patches = lax.all_to_all(packed, 'mp', 0, 0, tiled=True)  15.8 us
    ppermute x4, waiting for transfers between devices, along(): return lax.ppermute(value, axes, pairs)  15.2 us
    pallas_call x1, Pallas kernels, pack(): pl.pallas_call(pack_kernel, grid=(16,), in_specs=[pl.BlockSpec((1, 8, 8,...  9.83 us
    all_to_all x1, starting transfers between devices, on_device(): lax.all_to_all(partial_sums.reshape(64, 4, 1024), ('core', 'mp'), 0, 0, t...  8.01 us
    pallas_call x1, Pallas kernels, advance(): pl.pallas_call(advance_kernel, in_specs=[pl.BlockSpec(memory_space=pltpu....  5.88 us
  transfers between devices with their start and end apart: 8, of which 6 were waited for; matrix products, arithmetic and copies ran while one was open for 6% of the time, Pallas kernels for 4%

profile of v1, /device:TPU:15, one launch (start us, length us, event | category | flops | bytes accessed | tf_op | source)
XLA Modules:
  0.0 142.3 jit_solution(14357317741093615069)
XLA Ops:
  0.6 9.8 %shard_map.77 = (bf16[32,16,512]{2,1,0:T(8,128)(2,1)}, bf16[2,16,8,256]{3,2,1,0:T(8,128)(2,1)}, bf16[2,16,8,256]{3,2,1,0:T(8,128)(2,1)}) custom-call(f32[16,8,8,256]{3,2,1,0:T(8,128)} %fields_ref.3), custom_call_target="tpu_custom_call" | custom-call | flops 1000000 | bytes 2097152 | tf_op jit(solution)/shard_map/pallas_call | solution.py:44
  10.5 19.5 %all-to-all-start = ((bf16[32,16,512]{2,1,0:T(8,128)(2,1)}), bf16[32,16,512]{2,1,0:T(8,128)(2,1)S(1)}, u32[]{:S(2)}, u32[]{:S(2)}) async-start(bf16[32,16,512]{2,1,0:T(8,128)(2,1)} %get-tuple-element.10), calls=%async_computation | async-start | bytes 1048576 | tf_op jit(solution)/shard_map/all_to_all | solution.py:224
  30.0 15.8 %all-to-all-done = bf16[32,16,512]{2,1,0:T(8,128)(2,1)S(1)} async-done(((bf16[32,16,512]{2,1,0:T(8,128)(2,1)}), bf16[32,16,512]{2,1,0:T(8,128)(2,1)S(1)}, u32[]{:S(2)}, u32[]{:S(2)}) %all-to-all-start) | async-done | bytes 524320 | tf_op jit(solution)/shard_map/all_to_all | solution.py:224
  45.8 2.2 %copy-done.2 = bf16[2048,1024]{1,0:T(8,128)(2,1)S(1)} copy-done((bf16[2048,1024]{1,0:T(8,128)(2,1)S(1)}, bf16[2048,1024]{1,0:T(8,128)(2,1)}, u32[]{:S(2)}) %copy-start.2) | copy-done | bytes 4194328
  48.0 2.5 %shard_map.78 = bf16[2,2,16,4,1024]{4,3,2,1,0:T(4,128)(2,1)} custom-call(s32[1]{0:T(128)} %bitcast.6.core_ref, bf16[16,2,16,512]{3,2,1,0:T(8,128)(2,1)S(1)} %bitcast.41, bf16[2,2,512,1024]{3,2,1,0:T(8,128)(2,1)S(1)} %bitcast.40), custom_call_target="tpu_custom_call" | custom-call | flops 540000000 | bytes 3145728 | tf_op jit(solution)/shard_map/pallas_call | solution.py:77
  50.5 8.0 %all-to-all-start.1 = ((bf16[64,4,1024]{2,1,0:T(4,128)(2,1)}), bf16[64,4,1024]{2,1,0:T(4,128)(2,1)}, u32[]{:S(2)}, u32[]{:S(2)}) async-start(bf16[64,4,1024]{2,1,0:T(4,128)(2,1)} %bitcast.25), calls=%async_computation.1 | async-start | bytes 1048576 | tf_op jit(solution)/shard_map/all_to_all | solution.py:233
  58.5 2.2 %collective-permute-start.1 = (bf16[2,128,256]{2,1,0:T(8,128)(2,1)}, bf16[2,128,256]{2,1,0:T(8,128)(2,1)S(1)}, u32[]{:S(2)}, u32[]{:S(2)}) collective-permute-start(bf16[2,128,256]{2,1,0:T(8,128)(2,1)} %bitcast.55), channel_id=1, source_target_pairs={{1,0},{2,1},{3,2},{4,3},{5,4},{6,5},{7,6},{8,7},{9,8},{10,9},{11,1... | collective-permute-start | bytes 393224 | tf_op jit(solution)/shard_map/ppermute | solution.py:207
  60.7 5.8 %collective-permute-start = (bf16[2,128,256]{2,1,0:T(8,128)(2,1)}, bf16[2,128,256]{2,1,0:T(8,128)(2,1)}, u32[]{:S(2)}, u32[]{:S(2)}) collective-permute-start(bf16[2,128,256]{2,1,0:T(8,128)(2,1)} %bitcast.54), channel_id=1, source_target_pairs={{0,1},{1,2},{2,3},{3,4},{4,5},{5,6},{6,7},{7,8},{8,9},{9,10},{10,1... | collective-permute-start | bytes 393224 | tf_op jit(solution)/shard_map/ppermute | solution.py:207
  66.5 5.2 %collective-permute-done.1.yh_ref = bf16[2,128,256]{2,1,0:T(8,128)(2,1)S(1)} collective-permute-done((bf16[2,128,256]{2,1,0:T(8,128)(2,1)}, bf16[2,128,256]{2,1,0:T(8,128)(2,1)S(1)}, u32[]{:S(2)}, u32[]{:S(2)}) %collective-permute-start.1) | collective-permute-done | bytes 131104 | tf_op jit(solution)/shard_map/ppermute | solution.py:207
  71.7 0.8 collective-permute-done.yl_ref
  72.5 0.8 slice_bitcast_fusion
  73.4 1.8 %fusion.1 = (bf16[16,2,8,256]{3,2,0,1:T(8,128)(2,1)}, bf16[16,2,8,256]{3,2,0,1:T(8,128)(2,1)}) fusion(f32[16,8,8,256]{3,2,1,0:T(8,128)} %fields_ref.3), kind=kLoop, calls=%fused_computation.20 | loop fusion | bytes 524288 | tf_op jit(solution)/shard_map/slice | solution.py:242
  75.1 3.1 %all-to-all-done.1 = bf16[64,4,1024]{2,1,0:T(4,128)(2,1)} async-done(((bf16[64,4,1024]{2,1,0:T(4,128)(2,1)}), bf16[64,4,1024]{2,1,0:T(4,128)(2,1)}, u32[]{:S(2)}, u32[]{:S(2)}) %all-to-all-start.1) | async-done | bytes 524320 | tf_op jit(solution)/shard_map/all_to_all | solution.py:233
  78.2 1.3 convert_reduce_fusion
  79.5 0.7 collective-permute-start.4
  80.3 0.9 fusion
  81.2 0.8 multiply_convert_fusion
  82.0 0.8 broadcast_in_dim.2
  82.7 24.9 %all-to-all-start.2 = ((bf16[32,4,1024]{2,1,0:T(4,128)(2,1)}), bf16[32,4,1024]{2,1,0:T(4,128)(2,1)}, u32[]{:S(2)}, u32[]{:S(2)}) async-start(bf16[32,4,1024]{2,1,0:T(4,128)(2,1)} %broadcast_in_dim.2), calls=%async_computation.2 | async-start | bytes 524288 | tf_op jit(solution)/shard_map/all_to_all | solution.py:257
  107.7 1.6 %pad_maximum_fusion = bf16[288,256]{1,0:T(8,128)(2,1)} fusion(bf16[32,256]{1,0:T(8,128)(2,1)S(1)} %bitcast.48, bf16[256,256]{1,0:T(8,128)(2,1)} %bitcast.47), kind=kLoop, calls=%fused_computation.3 | loop fusion | flops 294912 | bytes 294912 | tf_op jit(solution)/shard_map/concatenate | solution.py:238
  109.3 7.4 %collective-permute-start.2 = (bf16[288,256]{1,0:T(8,128)(2,1)}, bf16[288,256]{1,0:T(8,128)(2,1)}, u32[]{:S(2)}, u32[]{:S(2)}) collective-permute-start(bf16[288,256]{1,0:T(8,128)(2,1)} %pad_maximum_fusion), channel_id=1, source_target_pairs={{0,32},{32,64},{64,96},{96,128},{128,160},{160,192},{192,224},{224... | collective-permute-start | bytes 442376 | tf_op jit(solution)/shard_map/ppermute | solution.py:207
  116.7 1.6 %pad_maximum_fusion.1 = bf16[288,256]{1,0:T(8,128)(2,1)} fusion(bf16[32,256]{1,0:T(8,128)(2,1)S(1)} %bitcast.49, bf16[256,256]{1,0:T(8,128)(2,1)} %bitcast.46), kind=kLoop, calls=%fused_computation.4 | loop fusion | flops 294912 | bytes 294912 | tf_op jit(solution)/shard_map/concatenate | solution.py:238
  118.2 1.9 %collective-permute-start.3 = (bf16[288,256]{1,0:T(8,128)(2,1)}, bf16[288,256]{1,0:T(8,128)(2,1)}, u32[]{:S(2)}, u32[]{:S(2)}) collective-permute-start(bf16[288,256]{1,0:T(8,128)(2,1)} %pad_maximum_fusion.1), channel_id=1, source_target_pairs={{32,0},{64,32},{96,64},{128,96},{160,128},{192,160},{224,192},{256... | collective-permute-start | bytes 442376 | tf_op jit(solution)/shard_map/ppermute | solution.py:207
  120.6 0.7 slice.60
  121.3 0.9 slice.55
  122.2 8.9 %collective-permute-done.3 = bf16[288,256]{1,0:T(8,128)(2,1)} collective-permute-done((bf16[288,256]{1,0:T(8,128)(2,1)}, bf16[288,256]{1,0:T(8,128)(2,1)}, u32[]{:S(2)}, u32[]{:S(2)}) %collective-permute-start.3) | collective-permute-done | bytes 147488 | tf_op jit(solution)/shard_map/ppermute | solution.py:207
  131.1 0.7 slice.61
  131.9 0.9 slice.59
  132.8 1.2 copy-done.1
  134.0 5.9 %shard_map.79 = f32[16,8,8,256]{3,2,1,0:T(8,128)} custom-call(f32[4]{0:T(128)S(1)} %add_convert_fusion.edge_ref, f32[16,8,8,256]{3,2,1,0:T(8,128)S(1)} %copy-done.1, bf16[13,8,8,256]{3,2,1,0:T(8,128)(2,1)S(1)} %copy-done.3, bf16[2,128,256]{2,1,0:T(8,128)(2,1)} %collective-permute-done.yl_ref, bf16[2,128,256]{2,1,0:T(8,128)(2,1)S(1)} %collective-permute-done.1.yh_ref, ...), custom_call_target="tpu_custom_call" | custom-call | flops 100000000 | bytes 4194304 | tf_op jit(solution)/shard_map/pallas_call | solution.py:189
  139.9 1.0 reshape.75
  140.9 1.3 convolution_convert_fusion
  (19 shorter events, 0.6 us)
Async XLA Ops:
  0.6 140.3 %copy-start = (bf16[1024,1408]{1,0:T(8,128)(2,1)S(1)}, bf16[1024,1408]{1,0:T(8,128)(2,1)}, u32[]{:S(2)}) copy-start(bf16[1024,1408]{1,0:T(8,128)(2,1)} %param.11) | copy-start | bytes 8650756
  10.5 35.3 %all-to-all-start = ((bf16[32,16,512]{2,1,0:T(8,128)(2,1)}), bf16[32,16,512]{2,1,0:T(8,128)(2,1)S(1)}, u32[]{:S(2)}, u32[]{:S(2)}) async-start(bf16[32,16,512]{2,1,0:T(8,128)(2,1)} %get-tuple-element.10), calls=%async_computation | async-start | bytes 1048576 | tf_op jit(solution)/shard_map/all_to_all | solution.py:224
  45.8 2.2 %copy-start.2 = (bf16[2048,1024]{1,0:T(8,128)(2,1)S(1)}, bf16[2048,1024]{1,0:T(8,128)(2,1)}, u32[]{:S(2)}) copy-start(bf16[2048,1024]{1,0:T(8,128)(2,1)} %param.8) | copy-start | bytes 12582916
  50.5 82.3 %copy-start.3 = (bf16[13,8,8,256]{3,2,1,0:T(8,128)(2,1)S(1)}, bf16[13,8,8,256]{3,2,1,0:T(8,128)(2,1)}, u32[]{:S(2)}) copy-start(bf16[13,8,8,256]{3,2,1,0:T(8,128)(2,1)} %source_ref.1) | copy-start | bytes 1277956
  50.5 27.8 %all-to-all-start.1 = ((bf16[64,4,1024]{2,1,0:T(4,128)(2,1)}), bf16[64,4,1024]{2,1,0:T(4,128)(2,1)}, u32[]{:S(2)}, u32[]{:S(2)}) async-start(bf16[64,4,1024]{2,1,0:T(4,128)(2,1)} %bitcast.25), calls=%async_computation.1 | async-start | bytes 1048576 | tf_op jit(solution)/shard_map/all_to_all | solution.py:233
  58.5 13.2 %collective-permute-start.1 = (bf16[2,128,256]{2,1,0:T(8,128)(2,1)}, bf16[2,128,256]{2,1,0:T(8,128)(2,1)S(1)}, u32[]{:S(2)}, u32[]{:S(2)}) collective-permute-start(bf16[2,128,256]{2,1,0:T(8,128)(2,1)} %bitcast.55), channel_id=1, source_target_pairs={{1,0},{2,1},{3,2},{4,3},{5,4},{6,5},{7,6},{8,7},{9,8},{10,9},{11,1... | collective-permute-start | bytes 393224 | tf_op jit(solution)/shard_map/ppermute | solution.py:207
  60.7 11.8 %collective-permute-start = (bf16[2,128,256]{2,1,0:T(8,128)(2,1)}, bf16[2,128,256]{2,1,0:T(8,128)(2,1)}, u32[]{:S(2)}, u32[]{:S(2)}) collective-permute-start(bf16[2,128,256]{2,1,0:T(8,128)(2,1)} %bitcast.54), channel_id=1, source_target_pairs={{0,1},{1,2},{2,3},{3,4},{4,5},{5,6},{6,7},{7,8},{8,9},{9,10},{10,1... | collective-permute-start | bytes 393224 | tf_op jit(solution)/shard_map/ppermute | solution.py:207
  79.5 0.7 collective-permute-start.4
  82.7 57.1 %all-to-all-start.2 = ((bf16[32,4,1024]{2,1,0:T(4,128)(2,1)}), bf16[32,4,1024]{2,1,0:T(4,128)(2,1)}, u32[]{:S(2)}, u32[]{:S(2)}) async-start(bf16[32,4,1024]{2,1,0:T(4,128)(2,1)} %broadcast_in_dim.2), calls=%async_computation.2 | async-start | bytes 524288 | tf_op jit(solution)/shard_map/all_to_all | solution.py:257
  109.3 11.3 %collective-permute-start.2 = (bf16[288,256]{1,0:T(8,128)(2,1)}, bf16[288,256]{1,0:T(8,128)(2,1)}, u32[]{:S(2)}, u32[]{:S(2)}) collective-permute-start(bf16[288,256]{1,0:T(8,128)(2,1)} %pad_maximum_fusion), channel_id=1, source_target_pairs={{0,32},{32,64},{64,96},{96,128},{128,160},{160,192},{192,224},{224... | collective-permute-start | bytes 442376 | tf_op jit(solution)/shard_map/ppermute | solution.py:207
  118.2 12.9 %collective-permute-start.3 = (bf16[288,256]{1,0:T(8,128)(2,1)}, bf16[288,256]{1,0:T(8,128)(2,1)}, u32[]{:S(2)}, u32[]{:S(2)}) collective-permute-start(bf16[288,256]{1,0:T(8,128)(2,1)} %pad_maximum_fusion.1), channel_id=1, source_target_pairs={{32,0},{64,32},{96,64},{128,96},{160,128},{192,160},{224,192},{256... | collective-permute-start | bytes 442376 | tf_op jit(solution)/shard_map/ppermute | solution.py:207
  132.8 1.2 copy-start.1

commit v2 on v1

v2 whole, which is shorter than its diff:
```python
import jax
import jax.numpy as jnp
from jax import lax
from jax.experimental import pallas as pl
from jax.experimental.pallas import tpu as pltpu
from jax.sharding import Mesh
from jax.sharding import PartitionSpec as P

PATCH = 16
time_step = 0.25
diffusivity = 0.2
epsilon = 1e-05

F32 = jnp.float32
BF16 = jnp.bfloat16
ALL = ("sq", "core", "mp")


def block_transpose(tiles):
    row = lax.broadcasted_iota(jnp.int32, (8, 128), 0)
    lane_block = lax.broadcasted_iota(jnp.int32, (8, 128), 1) // PATCH
    for s in (4, 2, 1):
        row_bit = (row // s) & 1
        keep, down = row_bit == ((lane_block // s) & 1), row_bit == 1
        after = [pltpu.roll(t, s, 0) for t in tiles]
        after = [pltpu.roll(t, 128 - PATCH * s, 1) for t in after]
        if s == 4:
            tiles = [jnp.where(keep, t, a) for t, a in zip(tiles, after)]
        else:
            before = [pltpu.roll(t, 8 - s, 0) for t in tiles]
            before = [pltpu.roll(t, PATCH * s, 1) for t in before]
            tiles = [
                jnp.where(keep, t, jnp.where(down, a, b)) for t, a, b in zip(tiles, after, before)
            ]
    return tiles


PACK_STEPS = 4


def pack_kernel(fields_hbm, packed_hbm, fields_ref, packed_ref, in_sem, out_sem):
    count = 16 // PACK_STEPS
    loads, stores = [], []
    for step in range(PACK_STEPS):
        some = pl.ds(step * count, count)
        loads.append(pltpu.make_async_copy(fields_hbm.at[some], fields_ref.at[some], in_sem.at[step]))
        some = pl.ds(step * 2 * count, 2 * count)
        stores.append(pltpu.make_async_copy(packed_ref.at[some], packed_hbm.at[some], out_sem.at[step]))
    for load in loads:
        load.start()
    for step in range(PACK_STEPS):
        loads[step].wait()
        places = [
            (step * count + k, half, g) for k in range(count) for half in range(2) for g in range(4)
        ]
        tiles = block_transpose(
            [
                fields_ref[f, half * 4 + g, :, c * 128 : (c + 1) * 128]
                for f, half, g in places
                for c in range(2)
            ]
        )
        for n, (f, half, g) in enumerate(places):
            both = jnp.concatenate(tiles[2 * n : 2 * n + 2], axis=0)
            packed_ref[f * 2 + half, :, g * 128 : (g + 1) * 128] = both.astype(BF16)
        stores[step].start()
    for store in stores:
        store.wait()


def pack(fields):
    return pl.pallas_call(
        pack_kernel,
        in_specs=[pl.BlockSpec(memory_space=pl.ANY)],
        out_specs=pl.BlockSpec(memory_space=pl.ANY),
        out_shape=jax.ShapeDtypeStruct((32, 16, 512), BF16),
        scratch_shapes=[
            pltpu.VMEM((16, 8, 8, 256), F32),
            pltpu.VMEM((32, 16, 512), BF16),
            pltpu.SemaphoreType.DMA((PACK_STEPS,)),
            pltpu.SemaphoreType.DMA((PACK_STEPS,)),
        ],
        cost_estimate=pl.CostEstimate(flops=1000000, bytes_accessed=2 << 20, transcendentals=0),
    )(fields)


VMEM = pl.BlockSpec(memory_space=pltpu.VMEM)
SMALL = pltpu.CompilerParams(vmem_limit_bytes=16 << 20)


def y_edge_kernel(fields_ref, first_ref, last_ref):
    for k in range(2):
        first_ref[k] = fields_ref[:, :, k, :].reshape(128, 256).astype(BF16)
        last_ref[k] = fields_ref[:, :, 6 + k, :].reshape(128, 256).astype(BF16)


def y_edges(fields):
    return pl.pallas_call(
        y_edge_kernel,
        in_specs=[VMEM],
        out_specs=[VMEM, VMEM],
        out_shape=[jax.ShapeDtypeStruct((2, 128, 256), BF16)] * 2,
        cost_estimate=pl.CostEstimate(flops=100000, bytes_accessed=2 << 20, transcendentals=0),
    )(fields)


def x_edge_kernel(head_ref, tail_ref, y_low_ref, y_high_ref, first_ref, last_ref, rows):
    rows[0] = y_low_ref[1].astype(F32)
    rows[1] = y_high_ref[0].astype(F32)
    for cells, out_ref, i in ((head_ref, first_ref, 0), (tail_ref, last_ref, 7)):
        for k in range(2):
            out_ref[k * 128 : (k + 1) * 128] = cells[:, k].reshape(128, 256).astype(BF16)
        for k in range(2):
            corner = rows[k].reshape(16, 8, 256)[:, i]
            out_ref[256 + k * 16 : 272 + k * 16] = corner.astype(BF16)


def x_edges(fields, y_low, y_high):
    return pl.pallas_call(
        x_edge_kernel,
        grid=(1,),
        in_specs=[
            pl.BlockSpec((16, 2, 8, 256), lambda n: (0, 0, 0, 0)),
            pl.BlockSpec((16, 2, 8, 256), lambda n: (0, 3, 0, 0)),
            pl.BlockSpec((2, 128, 256), lambda n: (0, 0, 0)),
            pl.BlockSpec((2, 128, 256), lambda n: (0, 0, 0)),
        ],
        out_specs=[pl.BlockSpec((288, 256), lambda n: (0, 0))] * 2,
        out_shape=[jax.ShapeDtypeStruct((288, 256), BF16)] * 2,
        scratch_shapes=[pltpu.VMEM((2, 128, 256), F32)],
        compiler_params=SMALL,
        cost_estimate=pl.CostEstimate(flops=100000, bytes_accessed=1 << 20, transcendentals=0),
    )(fields, fields, y_low, y_high)


def embed_kernel(patches_ref, weight_ref, out_ref):
    left = [patches_ref[:, b].reshape(256, 512) for b in range(2)]
    for n in range(4):
        columns = slice(n * 256, (n + 1) * 256)
        total = jnp.dot(left[0], weight_ref[0, :, columns], preferred_element_type=F32)
        total = total + jnp.dot(left[1], weight_ref[1, :, columns], preferred_element_type=F32)
        total = total.reshape(16, 2, 2, 4, 256)
        for a in range(2):
            for c in range(2):
                out_ref[a, c, :, :, columns] = total[:, c, a].astype(BF16)


def embed(patches, weight):
    return pl.pallas_call(
        embed_kernel,
        in_specs=[VMEM, VMEM],
        out_specs=VMEM,
        out_shape=jax.ShapeDtypeStruct((2, 2, 16, 4, 1024), BF16),
        compiler_params=SMALL,
        cost_estimate=pl.CostEstimate(flops=540000000, bytes_accessed=3 << 20, transcendentals=0),
    )(patches, weight)


def norm_kernel(place_ref, rows_ref, position_ref, gain_ref, out_ref):
    block = position_ref[...].astype(F32).reshape(4, 4, 1024)
    hidden = rows_ref[...]
    for k in range(4):
        hidden = hidden + jnp.where(place_ref[1] == k, block[k], 0.0)
    row_mean = jnp.mean(hidden, -1, keepdims=True)
    row_square = jnp.mean(hidden * hidden, -1, keepdims=True)
    variance = row_square - row_mean * row_mean
    normed = (hidden - row_mean) * lax.rsqrt(variance + epsilon) * gain_ref[...]
    out_ref[...] = jnp.broadcast_to(normed.astype(BF16)[None], (32, 4, 1024))


def norm(rows, position, norm_gain, mp):
    return pl.pallas_call(
        norm_kernel,
        grid_spec=pltpu.PrefetchScalarGridSpec(
            num_scalar_prefetch=1,
            grid=(1,),
            in_specs=[
                pl.BlockSpec((4, 1024), lambda n, place: (0, 0)),
                pl.BlockSpec((16, 1024), lambda n, place: (place[0], 0)),
                pl.BlockSpec((1, 1024), lambda n, place: (0, 0)),
            ],
            out_specs=pl.BlockSpec((32, 4, 1024), lambda n, place: (0, 0, 0)),
        ),
        out_shape=jax.ShapeDtypeStruct((32, 4, 1024), BF16),
        compiler_params=SMALL,
        cost_estimate=pl.CostEstimate(flops=100000, bytes_accessed=300000, transcendentals=0),
    )(jnp.stack([mp // 4, mp % 4]).astype(jnp.int32), rows, position, norm_gain.reshape(1, 1024))


def head_kernel(normed_ref, weight_ref, out_ref):
    left = normed_ref[...].astype(F32).reshape(128, 1024).astype(BF16)
    for start, size in ((0, 512), (512, 512), (1024, 384)):
        columns = slice(start, start + size)
        out_ref[:, columns] = jnp.dot(
            left, weight_ref[:, columns], preferred_element_type=F32
        ).astype(BF16)


def head(normed, head_weight):
    return pl.pallas_call(
        head_kernel,
        in_specs=[VMEM, VMEM],
        out_specs=VMEM,
        out_shape=jax.ShapeDtypeStruct((128, 1408), BF16),
        compiler_params=SMALL,
        cost_estimate=pl.CostEstimate(flops=370000000, bytes_accessed=4 << 20, transcendentals=0),
    )(normed, head_weight)


def advance_kernel(
    edge_ref, fields_ref, source_ref, yl_ref, yh_ref, xl_ref, xh_ref,
    out_ref, ylo, yhi, xlo, xhi, clo, chi, one_ref, face_ref,
):
    ylo[...] = yl_ref[...].astype(F32)
    yhi[...] = yh_ref[...].astype(F32)
    for payload, cells, corners in ((xl_ref, xlo, clo), (xh_ref, xhi, chi)):
        cells[...] = payload[0:256].astype(F32).reshape(2, 128, 256)
        corners[...] = payload[256:288].astype(F32).reshape(2, 16, 256)
    row = lax.broadcasted_iota(jnp.int32, (8, 256), 0)
    lane = lax.broadcasted_iota(jnp.int32, (8, 256), 1)
    first_row, last_row = row == 0, row == 7
    first_lane, last_lane = lane == 0, lane == 255

    def shifted(tile, low, high):
        before = jnp.where(first_row, low, pltpu.roll(tile, 1, 0))
        after = jnp.where(last_row, high, pltpu.roll(tile, 7, 0))
        return before, after

    def tendency(centre, velocity, xm, xp, ym, yp):
        zm = jnp.where(first_lane, 0.0, pltpu.roll(centre, 1, 1))
        zp = jnp.where(last_lane, 0.0, pltpu.roll(centre, 255, 1))
        laplacian = xp + xm + yp + ym + zp + zm - 6.0 * centre
        advection = velocity[0] * (xp - xm) + velocity[1] * (yp - ym) + velocity[2] * (zp - zm)
        return diffusivity * laplacian - 0.5 * advection

    def at8(f):
        return pl.ds(pl.multiple_of(f * 8, 8), 8)

    def first_stage(f, carry):
        mine = at8(f)
        for i in range(8):
            centre = fields_ref[f, i]
            xm = fields_ref[f, i - 1] if i > 0 else xlo[1, mine]
            xp = fields_ref[f, i + 1] if i < 7 else xhi[0, mine]
            low = ylo[1, pl.ds(f * 8 + i, 1)]
            high = yhi[0, pl.ds(f * 8 + i, 1)]
            ym, yp = shifted(centre, low, high)
            velocity = [fields_ref[k, i] for k in range(3)]
            one_ref[f, i] = centre + time_step * tendency(centre, velocity, xm, xp, ym, yp)
        for side in range(2):
            halo = xlo if side == 0 else xhi
            corner = clo if side == 0 else chi
            near = 1 if side == 0 else 0
            centre = halo[near, mine]
            outer = halo[1 - near, mine]
            inner = fields_ref[f, 0 if side == 0 else 7]
            xm, xp = (outer, inner) if side == 0 else (inner, outer)
            ym, yp = shifted(centre, corner[0, pl.ds(f, 1)], corner[1, pl.ds(f, 1)])
            velocity = [halo[near, k * 8 : k * 8 + 8] for k in range(3)]
            value = centre + time_step * tendency(centre, velocity, xm, xp, ym, yp)
            face_ref[side, mine] = value * edge_ref[side]
        for side in range(2):
            halo = ylo if side == 0 else yhi
            near = 1 if side == 0 else 0
            centre = halo[near, mine]
            outer = halo[1 - near, mine]
            inner = fields_ref[f, :, 0 if side == 0 else 7, :]
            ym, yp = (outer, inner) if side == 0 else (inner, outer)
            xm, xp = shifted(centre, clo[side, pl.ds(f, 1)], chi[side, pl.ds(f, 1)])
            velocity = [halo[near, k * 8 : k * 8 + 8] for k in range(3)]
            value = centre + time_step * tendency(centre, velocity, xm, xp, ym, yp)
            face_ref[2 + side, mine] = value * edge_ref[2 + side]
        return carry

    lax.fori_loop(0, 16, first_stage, 0)

    def second_stage(f, with_source):
        mine = at8(f)
        for i in range(8):
            centre = one_ref[f, i]
            xm = one_ref[f, i - 1] if i > 0 else face_ref[0, mine]
            xp = one_ref[f, i + 1] if i < 7 else face_ref[1, mine]
            low = face_ref[2, pl.ds(f * 8 + i, 1)]
            high = face_ref[3, pl.ds(f * 8 + i, 1)]
            ym, yp = shifted(centre, low, high)
            velocity = [one_ref[k, i] for k in range(3)]
            value = 0.5 * (fields_ref[f, i] + centre + time_step * tendency(centre, velocity, xm, xp, ym, yp))
            if with_source:
                value = value + time_step * source_ref[f - 3, i].astype(F32)
            out_ref[f, i] = value

    for f in range(3):
        second_stage(f, False)

    def species(f, carry):
        second_stage(f, True)
        return carry

    lax.fori_loop(3, 16, species, 0)


def advance(edges, fields, lagged_source, y_low, y_high, x_low, x_high):
    return pl.pallas_call(
        advance_kernel,
        in_specs=[pl.BlockSpec(memory_space=pltpu.SMEM)] + [VMEM] * 6,
        out_specs=VMEM,
        out_shape=jax.ShapeDtypeStruct((16, 8, 8, 256), F32),
        scratch_shapes=[pltpu.VMEM((2, 128, 256), F32)] * 4
        + [pltpu.VMEM((2, 16, 256), F32)] * 2
        + [pltpu.VMEM((16, 8, 8, 256), F32), pltpu.VMEM((4, 128, 256), F32)],
        compiler_params=SMALL,
        cost_estimate=pl.CostEstimate(flops=100000000, bytes_accessed=4 << 20, transcendentals=0),
    )(edges, fields, lagged_source, y_low, y_high, x_low, x_high)


def along(value, axes, step):
    count = 1
    for axis in axes:
        count *= lax.axis_size(axis)
    pairs = [(i, i + step) for i in range(count) if 0 <= i + step < count]
    return lax.ppermute(value, axes, pairs)


def on_device(fields, lagged_source, embed_weight, position, norm_gain, head_weight):
    core = lax.axis_index("core")
    mp = lax.axis_index("mp")
    seq = lax.axis_index("sq") * 2 + core
    x_axes = ("sq", "core")

    patches = lax.all_to_all(pack(fields), "mp", 0, 0, tiled=True)

    y_first, y_last = y_edges(fields)
    y_low = along(y_last, ("mp",), 1)
    y_high = along(y_first, ("mp",), -1)
    weight = lax.dynamic_slice_in_dim(embed_weight, core * 1024, 1024, 0).reshape(2, 512, 1024)
    patches, weight, y_low, y_high = lax.optimization_barrier((patches, weight, y_low, y_high))

    partial_sums = embed(patches.reshape(16, 2, 16, 512), weight)
    pieces = lax.all_to_all(partial_sums.reshape(64, 4, 1024), ("core", "mp"), 0, 0, tiled=True)

    x_first, x_last = x_edges(fields, y_low, y_high)
    x_low = along(x_last, x_axes, 1)
    x_high = along(x_first, x_axes, -1)
    pieces, x_low, x_high = lax.optimization_barrier((pieces, x_low, x_high))

    rows = jnp.sum(pieces.astype(F32), 0)
    swap = [(s * 32 + m, m * 32 + s) for s in range(32) for m in range(32)]
    rows = lax.ppermute(rows, ALL, swap)
    everyone = norm(rows, position, norm_gain, mp)
    normed = lax.all_to_all(everyone, "mp", 0, 0, tiled=True)

    edges = jnp.stack([seq > 0, seq < 31, mp > 0, mp < 31]).astype(F32)
    edges, _ = lax.optimization_barrier((edges, everyone))
    fields_next = advance(edges, fields, lagged_source, y_low, y_high, x_low, x_high)
    normed, fields_next = lax.optimization_barrier((normed, fields_next))

    return fields_next, head(normed, head_weight)


def solution(mesh):
    split = Mesh(mesh.devices.reshape(16, 2, 32), ALL)
    seq = ("sq", "core")
    placed = (
        P(None, seq, "mp", None),
        P(None, seq, "mp", None),
        P("mp", None),
        P(seq, None),
        P(),
        P(None, "mp"),
    )
    return jax.shard_map(
        on_device,
        mesh=split,
        in_specs=placed,
        out_specs=(P(None, seq, "mp", None), P(seq, "mp")),
        check_vma=False,
    )
```

time: 144 us -> 117 us (0.81)
  the two profiles are of different devices: /device:TPU:15 before, /device:TPU:96 now
where the time goes in v2:
time: 117 us
  starting transfers between devices  55.3 us (47%)
  waiting for transfers between devices  40.2 us (34%)
  Pallas kernels  15.4 us (13%)
  local copies, waits for them, and re-layouts  4.39 us (4%)
    all_to_all x1, starting transfers between devices, on_device(): patches = lax.all_to_all(pack(fields), 'mp', 0, 0, tiled=True)  20 us
    ppermute x4, starting transfers between devices, along(): return lax.ppermute(value, axes, pairs)  15.3 us
    ppermute x4, waiting for transfers between devices, along(): return lax.ppermute(value, axes, pairs)  14.4 us
    all_to_all x1, starting transfers between devices, on_device(): normed = lax.all_to_all(everyone, 'mp', 0, 0, tiled=True)  10.8 us
    ppermute x1, waiting for transfers between devices, on_device(): rows = lax.ppermute(rows, ALL, swap)  8.74 us
    all_to_all x1, waiting for transfers between devices, on_device(): lax.all_to_all(partial_sums.reshape(64, 4, 1024), ('core', 'mp'), 0, 0, t...  7.38 us
    all_to_all x1, starting transfers between devices, on_device(): lax.all_to_all(partial_sums.reshape(64, 4, 1024), ('core', 'mp'), 0, 0, t...  7.38 us
    all_to_all x1, waiting for transfers between devices, on_device(): normed = lax.all_to_all(everyone, 'mp', 0, 0, tiled=True)  6.94 us
  transfers between devices with their start and end apart: 8, of which 7 were waited for; matrix products, arithmetic and copies ran while one was open for 2% of the time, Pallas kernels for 7%

profile of v2, /device:TPU:96, one launch (start us, length us, event | category | flops | bytes accessed | tf_op | source)
XLA Modules:
  0.0 116.5 jit_solution(14794257275250212390)
XLA Ops:
  0.6 3.0 %shard_map.77 = bf16[32,16,512]{2,1,0:T(8,128)(2,1)} custom-call(f32[16,8,8,256]{3,2,1,0:T(8,128)} %fields_ref.3), custom_call_target="tpu_custom_call" | custom-call | flops 1000000 | bytes 2097152 | tf_op jit(solution)/shard_map/pallas_call | solution.py:72
  3.7 20.0 %all-to-all-start = ((bf16[32,16,512]{2,1,0:T(8,128)(2,1)}), bf16[32,16,512]{2,1,0:T(8,128)(2,1)}, u32[]{:S(2)}, u32[]{:S(2)}) async-start(bf16[32,16,512]{2,1,0:T(8,128)(2,1)} %shard_map.77), calls=%async_computation | async-start | bytes 1048576 | tf_op jit(solution)/shard_map/all_to_all | solution.py:330
  23.7 2.4 %shard_map.78 = (bf16[2,128,256]{2,1,0:T(8,128)(2,1)}, bf16[2,128,256]{2,1,0:T(8,128)(2,1)}) custom-call(f32[16,8,8,256]{3,2,1,0:T(8,128)} %fields_ref.3), custom_call_target="tpu_custom_call" | custom-call | flops 100000 | bytes 2097152 | tf_op jit(solution)/shard_map/pallas_call | solution.py:98
  26.1 3.6 %collective-permute-start = (bf16[2,128,256]{2,1,0:T(8,128)(2,1)}, bf16[2,128,256]{2,1,0:T(8,128)(2,1)S(1)}, u32[]{:S(2)}, u32[]{:S(2)}) collective-permute-start(bf16[2,128,256]{2,1,0:T(8,128)(2,1)} %get-tuple-element.16), channel_id=1, source_target_pairs={{0,1},{1,2},{2,3},{3,4},{4,5},{5,6},{6,7},{7,8},{8,9},{9,10},{10,1... | collective-permute-start | bytes 393224 | tf_op jit(solution)/shard_map/ppermute | solution.py:321
  29.7 1.3 %collective-permute-start.1 = (bf16[2,128,256]{2,1,0:T(8,128)(2,1)}, bf16[2,128,256]{2,1,0:T(8,128)(2,1)S(1)}, u32[]{:S(2)}, u32[]{:S(2)}) collective-permute-start(bf16[2,128,256]{2,1,0:T(8,128)(2,1)} %get-tuple-element.17), channel_id=1, source_target_pairs={{1,0},{2,1},{3,2},{4,3},{5,4},{6,5},{7,6},{8,7},{9,8},{10,9},{11,1... | collective-permute-start | bytes 393224 | tf_op jit(solution)/shard_map/ppermute | solution.py:321
  31.0 1.8 %constant_dynamic-slice_fusion = bf16[1024,1024]{1,0:T(8,128)(2,1)S(1)} fusion(bf16[2048,1024]{1,0:T(8,128)(2,1)} %param.8, s32[]{:T(128)S(6)} %select_n.16), kind=kLoop, calls=%fused_computation.3 | loop fusion | bytes 4194308 | tf_op jit(solution)/shard_map/dynamic_slice | solution.py:335
  32.8 0.0 copy-start
  32.8 2.0 %collective-permute-done.y_low_ref.yl_ref = bf16[2,128,256]{2,1,0:T(8,128)(2,1)S(1)} collective-permute-done((bf16[2,128,256]{2,1,0:T(8,128)(2,1)}, bf16[2,128,256]{2,1,0:T(8,128)(2,1)S(1)}, u32[]{:S(2)}, u32[]{:S(2)}) %collective-permute-start) | collective-permute-done | bytes 131104 | tf_op jit(solution)/shard_map/ppermute | solution.py:321
  34.8 6.2 %collective-permute-done.1.y_high_ref.yh_ref = bf16[2,128,256]{2,1,0:T(8,128)(2,1)S(1)} collective-permute-done((bf16[2,128,256]{2,1,0:T(8,128)(2,1)}, bf16[2,128,256]{2,1,0:T(8,128)(2,1)S(1)}, u32[]{:S(2)}, u32[]{:S(2)}) %collective-permute-start.1) | collective-permute-done | bytes 131104 | tf_op jit(solution)/shard_map/ppermute | solution.py:321
  41.0 2.8 %all-to-all-done = bf16[32,16,512]{2,1,0:T(8,128)(2,1)} async-done(((bf16[32,16,512]{2,1,0:T(8,128)(2,1)}), bf16[32,16,512]{2,1,0:T(8,128)(2,1)}, u32[]{:S(2)}, u32[]{:S(2)}) %all-to-all-start) | async-done | bytes 524320 | tf_op jit(solution)/shard_map/all_to_all | solution.py:330
  43.7 1.8 %shard_map.79 = bf16[2,2,16,4,1024]{4,3,2,1,0:T(4,128)(2,1)S(1)} custom-call(bf16[16,2,16,512]{3,2,1,0:T(8,128)(2,1)} %bitcast.3.patches_ref, bf16[2,512,1024]{2,1,0:T(8,128)(2,1)S(1)} %bitcast.10), custom_call_target="tpu_custom_call" | custom-call | flops 540000000 | bytes 3145728 | tf_op jit(solution)/shard_map/pallas_call | solution.py:149
  45.5 0.0 copy-start.2
  45.5 0.8 copy-done.2
  46.3 7.4 %all-to-all-start.1 = ((bf16[64,4,1024]{2,1,0:T(4,128)(2,1)}), bf16[64,4,1024]{2,1,0:T(4,128)(2,1)S(1)}, u32[]{:S(2)}, u32[]{:S(2)}) async-start(bf16[64,4,1024]{2,1,0:T(4,128)(2,1)} %bitcast.11), calls=%async_computation.1 | async-start | bytes 1048576 | tf_op jit(solution)/shard_map/all_to_all | solution.py:339
  53.7 0.1 shard_map.80
  53.8 2.1 %collective-permute-start.2 = (bf16[288,256]{1,0:T(8,128)(2,1)S(1)}, bf16[288,256]{1,0:T(8,128)(2,1)S(1)}, u32[]{:S(2)}, u32[]{:S(2)}) collective-permute-start(bf16[288,256]{1,0:T(8,128)(2,1)S(1)} %get-tuple-element.22), channel_id=1, source_target_pairs={{0,32},{32,64},{64,96},{96,128},{128,160},{160,192},{192,224},{224... | collective-permute-start | bytes 442376 | tf_op jit(solution)/shard_map/ppermute | solution.py:321
  55.9 8.3 %collective-permute-start.3 = (bf16[288,256]{1,0:T(8,128)(2,1)S(1)}, bf16[288,256]{1,0:T(8,128)(2,1)S(1)}, u32[]{:S(2)}, u32[]{:S(2)}) collective-permute-start(bf16[288,256]{1,0:T(8,128)(2,1)S(1)} %get-tuple-element.23), channel_id=1, source_target_pairs={{32,0},{64,32},{96,64},{128,96},{160,128},{192,160},{224,192},{256... | collective-permute-start | bytes 442376 | tf_op jit(solution)/shard_map/ppermute | solution.py:321
  64.2 6.2 %collective-permute-done.2.xl_ref = bf16[288,256]{1,0:T(8,128)(2,1)S(1)} collective-permute-done((bf16[288,256]{1,0:T(8,128)(2,1)S(1)}, bf16[288,256]{1,0:T(8,128)(2,1)S(1)}, u32[]{:S(2)}, u32[]{:S(2)}) %collective-permute-start.2) | collective-permute-done | bytes 147488 | tf_op jit(solution)/shard_map/ppermute | solution.py:321
  70.4 0.0 collective-permute-done.3.xh_ref
  70.4 7.4 %all-to-all-done.1 = bf16[64,4,1024]{2,1,0:T(4,128)(2,1)S(1)} async-done(((bf16[64,4,1024]{2,1,0:T(4,128)(2,1)}), bf16[64,4,1024]{2,1,0:T(4,128)(2,1)S(1)}, u32[]{:S(2)}, u32[]{:S(2)}) %all-to-all-start.1) | async-done | bytes 524320 | tf_op jit(solution)/shard_map/all_to_all | solution.py:339
  77.7 0.2 convert_reduce_fusion
  78.0 1.9 %collective-permute-start.4 = (f32[4,1024]{1,0:T(4,128)S(1)}, f32[4,1024]{1,0:T(4,128)S(1)}, u32[]{:S(2)}, u32[]{:S(2)}) collective-permute-start(f32[4,1024]{1,0:T(4,128)S(1)} %convert_reduce_fusion), channel_id=1, source_target_pairs={{0,0},{1,32},{2,64},{3,96},{4,128},{5,160},{6,192},{7,224},{8,256}... | collective-permute-start | bytes 49160 | tf_op jit(solution)/shard_map/ppermute | solution.py:348
  79.9 0.1 pad_add_fusion.place_ref
  80.0 8.7 %collective-permute-done.4.rows_ref = f32[4,1024]{1,0:T(4,128)S(1)} collective-permute-done((f32[4,1024]{1,0:T(4,128)S(1)}, f32[4,1024]{1,0:T(4,128)S(1)}, u32[]{:S(2)}, u32[]{:S(2)}) %collective-permute-start.4) | collective-permute-done | bytes 16416 | tf_op jit(solution)/shard_map/ppermute | solution.py:348
  88.7 1.4 %shard_map.81 = bf16[32,4,1024]{2,1,0:T(4,128)(2,1)} custom-call(s32[2]{0:T(128)S(1)} %pad_add_fusion.place_ref, f32[4,1024]{1,0:T(4,128)S(1)} %collective-permute-done.4.rows_ref, bf16[128,1024]{1,0:T(8,128)(2,1)S(1)} %copy-done.4, f32[1,1024]{1,0:T(1,128)S(1)} %bitcast.12), custom_call_target="tpu_custom_call" | custom-call | flops 100000 | bytes 300000 | tf_op jit(solution)/shard_map/pallas_call | solution.py:172
  90.1 10.8 %all-to-all-start.2 = ((bf16[32,4,1024]{2,1,0:T(4,128)(2,1)}), bf16[32,4,1024]{2,1,0:T(4,128)(2,1)S(1)}, u32[]{:S(2)}, u32[]{:S(2)}) async-start(bf16[32,4,1024]{2,1,0:T(4,128)(2,1)} %shard_map.81), calls=%async_computation.2 | async-start | bytes 524288 | tf_op jit(solution)/shard_map/all_to_all | solution.py:350
  100.9 0.1 add_convert_fusion.edge_ref
  101.0 0.0 copy-done.3
  101.0 5.4 %shard_map.82 = f32[16,8,8,256]{3,2,1,0:T(8,128)} custom-call(f32[4]{0:T(128)S(1)} %add_convert_fusion.edge_ref, f32[16,8,8,256]{3,2,1,0:T(8,128)S(1)} %copy-done, bf16[13,8,8,256]{3,2,1,0:T(8,128)(2,1)S(1)} %copy-done.3, bf16[2,128,256]{2,1,0:T(8,128)(2,1)S(1)} %collective-permute-done.y_low_ref.yl_ref, ...), custom_call_target="tpu_custom_call" | custom-call | flops 100000000 | bytes 4194304 | tf_op jit(solution)/shard_map/pallas_call | solution.py:303
  106.4 6.9 %all-to-all-done.2.normed_ref = bf16[32,4,1024]{2,1,0:T(4,128)(2,1)S(1)} async-done(((bf16[32,4,1024]{2,1,0:T(4,128)(2,1)}), bf16[32,4,1024]{2,1,0:T(4,128)(2,1)S(1)}, u32[]{:S(2)}, u32[]{:S(2)}) %all-to-all-start.2) | async-done | bytes 262176 | tf_op jit(solution)/shard_map/all_to_all | solution.py:350
  113.4 1.8 %copy-done.1 = bf16[1024,1408]{1,0:T(8,128)(2,1)S(1)} copy-done((bf16[1024,1408]{1,0:T(8,128)(2,1)S(1)}, bf16[1024,1408]{1,0:T(8,128)(2,1)}, u32[]{:S(2)}) %copy-start.1) | copy-done | bytes 2883608
  115.2 1.3 %shard_map.83 = bf16[128,1408]{1,0:T(8,128)(2,1)} custom-call(bf16[32,4,1024]{2,1,0:T(4,128)(2,1)S(1)} %all-to-all-done.2.normed_ref, bf16[1024,1408]{1,0:T(8,128)(2,1)S(1)} %copy-done.1), custom_call_target="tpu_custom_call" | custom-call | flops 370000000 | bytes 4194304 | tf_op jit(solution)/shard_map/pallas_call | solution.py:200
  (7 shorter events, 0.0 us)
Async XLA Ops:
  3.7 40.1 %all-to-all-start = ((bf16[32,16,512]{2,1,0:T(8,128)(2,1)}), bf16[32,16,512]{2,1,0:T(8,128)(2,1)}, u32[]{:S(2)}, u32[]{:S(2)}) async-start(bf16[32,16,512]{2,1,0:T(8,128)(2,1)} %shard_map.77), calls=%async_computation | async-start | bytes 1048576 | tf_op jit(solution)/shard_map/all_to_all | solution.py:330
  26.1 8.7 %collective-permute-start = (bf16[2,128,256]{2,1,0:T(8,128)(2,1)}, bf16[2,128,256]{2,1,0:T(8,128)(2,1)S(1)}, u32[]{:S(2)}, u32[]{:S(2)}) collective-permute-start(bf16[2,128,256]{2,1,0:T(8,128)(2,1)} %get-tuple-element.16), channel_id=1, source_target_pairs={{0,1},{1,2},{2,3},{3,4},{4,5},{5,6},{6,7},{7,8},{8,9},{9,10},{10,1... | collective-permute-start | bytes 393224 | tf_op jit(solution)/shard_map/ppermute | solution.py:321
  29.7 11.3 %collective-permute-start.1 = (bf16[2,128,256]{2,1,0:T(8,128)(2,1)}, bf16[2,128,256]{2,1,0:T(8,128)(2,1)S(1)}, u32[]{:S(2)}, u32[]{:S(2)}) collective-permute-start(bf16[2,128,256]{2,1,0:T(8,128)(2,1)} %get-tuple-element.17), channel_id=1, source_target_pairs={{1,0},{2,1},{3,2},{4,3},{5,4},{6,5},{7,6},{8,7},{9,8},{10,9},{11,1... | collective-permute-start | bytes 393224 | tf_op jit(solution)/shard_map/ppermute | solution.py:321
  32.8 20.9 %copy-start = (f32[16,8,8,256]{3,2,1,0:T(8,128)S(1)}, f32[16,8,8,256]{3,2,1,0:T(8,128)}, u32[]{:S(2)}) copy-start(f32[16,8,8,256]{3,2,1,0:T(8,128)} %fields_ref.3) | copy-start | bytes 3145732
  43.7 45.0 %copy-start.5 = (f32[1024]{0:T(1024)S(1)}, f32[1024]{0:T(1024)}, u32[]{:S(2)}) copy-start(f32[1024]{0:T(1024)} %param.10) | copy-start | bytes 12292
  45.5 0.8 copy-start.2
  46.3 42.4 %copy-start.4 = (bf16[128,1024]{1,0:T(8,128)(2,1)S(1)}, bf16[128,1024]{1,0:T(8,128)(2,1)}, u32[]{:S(2)}) copy-start(bf16[128,1024]{1,0:T(8,128)(2,1)} %position_ref.1) | copy-start | bytes 786436
  46.3 54.7 %copy-start.3 = (bf16[13,8,8,256]{3,2,1,0:T(8,128)(2,1)S(1)}, bf16[13,8,8,256]{3,2,1,0:T(8,128)(2,1)}, u32[]{:S(2)}) copy-start(bf16[13,8,8,256]{3,2,1,0:T(8,128)(2,1)} %source_ref.1) | copy-start | bytes 1277956
  46.3 31.4 %all-to-all-start.1 = ((bf16[64,4,1024]{2,1,0:T(4,128)(2,1)}), bf16[64,4,1024]{2,1,0:T(4,128)(2,1)S(1)}, u32[]{:S(2)}, u32[]{:S(2)}) async-start(bf16[64,4,1024]{2,1,0:T(4,128)(2,1)} %bitcast.11), calls=%async_computation.1 | async-start | bytes 1048576 | tf_op jit(solution)/shard_map/all_to_all | solution.py:339
  53.8 16.6 %collective-permute-start.2 = (bf16[288,256]{1,0:T(8,128)(2,1)S(1)}, bf16[288,256]{1,0:T(8,128)(2,1)S(1)}, u32[]{:S(2)}, u32[]{:S(2)}) collective-permute-start(bf16[288,256]{1,0:T(8,128)(2,1)S(1)} %get-tuple-element.22), channel_id=1, source_target_pairs={{0,32},{32,64},{64,96},{96,128},{128,160},{160,192},{192,224},{224... | collective-permute-start | bytes 442376 | tf_op jit(solution)/shard_map/ppermute | solution.py:321
  55.9 14.5 %collective-permute-start.3 = (bf16[288,256]{1,0:T(8,128)(2,1)S(1)}, bf16[288,256]{1,0:T(8,128)(2,1)S(1)}, u32[]{:S(2)}, u32[]{:S(2)}) collective-permute-start(bf16[288,256]{1,0:T(8,128)(2,1)S(1)} %get-tuple-element.23), channel_id=1, source_target_pairs={{32,0},{64,32},{96,64},{128,96},{160,128},{192,160},{224,192},{256... | collective-permute-start | bytes 442376 | tf_op jit(solution)/shard_map/ppermute | solution.py:321
  78.0 10.7 %collective-permute-start.4 = (f32[4,1024]{1,0:T(4,128)S(1)}, f32[4,1024]{1,0:T(4,128)S(1)}, u32[]{:S(2)}, u32[]{:S(2)}) collective-permute-start(f32[4,1024]{1,0:T(4,128)S(1)} %convert_reduce_fusion), channel_id=1, source_target_pairs={{0,0},{1,32},{2,64},{3,96},{4,128},{5,160},{6,192},{7,224},{8,256}... | collective-permute-start | bytes 49160 | tf_op jit(solution)/shard_map/ppermute | solution.py:348
  90.1 23.3 %all-to-all-start.2 = ((bf16[32,4,1024]{2,1,0:T(4,128)(2,1)}), bf16[32,4,1024]{2,1,0:T(4,128)(2,1)S(1)}, u32[]{:S(2)}, u32[]{:S(2)}) async-start(bf16[32,4,1024]{2,1,0:T(4,128)(2,1)} %shard_map.81), calls=%async_computation.2 | async-start | bytes 524288 | tf_op jit(solution)/shard_map/all_to_all | solution.py:350
  113.4 1.8 %copy-start.1 = (bf16[1024,1408]{1,0:T(8,128)(2,1)S(1)}, bf16[1024,1408]{1,0:T(8,128)(2,1)}, u32[]{:S(2)}) copy-start(bf16[1024,1408]{1,0:T(8,128)(2,1)} %weight_ref.1) | copy-start | bytes 8650756

commit v3 on v2

--- a/solution.py
+++ b/solution.py
@@ -133,24 +133,40 @@
     )(fields, fields, y_low, y_high)
 
 
-def embed_kernel(patches_ref, weight_ref, out_ref):
+EMBED_STEPS = 4
+
+
+def embed_kernel(patches_ref, weight_ref, out_hbm, out_ref, sem):
     left = [patches_ref[:, b].reshape(256, 512) for b in range(2)]
-    for n in range(4):
-        columns = slice(n * 256, (n + 1) * 256)
+    size = 1024 // EMBED_STEPS
+    stores = []
+    for n in range(EMBED_STEPS):
+        columns = pl.ds(n * size, size)
         total = jnp.dot(left[0], weight_ref[0, :, columns], preferred_element_type=F32)
         total = total + jnp.dot(left[1], weight_ref[1, :, columns], preferred_element_type=F32)
-        total = total.reshape(16, 2, 2, 4, 256)
+        total = total.reshape(16, 2, 2, 4, size)
         for a in range(2):
             for c in range(2):
                 out_ref[a, c, :, :, columns] = total[:, c, a].astype(BF16)
+        store = pltpu.make_async_copy(
+            out_ref.at[:, :, :, :, columns], out_hbm.at[:, :, :, :, columns], sem.at[n]
+        )
+        store.start()
+        stores.append(store)
+    for store in stores:
+        store.wait()
 
 
 def embed(patches, weight):
     return pl.pallas_call(
         embed_kernel,
         in_specs=[VMEM, VMEM],
-        out_specs=VMEM,
-        out_shape=jax.ShapeDtypeStruct((2, 2, 16, 4, 1024), BF16),
+        out_specs=pl.BlockSpec(memory_space=pltpu.HBM),
+        out_shape=pltpu.HBM((2, 2, 16, 4, 1024), BF16),
+        scratch_shapes=[
+            pltpu.VMEM((2, 2, 16, 4, 1024), BF16),
+            pltpu.SemaphoreType.DMA((EMBED_STEPS,)),
+        ],
         compiler_params=SMALL,
         cost_estimate=pl.CostEstimate(flops=540000000, bytes_accessed=3 << 20, transcendentals=0),
     )(patches, weight)
@@ -168,7 +184,7 @@
     out_ref[...] = jnp.broadcast_to(normed.astype(BF16)[None], (32, 4, 1024))
 
 
-def norm(rows, position, norm_gain, mp):
+def norm(rows, position, norm_gain, place):
     return pl.pallas_call(
         norm_kernel,
         grid_spec=pltpu.PrefetchScalarGridSpec(
@@ -184,27 +200,54 @@
         out_shape=jax.ShapeDtypeStruct((32, 4, 1024), BF16),
         compiler_params=SMALL,
         cost_estimate=pl.CostEstimate(flops=100000, bytes_accessed=300000, transcendentals=0),
-    )(jnp.stack([mp // 4, mp % 4]).astype(jnp.int32), rows, position, norm_gain.reshape(1, 1024))
-
-
-def head_kernel(normed_ref, weight_ref, out_ref):
-    left = normed_ref[...].astype(F32).reshape(128, 1024).astype(BF16)
-    for start, size in ((0, 512), (512, 512), (1024, 384)):
-        columns = slice(start, start + size)
-        out_ref[:, columns] = jnp.dot(
-            left, weight_ref[:, columns], preferred_element_type=F32
-        ).astype(BF16)
-
-
-def head(normed, head_weight):
+    )(jnp.stack([place // 4, place % 4]).astype(jnp.int32), rows, position, norm_gain.reshape(1, 1024))
+
+
+HEAD_COLUMNS = ((0, 384), (384, 384), (768, 384), (1152, 256))
+
+
+def head_kernel(order_ref, normed_ref, weight_hbm, out_hbm, rows_ref, weight_ref, out_ref, in_sem, out_sem):
+    loads, stores = [], []
+    for n, (start, size) in enumerate(HEAD_COLUMNS):
+        columns = pl.ds(start, size)
+        loads.append(
+            pltpu.make_async_copy(weight_hbm.at[:, columns], weight_ref.at[:, columns], in_sem.at[n])
+        )
+        stores.append(
+            pltpu.make_async_copy(out_ref.at[:, columns], out_hbm.at[:, columns], out_sem.at[n])
+        )
+    for load in loads:
+        load.start()
+    for s in range(32):
+        rows_ref[4 * s : 4 * s + 4] = normed_ref[order_ref[s]].astype(F32)
+    left = rows_ref[...].astype(BF16)
+    for n, (start, size) in enumerate(HEAD_COLUMNS):
+        columns = pl.ds(start, size)
+        loads[n].wait()
+        product = jnp.dot(left, weight_ref[:, columns], preferred_element_type=F32)
+        out_ref[:, columns] = product.astype(BF16)
+        stores[n].start()
+    for store in stores:
+        store.wait()
+
+
+def head(order, normed, head_weight):
+    count = len(HEAD_COLUMNS)
     return pl.pallas_call(
         head_kernel,
-        in_specs=[VMEM, VMEM],
-        out_specs=VMEM,
+        in_specs=[pl.BlockSpec(memory_space=pltpu.SMEM), VMEM, pl.BlockSpec(memory_space=pl.ANY)],
+        out_specs=pl.BlockSpec(memory_space=pl.ANY),
         out_shape=jax.ShapeDtypeStruct((128, 1408), BF16),
-        compiler_params=SMALL,
+        scratch_shapes=[
+            pltpu.VMEM((128, 1024), F32),
+            pltpu.VMEM((1024, 1408), BF16),
+            pltpu.VMEM((128, 1408), BF16),
+            pltpu.SemaphoreType.DMA((count,)),
+            pltpu.SemaphoreType.DMA((count,)),
+        ],
+        compiler_params=pltpu.CompilerParams(vmem_limit_bytes=62 << 20),
         cost_estimate=pl.CostEstimate(flops=370000000, bytes_accessed=4 << 20, transcendentals=0),
-    )(normed, head_weight)
+    )(order, normed, head_weight)
 
 
 def advance_kernel(
@@ -321,6 +364,13 @@
     return lax.ppermute(value, axes, pairs)
 
 
+X_LANDING = ((0, 1, 3, 2), (1, 0, 3, 2), (0, 1, 2, 3), (0, 1, 3, 2))
+
+
+def landing(s, m):
+    return (s // 4 + 4) % 8 * 4 + X_LANDING[m % 4][s % 4]
+
+
 def on_device(fields, lagged_source, embed_weight, position, norm_gain, head_weight):
     core = lax.axis_index("core")
     mp = lax.axis_index("mp")
@@ -344,9 +394,15 @@
     pieces, x_low, x_high = lax.optimization_barrier((pieces, x_low, x_high))
 
     rows = jnp.sum(pieces.astype(F32), 0)
-    swap = [(s * 32 + m, m * 32 + s) for s in range(32) for m in range(32)]
+    swap = [(s * 32 + m, m * 32 + landing(s, m)) for s in range(32) for m in range(32)]
     rows = lax.ppermute(rows, ALL, swap)
-    everyone = norm(rows, position, norm_gain, mp)
+    held = [[0] * 32 for m in range(32)]
+    for m in range(32):
+        for s in range(32):
+            held[m][landing(s, m)] = s
+    place = jnp.array(held, jnp.int32)[seq, mp]
+    order = jnp.array([[landing(s, m) for s in range(32)] for m in range(32)], jnp.int32)[seq]
+    everyone = norm(rows, position, norm_gain, place)
     normed = lax.all_to_all(everyone, "mp", 0, 0, tiled=True)
 
     edges = jnp.stack([seq > 0, seq < 31, mp > 0, mp < 31]).astype(F32)
@@ -354,7 +410,7 @@
     fields_next = advance(edges, fields, lagged_source, y_low, y_high, x_low, x_high)
     normed, fields_next = lax.optimization_barrier((normed, fields_next))
 
-    return fields_next, head(normed, head_weight)
+    return fields_next, head(order, normed, head_weight)
 
 
 def solution(mesh):

time: 117 us -> 115 us (0.983)
  the two profiles are of different devices: /device:TPU:96 before, /device:TPU:63 now
where the time goes in v3:
time: 115 us; the launch traced here: 114 us
  starting transfers between devices  57.2 us (50%)
  waiting for transfers between devices  29.1 us (25%)
  Pallas kernels  18.9 us (16%)
  local copies, waits for them, and re-layouts  5.06 us (4%)
  between operations  3.4 us (3%)
    all_to_all x1, starting transfers between devices, on_device(): patches = lax.all_to_all(pack(fields), 'mp', 0, 0, tiled=True)  19.6 us
    ppermute x4, starting transfers between devices, along(): return lax.ppermute(value, axes, pairs)  14.5 us
    ppermute x4, waiting for transfers between devices, along(): return lax.ppermute(value, axes, pairs)  12.8 us
    all_to_all x1, starting transfers between devices, on_device(): lax.all_to_all(partial_sums.reshape(64, 4, 1024), ('core', 'mp'), 0, 0, t...  12.4 us
    all_to_all x1, starting transfers between devices, on_device(): normed = lax.all_to_all(everyone, 'mp', 0, 0, tiled=True)  8.84 us
    ppermute x1, waiting for transfers between devices, on_device(): rows = lax.ppermute(rows, ALL, swap)  8.19 us
    pallas_call x1, Pallas kernels, advance(): pl.pallas_call(advance_kernel, in_specs=[pl.BlockSpec(memory_space=pltpu....  5.44 us
    all_to_all x1, waiting for transfers between devices, on_device(): normed = lax.all_to_all(everyone, 'mp', 0, 0, tiled=True)  4.34 us
  transfers between devices with their start and end apart: 8, of which 8 were waited for; matrix products, arithmetic and copies ran while one was open for 4% of the time, Pallas kernels for 7%

profile of v3, /device:TPU:63, one launch (start us, length us, event | category | flops | bytes accessed | tf_op | source)
XLA Modules:
  0.0 114.0 jit_solution(2422005200838602794)
XLA Ops:
  0.6 3.0 %shard_map.95 = bf16[32,16,512]{2,1,0:T(8,128)(2,1)} custom-call(f32[16,8,8,256]{3,2,1,0:T(8,128)} %fields_ref.3), custom_call_target="tpu_custom_call" | custom-call | flops 1000000 | bytes 2097152 | tf_op jit(solution)/shard_map/pallas_call | solution.py:72
  3.7 19.6 %all-to-all-start = ((bf16[32,16,512]{2,1,0:T(8,128)(2,1)}), bf16[32,16,512]{2,1,0:T(8,128)(2,1)}, u32[]{:S(2)}, u32[]{:S(2)}) async-start(bf16[32,16,512]{2,1,0:T(8,128)(2,1)} %shard_map.95), calls=%async_computation | async-start | bytes 1048576 | tf_op jit(solution)/shard_map/all_to_all | solution.py:380
  23.3 2.4 %shard_map.96 = (bf16[2,128,256]{2,1,0:T(8,128)(2,1)}, bf16[2,128,256]{2,1,0:T(8,128)(2,1)}) custom-call(f32[16,8,8,256]{3,2,1,0:T(8,128)} %fields_ref.3), custom_call_target="tpu_custom_call" | custom-call | flops 100000 | bytes 2097152 | tf_op jit(solution)/shard_map/pallas_call | solution.py:98
  25.7 3.1 %collective-permute-start = (bf16[2,128,256]{2,1,0:T(8,128)(2,1)}, bf16[2,128,256]{2,1,0:T(8,128)(2,1)S(1)}, u32[]{:S(2)}, u32[]{:S(2)}) collective-permute-start(bf16[2,128,256]{2,1,0:T(8,128)(2,1)} %get-tuple-element.16), channel_id=1, source_target_pairs={{0,1},{1,2},{2,3},{3,4},{4,5},{5,6},{6,7},{7,8},{8,9},{9,10},{10,1... | collective-permute-start | bytes 393224 | tf_op jit(solution)/shard_map/ppermute | solution.py:364
  28.8 2.2 %collective-permute-start.1 = (bf16[2,128,256]{2,1,0:T(8,128)(2,1)}, bf16[2,128,256]{2,1,0:T(8,128)(2,1)S(1)}, u32[]{:S(2)}, u32[]{:S(2)}) collective-permute-start(bf16[2,128,256]{2,1,0:T(8,128)(2,1)} %get-tuple-element.17), channel_id=1, source_target_pairs={{1,0},{2,1},{3,2},{4,3},{5,4},{6,5},{7,6},{8,7},{9,8},{10,9},{11,1... | collective-permute-start | bytes 393224 | tf_op jit(solution)/shard_map/ppermute | solution.py:364
  31.0 1.8 %constant_dynamic-slice_fusion = bf16[1024,1024]{1,0:T(8,128)(2,1)S(1)} fusion(bf16[2048,1024]{1,0:T(8,128)(2,1)} %param.10, s32[]{:T(128)S(6)} %select_n.25), kind=kLoop, calls=%fused_computation.4 | loop fusion | bytes 4194308 | tf_op jit(solution)/shard_map/dynamic_slice | solution.py:385
  32.7 0.0 copy-start
  32.7 2.1 %collective-permute-done.y_low_ref.yl_ref = bf16[2,128,256]{2,1,0:T(8,128)(2,1)S(1)} collective-permute-done((bf16[2,128,256]{2,1,0:T(8,128)(2,1)}, bf16[2,128,256]{2,1,0:T(8,128)(2,1)S(1)}, u32[]{:S(2)}, u32[]{:S(2)}) %collective-permute-start) | collective-permute-done | bytes 131104 | tf_op jit(solution)/shard_map/ppermute | solution.py:364
  34.9 3.7 %collective-permute-done.1.y_high_ref.yh_ref = bf16[2,128,256]{2,1,0:T(8,128)(2,1)S(1)} collective-permute-done((bf16[2,128,256]{2,1,0:T(8,128)(2,1)}, bf16[2,128,256]{2,1,0:T(8,128)(2,1)S(1)}, u32[]{:S(2)}, u32[]{:S(2)}) %collective-permute-start.1) | collective-permute-done | bytes 131104 | tf_op jit(solution)/shard_map/ppermute | solution.py:364
  38.6 0.6 all-to-all-done
  39.2 2.5 %shard_map.97 = bf16[2,2,16,4,1024]{4,3,2,1,0:T(4,128)(2,1)} custom-call(bf16[16,2,16,512]{3,2,1,0:T(8,128)(2,1)} %bitcast.4.patches_ref, bf16[2,512,1024]{2,1,0:T(8,128)(2,1)S(1)} %bitcast.13), custom_call_target="tpu_custom_call" | custom-call | flops 540000000 | bytes 3145728 | tf_op jit(solution)/shard_map/pallas_call | solution.py:161
  41.7 0.0 copy-start.1
  41.7 12.4 %all-to-all-start.1 = ((bf16[64,4,1024]{2,1,0:T(4,128)(2,1)}), bf16[64,4,1024]{2,1,0:T(4,128)(2,1)S(1)}, u32[]{:S(2)}, u32[]{:S(2)}) async-start(bf16[64,4,1024]{2,1,0:T(4,128)(2,1)} %bitcast.15), calls=%async_computation.1 | async-start | bytes 1048576 | tf_op jit(solution)/shard_map/all_to_all | solution.py:389
  54.1 0.1 shard_map.98
  54.2 7.3 %collective-permute-start.2 = (bf16[288,256]{1,0:T(8,128)(2,1)S(1)}, bf16[288,256]{1,0:T(8,128)(2,1)S(1)}, u32[]{:S(2)}, u32[]{:S(2)}) collective-permute-start(bf16[288,256]{1,0:T(8,128)(2,1)S(1)} %get-tuple-element.22), channel_id=1, source_target_pairs={{0,32},{32,64},{64,96},{96,128},{128,160},{160,192},{192,224},{224... | collective-permute-start | bytes 442376 | tf_op jit(solution)/shard_map/ppermute | solution.py:364
  61.5 1.9 %collective-permute-start.3 = (bf16[288,256]{1,0:T(8,128)(2,1)S(1)}, bf16[288,256]{1,0:T(8,128)(2,1)S(1)}, u32[]{:S(2)}, u32[]{:S(2)}) collective-permute-start(bf16[288,256]{1,0:T(8,128)(2,1)S(1)} %get-tuple-element.23), channel_id=1, source_target_pairs={{32,0},{64,32},{96,64},{128,96},{160,128},{192,160},{224,192},{256... | collective-permute-start | bytes 442376 | tf_op jit(solution)/shard_map/ppermute | solution.py:364
  63.4 1.3 %dynamic_slice.9 = s32[1,1]{1,0:T(1,128)} dynamic-slice(s32[32,32]{1,0:T(8,128)} %constant.55.clone, s32[]{:T(128)S(6)} %select_n.21, s32[]{:T(128)S(6)} %select_n.22), dynamic_slice_sizes={1,1} | dynamic-slice | bytes 12 | tf_op jit(solution)/shard_map/dynamic_slice | solution.py:403
  67.3 0.5 collective-permute-done.2.xl_ref
  67.9 6.4 %collective-permute-done.3.xh_ref = bf16[288,256]{1,0:T(8,128)(2,1)S(1)} collective-permute-done((bf16[288,256]{1,0:T(8,128)(2,1)S(1)}, bf16[288,256]{1,0:T(8,128)(2,1)S(1)}, u32[]{:S(2)}, u32[]{:S(2)}) %collective-permute-start.3) | collective-permute-done | bytes 147488 | tf_op jit(solution)/shard_map/ppermute | solution.py:364
  74.3 3.2 %all-to-all-done.1 = bf16[64,4,1024]{2,1,0:T(4,128)(2,1)S(1)} async-done(((bf16[64,4,1024]{2,1,0:T(4,128)(2,1)}), bf16[64,4,1024]{2,1,0:T(4,128)(2,1)S(1)}, u32[]{:S(2)}, u32[]{:S(2)}) %all-to-all-start.1) | async-done | bytes 524320 | tf_op jit(solution)/shard_map/all_to_all | solution.py:389
  77.5 0.2 convert_reduce_fusion
  77.7 1.9 %collective-permute-start.4 = (f32[4,1024]{1,0:T(4,128)S(1)}, f32[4,1024]{1,0:T(4,128)S(1)}, u32[]{:S(2)}, u32[]{:S(2)}) collective-permute-start(f32[4,1024]{1,0:T(4,128)S(1)} %convert_reduce_fusion), channel_id=1, source_target_pairs={{0,16},{1,49},{2,80},{3,112},{4,144},{5,177},{6,208},{7,240},{8,27... | collective-permute-start | bytes 49160 | tf_op jit(solution)/shard_map/ppermute | solution.py:398
  79.6 0.1 pad_add_fusion.place_ref
  79.7 8.2 %collective-permute-done.4.rows_ref = f32[4,1024]{1,0:T(4,128)S(1)} collective-permute-done((f32[4,1024]{1,0:T(4,128)S(1)}, f32[4,1024]{1,0:T(4,128)S(1)}, u32[]{:S(2)}, u32[]{:S(2)}) %collective-permute-start.4) | collective-permute-done | bytes 16416 | tf_op jit(solution)/shard_map/ppermute | solution.py:398
  87.9 1.4 %shard_map.99 = bf16[32,4,1024]{2,1,0:T(4,128)(2,1)} custom-call(s32[2]{0:T(128)S(1)} %pad_add_fusion.place_ref, f32[4,1024]{1,0:T(4,128)S(1)} %collective-permute-done.4.rows_ref, bf16[128,1024]{1,0:T(8,128)(2,1)S(1)} %copy-done.2, f32[1,1024]{1,0:T(1,128)S(1)} %bitcast.14), custom_call_target="tpu_custom_call" | custom-call | flops 100000 | bytes 300000 | tf_op jit(solution)/shard_map/pallas_call | solution.py:188
  89.3 8.8 %all-to-all-start.2 = ((bf16[32,4,1024]{2,1,0:T(4,128)(2,1)}), bf16[32,4,1024]{2,1,0:T(4,128)(2,1)S(1)}, u32[]{:S(2)}, u32[]{:S(2)}) async-start(bf16[32,4,1024]{2,1,0:T(4,128)(2,1)} %shard_map.99), calls=%async_computation.2 | async-start | bytes 524288 | tf_op jit(solution)/shard_map/all_to_all | solution.py:406
  98.1 1.3 %dynamic-slice_bitcast_fusion.order_ref = s32[32]{0:T(128)} fusion(s32[32,32]{1,0:T(8,128)} %constant.55.clone, s32[]{:T(128)S(6)} %select_n.21), kind=kLoop, calls=%fused_computation.3 | loop fusion | bytes 260 | tf_op jit(solution)/shard_map/squeeze | solution.py:404
  99.4 0.1 add_convert_fusion.edge_ref
  99.5 5.4 %shard_map.100 = f32[16,8,8,256]{3,2,1,0:T(8,128)} custom-call(f32[4]{0:T(128)S(1)} %add_convert_fusion.edge_ref, f32[16,8,8,256]{3,2,1,0:T(8,128)S(1)} %copy-done, bf16[13,8,8,256]{3,2,1,0:T(8,128)(2,1)S(1)} %copy-done.1, bf16[2,128,256]{2,1,0:T(8,128)(2,1)S(1)} %collective-permute-done.y_low_ref.yl_ref, ...), custom_call_target="tpu_custom_call" | custom-call | flops 100000000 | bytes 4194304 | tf_op jit(solution)/shard_map/pallas_call | solution.py:346
  105.0 4.3 %all-to-all-done.2.normed_ref = bf16[32,4,1024]{2,1,0:T(4,128)(2,1)S(1)} async-done(((bf16[32,4,1024]{2,1,0:T(4,128)(2,1)}), bf16[32,4,1024]{2,1,0:T(4,128)(2,1)S(1)}, u32[]{:S(2)}, u32[]{:S(2)}) %all-to-all-start.2) | async-done | bytes 262176 | tf_op jit(solution)/shard_map/all_to_all | solution.py:406
  109.3 0.7 copy-done.4
  110.0 4.0 %shard_map.101 = bf16[128,1408]{1,0:T(8,128)(2,1)} custom-call(s32[32]{0:T(128)} %dynamic-slice_bitcast_fusion.order_ref, bf16[32,4,1024]{2,1,0:T(4,128)(2,1)} %copy-done.4, bf16[1024,1408]{1,0:T(8,128)(2,1)} %weight_hbm.1), custom_call_target="tpu_custom_call" | custom-call | flops 370000000 | bytes 4194304 | tf_op jit(solution)/shard_map/pallas_call | solution.py:236
  (7 shorter events, 0.0 us)
Async XLA Ops:
  3.7 35.5 %all-to-all-start = ((bf16[32,16,512]{2,1,0:T(8,128)(2,1)}), bf16[32,16,512]{2,1,0:T(8,128)(2,1)}, u32[]{:S(2)}, u32[]{:S(2)}) async-start(bf16[32,16,512]{2,1,0:T(8,128)(2,1)} %shard_map.95), calls=%async_computation | async-start | bytes 1048576 | tf_op jit(solution)/shard_map/all_to_all | solution.py:380
  25.7 9.2 %collective-permute-start = (bf16[2,128,256]{2,1,0:T(8,128)(2,1)}, bf16[2,128,256]{2,1,0:T(8,128)(2,1)S(1)}, u32[]{:S(2)}, u32[]{:S(2)}) collective-permute-start(bf16[2,128,256]{2,1,0:T(8,128)(2,1)} %get-tuple-element.16), channel_id=1, source_target_pairs={{0,1},{1,2},{2,3},{3,4},{4,5},{5,6},{6,7},{7,8},{8,9},{9,10},{10,1... | collective-permute-start | bytes 393224 | tf_op jit(solution)/shard_map/ppermute | solution.py:364
  28.8 9.8 %collective-permute-start.1 = (bf16[2,128,256]{2,1,0:T(8,128)(2,1)}, bf16[2,128,256]{2,1,0:T(8,128)(2,1)S(1)}, u32[]{:S(2)}, u32[]{:S(2)}) collective-permute-start(bf16[2,128,256]{2,1,0:T(8,128)(2,1)} %get-tuple-element.17), channel_id=1, source_target_pairs={{1,0},{2,1},{3,2},{4,3},{5,4},{6,5},{7,6},{8,7},{9,8},{10,9},{11,1... | collective-permute-start | bytes 393224 | tf_op jit(solution)/shard_map/ppermute | solution.py:364
  32.7 21.4 %copy-start = (f32[16,8,8,256]{3,2,1,0:T(8,128)S(1)}, f32[16,8,8,256]{3,2,1,0:T(8,128)}, u32[]{:S(2)}) copy-start(f32[16,8,8,256]{3,2,1,0:T(8,128)} %fields_ref.3) | copy-start | bytes 3145732
  39.2 48.7 %copy-start.3 = (f32[1024]{0:T(1024)S(1)}, f32[1024]{0:T(1024)}, u32[]{:S(2)}) copy-start(f32[1024]{0:T(1024)} %param.12) | copy-start | bytes 12292
  41.7 46.2 %copy-start.2 = (bf16[128,1024]{1,0:T(8,128)(2,1)S(1)}, bf16[128,1024]{1,0:T(8,128)(2,1)}, u32[]{:S(2)}) copy-start(bf16[128,1024]{1,0:T(8,128)(2,1)} %position_ref.1) | copy-start | bytes 786436
  41.7 57.8 %copy-start.1 = (bf16[13,8,8,256]{3,2,1,0:T(8,128)(2,1)S(1)}, bf16[13,8,8,256]{3,2,1,0:T(8,128)(2,1)}, u32[]{:S(2)}) copy-start(bf16[13,8,8,256]{3,2,1,0:T(8,128)(2,1)} %source_ref.1) | copy-start | bytes 1277956
  41.7 35.7 %all-to-all-start.1 = ((bf16[64,4,1024]{2,1,0:T(4,128)(2,1)}), bf16[64,4,1024]{2,1,0:T(4,128)(2,1)S(1)}, u32[]{:S(2)}, u32[]{:S(2)}) async-start(bf16[64,4,1024]{2,1,0:T(4,128)(2,1)} %bitcast.15), calls=%async_computation.1 | async-start | bytes 1048576 | tf_op jit(solution)/shard_map/all_to_all | solution.py:389
  54.2 13.7 %collective-permute-start.2 = (bf16[288,256]{1,0:T(8,128)(2,1)S(1)}, bf16[288,256]{1,0:T(8,128)(2,1)S(1)}, u32[]{:S(2)}, u32[]{:S(2)}) collective-permute-start(bf16[288,256]{1,0:T(8,128)(2,1)S(1)} %get-tuple-element.22), channel_id=1, source_target_pairs={{0,32},{32,64},{64,96},{96,128},{128,160},{160,192},{192,224},{224... | collective-permute-start | bytes 442376 | tf_op jit(solution)/shard_map/ppermute | solution.py:364
  61.5 12.8 %collective-permute-start.3 = (bf16[288,256]{1,0:T(8,128)(2,1)S(1)}, bf16[288,256]{1,0:T(8,128)(2,1)S(1)}, u32[]{:S(2)}, u32[]{:S(2)}) collective-permute-start(bf16[288,256]{1,0:T(8,128)(2,1)S(1)} %get-tuple-element.23), channel_id=1, source_target_pairs={{32,0},{64,32},{96,64},{128,96},{160,128},{192,160},{224,192},{256... | collective-permute-start | bytes 442376 | tf_op jit(solution)/shard_map/ppermute | solution.py:364
  77.7 10.2 %collective-permute-start.4 = (f32[4,1024]{1,0:T(4,128)S(1)}, f32[4,1024]{1,0:T(4,128)S(1)}, u32[]{:S(2)}, u32[]{:S(2)}) collective-permute-start(f32[4,1024]{1,0:T(4,128)S(1)} %convert_reduce_fusion), channel_id=1, source_target_pairs={{0,16},{1,49},{2,80},{3,112},{4,144},{5,177},{6,208},{7,240},{8,27... | collective-permute-start | bytes 49160 | tf_op jit(solution)/shard_map/ppermute | solution.py:398
  89.3 20.0 %all-to-all-start.2 = ((bf16[32,4,1024]{2,1,0:T(4,128)(2,1)}), bf16[32,4,1024]{2,1,0:T(4,128)(2,1)S(1)}, u32[]{:S(2)}, u32[]{:S(2)}) async-start(bf16[32,4,1024]{2,1,0:T(4,128)(2,1)} %shard_map.99), calls=%async_computation.2 | async-start | bytes 524288 | tf_op jit(solution)/shard_map/all_to_all | solution.py:406
  109.3 0.7 copy-start.4

commit v4 on v2

--- a/solution.py
+++ b/solution.py
@@ -128,32 +128,68 @@
         out_specs=[pl.BlockSpec((288, 256), lambda n: (0, 0))] * 2,
         out_shape=[jax.ShapeDtypeStruct((288, 256), BF16)] * 2,
         scratch_shapes=[pltpu.VMEM((2, 128, 256), F32)],
-        compiler_params=SMALL,
         cost_estimate=pl.CostEstimate(flops=100000, bytes_accessed=1 << 20, transcendentals=0),
     )(fields, fields, y_low, y_high)
 
 
-def embed_kernel(patches_ref, weight_ref, out_ref):
+EMBED_STEPS = 4
+
+
+def embed_kernel(
+    member_ref, core_ref, patches_hbm, weight_hbm, out_hbm,
+    patches_ref, weight_ref, out_ref, patch_sem, in_sem, out_sem,
+):
+    size = 1024 // EMBED_STEPS
+    arrive = pltpu.make_async_copy(patches_hbm, patches_ref, patch_sem)
+    arrive.start()
+    loads = []
+    for n in range(EMBED_STEPS):
+        columns = pl.ds(n * size, size)
+        load = pltpu.make_async_copy(
+            weight_hbm.at[core_ref[0], :, :, columns], weight_ref.at[:, :, columns], in_sem.at[n]
+        )
+        load.start()
+        loads.append(load)
+    arrive.wait()
     left = [patches_ref[:, b].reshape(256, 512) for b in range(2)]
-    for n in range(4):
-        columns = slice(n * 256, (n + 1) * 256)
+    stores = []
+    for n in range(EMBED_STEPS):
+        columns = pl.ds(n * size, size)
+        loads[n].wait()
         total = jnp.dot(left[0], weight_ref[0, :, columns], preferred_element_type=F32)
         total = total + jnp.dot(left[1], weight_ref[1, :, columns], preferred_element_type=F32)
-        total = total.reshape(16, 2, 2, 4, 256)
+        total = total.reshape(16, 2, 2, 4, size).astype(BF16)
         for a in range(2):
             for c in range(2):
-                out_ref[a, c, :, :, columns] = total[:, c, a].astype(BF16)
-
-
-def embed(patches, weight):
+                for py in range(16):
+                    out_ref[a, member_ref[a * 32 + c * 16 + py], :, columns] = total[py, c, a]
+        store = pltpu.make_async_copy(
+            out_ref.at[:, :, :, columns], out_hbm.at[:, :, :, columns], out_sem.at[n]
+        )
+        store.start()
+        stores.append(store)
+    for store in stores:
+        store.wait()
+
+
+def embed(member, core, patches, weight):
+    smem = pl.BlockSpec(memory_space=pltpu.SMEM)
+    anywhere = pl.BlockSpec(memory_space=pl.ANY)
     return pl.pallas_call(
         embed_kernel,
-        in_specs=[VMEM, VMEM],
-        out_specs=VMEM,
-        out_shape=jax.ShapeDtypeStruct((2, 2, 16, 4, 1024), BF16),
-        compiler_params=SMALL,
+        in_specs=[smem, smem, anywhere, anywhere],
+        out_specs=anywhere,
+        out_shape=jax.ShapeDtypeStruct((2, 32, 4, 1024), BF16),
+        scratch_shapes=[
+            pltpu.VMEM((16, 2, 16, 512), BF16),
+            pltpu.VMEM((2, 512, 1024), BF16),
+            pltpu.VMEM((2, 32, 4, 1024), BF16),
+            pltpu.SemaphoreType.DMA,
+            pltpu.SemaphoreType.DMA((EMBED_STEPS,)),
+            pltpu.SemaphoreType.DMA((EMBED_STEPS,)),
+        ],
         cost_estimate=pl.CostEstimate(flops=540000000, bytes_accessed=3 << 20, transcendentals=0),
-    )(patches, weight)
+    )(member, core, patches, weight)
 
 
 def norm_kernel(place_ref, rows_ref, position_ref, gain_ref, out_ref):
@@ -168,7 +204,7 @@
     out_ref[...] = jnp.broadcast_to(normed.astype(BF16)[None], (32, 4, 1024))
 
 
-def norm(rows, position, norm_gain, mp):
+def norm(rows, position, norm_gain, place):
     return pl.pallas_call(
         norm_kernel,
         grid_spec=pltpu.PrefetchScalarGridSpec(
@@ -182,29 +218,26 @@
             out_specs=pl.BlockSpec((32, 4, 1024), lambda n, place: (0, 0, 0)),
         ),
         out_shape=jax.ShapeDtypeStruct((32, 4, 1024), BF16),
-        compiler_params=SMALL,
         cost_estimate=pl.CostEstimate(flops=100000, bytes_accessed=300000, transcendentals=0),
-    )(jnp.stack([mp // 4, mp % 4]).astype(jnp.int32), rows, position, norm_gain.reshape(1, 1024))
-
-
-def head_kernel(normed_ref, weight_ref, out_ref):
-    left = normed_ref[...].astype(F32).reshape(128, 1024).astype(BF16)
-    for start, size in ((0, 512), (512, 512), (1024, 384)):
-        columns = slice(start, start + size)
-        out_ref[:, columns] = jnp.dot(
-            left, weight_ref[:, columns], preferred_element_type=F32
-        ).astype(BF16)
-
-
-def head(normed, head_weight):
-    return pl.pallas_call(
-        head_kernel,
+    )(jnp.stack([place // 4, place % 4]).astype(jnp.int32), rows, position, norm_gain.reshape(1, 1024))
+
+
+def arrange_kernel(source_ref, normed_ref, out_ref):
+    gathered = normed_ref[...].astype(F32).reshape(128, 1024).astype(BF16)
+    column = lax.broadcasted_iota(jnp.int32, (128, 128), 1)
+    order = jnp.where(column == source_ref[...], 1.0, 0.0).astype(BF16)
+    out_ref[...] = jnp.dot(order, gathered, preferred_element_type=F32).astype(BF16)
+
+
+def arrange(source, normed):
+    return pl.pallas_call(
+        arrange_kernel,
         in_specs=[VMEM, VMEM],
         out_specs=VMEM,
-        out_shape=jax.ShapeDtypeStruct((128, 1408), BF16),
+        out_shape=jax.ShapeDtypeStruct((128, 1024), BF16),
         compiler_params=SMALL,
-        cost_estimate=pl.CostEstimate(flops=370000000, bytes_accessed=4 << 20, transcendentals=0),
-    )(normed, head_weight)
+        cost_estimate=pl.CostEstimate(flops=34000000, bytes_accessed=1 << 19, transcendentals=0),
+    )(source, normed)
 
 
 def advance_kernel(
@@ -308,7 +341,6 @@
         scratch_shapes=[pltpu.VMEM((2, 128, 256), F32)] * 4
         + [pltpu.VMEM((2, 16, 256), F32)] * 2
         + [pltpu.VMEM((16, 8, 8, 256), F32), pltpu.VMEM((4, 128, 256), F32)],
-        compiler_params=SMALL,
         cost_estimate=pl.CostEstimate(flops=100000000, bytes_accessed=4 << 20, transcendentals=0),
     )(edges, fields, lagged_source, y_low, y_high, x_low, x_high)
 
@@ -321,6 +353,21 @@
     return lax.ppermute(value, axes, pairs)
 
 
+def route(s, t):
+    z = (t // 4 - s // 4) % 8
+    differ = (s ^ t) & 1
+    if ((s ^ t) >> 1) & 1:
+        return z * 4 + 3 * differ, z * 4 + 3 - 3 * differ
+    return z * 4 + 1 + differ, z * 4 + 1 + differ
+
+
+ROUTES = [[route(s, t) for t in range(32)] for s in range(32)]
+SWAP = [(s * 32 + ROUTES[s][t][0], t * 32 + ROUTES[s][t][1]) for s in range(32) for t in range(32)]
+MEMBER = [[ROUTES[2 * p + a][t][0] for a in range(2) for t in range(32)] for p in range(16)]
+SOURCE = [[ROUTES[s][t][1] * 4 + k for s in range(32) for k in range(4)] for t in range(32)]
+PLACE = [sorted(range(32), key=lambda s: ROUTES[s][t][1]) for t in range(32)]
+
+
 def on_device(fields, lagged_source, embed_weight, position, norm_gain, head_weight):
     core = lax.axis_index("core")
     mp = lax.axis_index("mp")
@@ -332,21 +379,26 @@
     y_first, y_last = y_edges(fields)
     y_low = along(y_last, ("mp",), 1)
     y_high = along(y_first, ("mp",), -1)
-    weight = lax.dynamic_slice_in_dim(embed_weight, core * 1024, 1024, 0).reshape(2, 512, 1024)
-    patches, weight, y_low, y_high = lax.optimization_barrier((patches, weight, y_low, y_high))
-
-    partial_sums = embed(patches.reshape(16, 2, 16, 512), weight)
+    member = jnp.array(MEMBER, jnp.int32)[lax.axis_index("sq")]
+    patches, member, y_low, y_high = lax.optimization_barrier((patches, member, y_low, y_high))
+
+    weight = embed_weight.reshape(2, 2, 512, 1024)
+    patches = patches.reshape(16, 2, 16, 512)
+    partial_sums = embed(member, core.astype(jnp.int32).reshape(1), patches, weight)
     pieces = lax.all_to_all(partial_sums.reshape(64, 4, 1024), ("core", "mp"), 0, 0, tiled=True)
 
     x_first, x_last = x_edges(fields, y_low, y_high)
     x_low = along(x_last, x_axes, 1)
     x_high = along(x_first, x_axes, -1)
-    pieces, x_low, x_high = lax.optimization_barrier((pieces, x_low, x_high))
+    source = jnp.array(SOURCE, jnp.int32)[seq].reshape(128, 1)
+    place = jnp.array(PLACE, jnp.int32)[seq, mp]
+    pieces, x_low, x_high, source, place = lax.optimization_barrier(
+        (pieces, x_low, x_high, source, place)
+    )
 
     rows = jnp.sum(pieces.astype(F32), 0)
-    swap = [(s * 32 + m, m * 32 + s) for s in range(32) for m in range(32)]
-    rows = lax.ppermute(rows, ALL, swap)
-    everyone = norm(rows, position, norm_gain, mp)
+    rows = lax.ppermute(rows, ALL, SWAP)
+    everyone = norm(rows, position, norm_gain, place)
     normed = lax.all_to_all(everyone, "mp", 0, 0, tiled=True)
 
     edges = jnp.stack([seq > 0, seq < 31, mp > 0, mp < 31]).astype(F32)
@@ -354,7 +406,9 @@
     fields_next = advance(edges, fields, lagged_source, y_low, y_high, x_low, x_high)
     normed, fields_next = lax.optimization_barrier((normed, fields_next))
 
-    return fields_next, head(normed, head_weight)
+    left = arrange(source, normed)
+    source_terms = jnp.dot(left, head_weight, preferred_element_type=F32).astype(BF16)
+    return fields_next, source_terms
 
 
 def solution(mesh):

time: 117 us -> 118 us (level)
  the two profiles are of different devices: /device:TPU:96 before, /device:TPU:15 now
where the time goes in v4:
time: 118 us; the launch traced here: 117 us
  starting transfers between devices  59.6 us (51%)
  waiting for transfers between devices  23.5 us (20%)
  Pallas kernels  21.1 us (18%)
  local copies, waits for them, and re-layouts  6 us (5%)
  between operations  3.13 us (3%)
  other arithmetic  2.11 us (2%)
  matrix products  1.33 us (1%)
    all_to_all x1, starting transfers between devices, on_device(): patches = lax.all_to_all(pack(fields), 'mp', 0, 0, tiled=True)  19.5 us
    ppermute x4, waiting for transfers between devices, along(): return lax.ppermute(value, axes, pairs)  13.9 us
    ppermute x4, starting transfers between devices, along(): return lax.ppermute(value, axes, pairs)  13.2 us
    all_to_all x1, starting transfers between devices, on_device(): lax.all_to_all(partial_sums.reshape(64, 4, 1024), ('core', 'mp'), 0, 0, t...  12.5 us
    all_to_all x1, starting transfers between devices, on_device(): normed = lax.all_to_all(everyone, 'mp', 0, 0, tiled=True)  12.4 us
    pallas_call x1, Pallas kernels, advance(): pl.pallas_call(advance_kernel, in_specs=[pl.BlockSpec(memory_space=pltpu....  6.4 us
    pallas_call x1, Pallas kernels, embed(): pl.pallas_call(embed_kernel, in_specs=[smem, smem, anywhere, anywhere], o...  4.75 us
    all_to_all x1, waiting for transfers between devices, on_device(): normed = lax.all_to_all(everyone, 'mp', 0, 0, tiled=True)  3.96 us
  transfers between devices with their start and end apart: 8, of which 7 were waited for; matrix products, arithmetic and copies ran while one was open for 5% of the time, Pallas kernels for 9%

profile of v4, /device:TPU:15, one launch (start us, length us, event | category | flops | bytes accessed | tf_op | source)
XLA Modules:
  0.0 116.7 jit_solution(3721877672454034158)
XLA Ops:
  0.6 3.2 %shard_map.104 = bf16[32,16,512]{2,1,0:T(8,128)(2,1)} custom-call(f32[16,8,8,256]{3,2,1,0:T(8,128)} %fields_ref.3), custom_call_target="tpu_custom_call" | custom-call | flops 1000000 | bytes 2097152 | tf_op jit(solution)/shard_map/pallas_call | solution.py:72
  3.8 19.5 %all-to-all-start = ((bf16[32,16,512]{2,1,0:T(8,128)(2,1)}), bf16[32,16,512]{2,1,0:T(8,128)(2,1)S(1)}, u32[]{:S(2)}, u32[]{:S(2)}) async-start(bf16[32,16,512]{2,1,0:T(8,128)(2,1)} %shard_map.104), calls=%async_computation | async-start | bytes 1048576 | tf_op jit(solution)/shard_map/all_to_all | solution.py:377
  23.4 2.4 %shard_map.105 = (bf16[2,128,256]{2,1,0:T(8,128)(2,1)}, bf16[2,128,256]{2,1,0:T(8,128)(2,1)}) custom-call(f32[16,8,8,256]{3,2,1,0:T(8,128)} %fields_ref.3), custom_call_target="tpu_custom_call" | custom-call | flops 100000 | bytes 2097152 | tf_op jit(solution)/shard_map/pallas_call | solution.py:98
  25.8 3.1 %collective-permute-start = (bf16[2,128,256]{2,1,0:T(8,128)(2,1)}, bf16[2,128,256]{2,1,0:T(8,128)(2,1)S(1)}, u32[]{:S(2)}, u32[]{:S(2)}) collective-permute-start(bf16[2,128,256]{2,1,0:T(8,128)(2,1)} %get-tuple-element.18), channel_id=1, source_target_pairs={{0,1},{1,2},{2,3},{3,4},{4,5},{5,6},{6,7},{7,8},{8,9},{9,10},{10,1... | collective-permute-start | bytes 393224 | tf_op jit(solution)/shard_map/ppermute | solution.py:353
  28.9 2.2 %collective-permute-start.1 = (bf16[2,128,256]{2,1,0:T(8,128)(2,1)}, bf16[2,128,256]{2,1,0:T(8,128)(2,1)}, u32[]{:S(2)}, u32[]{:S(2)}) collective-permute-start(bf16[2,128,256]{2,1,0:T(8,128)(2,1)} %get-tuple-element.19), channel_id=1, source_target_pairs={{1,0},{2,1},{3,2},{4,3},{5,4},{6,5},{7,6},{8,7},{9,8},{10,9},{11,1... | collective-permute-start | bytes 393224 | tf_op jit(solution)/shard_map/ppermute | solution.py:353
  31.1 1.3 %dynamic-slice_bitcast_fusion.1.member_ref = s32[64]{0:T(128)} fusion(s32[16,64]{1,0:T(8,128)} %constant.57.clone, s32[]{:T(128)S(6)} %select_n.21), kind=kLoop, calls=%fused_computation.5 | loop fusion | bytes 516 | tf_op jit(solution)/shard_map/squeeze | solution.py:382
  32.4 2.5 %collective-permute-done.y_low_ref.yl_ref = bf16[2,128,256]{2,1,0:T(8,128)(2,1)S(1)} collective-permute-done((bf16[2,128,256]{2,1,0:T(8,128)(2,1)}, bf16[2,128,256]{2,1,0:T(8,128)(2,1)S(1)}, u32[]{:S(2)}, u32[]{:S(2)}) %collective-permute-start) | collective-permute-done | bytes 131104 | tf_op jit(solution)/shard_map/ppermute | solution.py:353
  34.9 3.9 %collective-permute-done.1.y_high_ref.yh_ref = bf16[2,128,256]{2,1,0:T(8,128)(2,1)} collective-permute-done((bf16[2,128,256]{2,1,0:T(8,128)(2,1)}, bf16[2,128,256]{2,1,0:T(8,128)(2,1)}, u32[]{:S(2)}, u32[]{:S(2)}) %collective-permute-start.1) | collective-permute-done | bytes 131104 | tf_op jit(solution)/shard_map/ppermute | solution.py:353
  38.8 0.4 all-to-all-done
  39.2 0.8 copy-done.1
  40.0 4.8 %shard_map.106 = bf16[2,32,4,1024]{3,2,1,0:T(4,128)(2,1)} custom-call(s32[64]{0:T(128)} %dynamic-slice_bitcast_fusion.1.member_ref, s32[1]{0:T(128)} %bitcast.1.core_ref, bf16[16,2,16,512]{3,2,1,0:T(8,128)(2,1)} %bitcast.19, bf16[2,2,512,1024]{3,2,1,0:T(8,128)(2,1)} %bitcast.18), custom_call_target="tpu_custom_call" | custom-call | flops 540000000 | bytes 3145728 | tf_op jit(solution)/shard_map/pallas_call | solution.py:178
  44.7 12.5 %all-to-all-start.1 = ((bf16[64,4,1024]{2,1,0:T(4,128)(2,1)}), bf16[64,4,1024]{2,1,0:T(4,128)(2,1)S(1)}, u32[]{:S(2)}, u32[]{:S(2)}) async-start(bf16[64,4,1024]{2,1,0:T(4,128)(2,1)} %bitcast.20), calls=%async_computation.1 | async-start | bytes 1048576 | tf_op jit(solution)/shard_map/all_to_all | solution.py:388
  57.3 1.9 %shard_map.107 = (bf16[288,256]{1,0:T(8,128)(2,1)}, bf16[288,256]{1,0:T(8,128)(2,1)}) custom-call(f32[16,8,8,256]{3,2,1,0:T(8,128)} %fields_ref.3, f32[16,8,8,256]{3,2,1,0:T(8,128)} %fields_ref.3, bf16[2,128,256]{2,1,0:T(8,128)(2,1)} %copy-done.2, bf16[2,128,256]{2,1,0:T(8,128)(2,1)} %collective-permute-done.1.y_high_ref.yh_ref), custom_call_target="tpu_custom_call" | custom-call | flops 100000 | bytes 1048576 | tf_op jit(solution)/shard_map/pallas_call | solution.py:119
  59.1 6.0 %collective-permute-start.2 = (bf16[288,256]{1,0:T(8,128)(2,1)}, bf16[288,256]{1,0:T(8,128)(2,1)S(1)}, u32[]{:S(2)}, u32[]{:S(2)}) collective-permute-start(bf16[288,256]{1,0:T(8,128)(2,1)} %get-tuple-element.24), channel_id=1, source_target_pairs={{0,32},{32,64},{64,96},{96,128},{128,160},{160,192},{192,224},{224... | collective-permute-start | bytes 442376 | tf_op jit(solution)/shard_map/ppermute | solution.py:353
  65.2 1.9 %collective-permute-start.3 = (bf16[288,256]{1,0:T(8,128)(2,1)}, bf16[288,256]{1,0:T(8,128)(2,1)}, u32[]{:S(2)}, u32[]{:S(2)}) collective-permute-start(bf16[288,256]{1,0:T(8,128)(2,1)} %get-tuple-element.25), channel_id=1, source_target_pairs={{32,0},{64,32},{96,64},{128,96},{160,128},{192,160},{224,192},{256... | collective-permute-start | bytes 442376 | tf_op jit(solution)/shard_map/ppermute | solution.py:353
  67.1 1.3 %dynamic_slice.11 = s32[1,1]{1,0:T(1,128)} dynamic-slice(s32[32,32]{1,0:T(8,128)} %constant.59.clone, s32[]{:T(128)S(6)} %select_n.22, s32[]{:T(128)S(6)} %select_n.23), dynamic_slice_sizes={1,1} | dynamic-slice | bytes 12 | tf_op jit(solution)/shard_map/dynamic_slice | solution.py:394
  68.4 1.3 %dynamic-slice_bitcast_fusion = s32[128,1]{0,1:T(1,128)} fusion(s32[32,128]{1,0:T(8,128)} %constant.58.clone, s32[]{:T(128)S(6)} %select_n.22), kind=kLoop, calls=%fused_computation.4 | loop fusion | bytes 1028 | tf_op jit(solution)/shard_map/reshape;squeeze | solution.py:393
  69.7 7.4 %collective-permute-done.3.xh_ref = bf16[288,256]{1,0:T(8,128)(2,1)} collective-permute-done((bf16[288,256]{1,0:T(8,128)(2,1)}, bf16[288,256]{1,0:T(8,128)(2,1)}, u32[]{:S(2)}, u32[]{:S(2)}) %collective-permute-start.3) | collective-permute-done | bytes 147488 | tf_op jit(solution)/shard_map/ppermute | solution.py:353
  77.1 1.9 %all-to-all-done.1 = bf16[64,4,1024]{2,1,0:T(4,128)(2,1)S(1)} async-done(((bf16[64,4,1024]{2,1,0:T(4,128)(2,1)}), bf16[64,4,1024]{2,1,0:T(4,128)(2,1)S(1)}, u32[]{:S(2)}, u32[]{:S(2)}) %all-to-all-start.1) | async-done | bytes 524320 | tf_op jit(solution)/shard_map/all_to_all | solution.py:388
  81.3 0.8 convert_reduce_fusion
  82.2 1.9 %collective-permute-start.4 = (f32[4,1024]{1,0:T(4,128)}, f32[4,1024]{1,0:T(4,128)S(1)}, u32[]{:S(2)}, u32[]{:S(2)}) collective-permute-start(f32[4,1024]{1,0:T(4,128)} %convert_reduce_fusion), channel_id=1, source_target_pairs={{1,1},{2,34},{0,67},{3,96},{5,133},{6,166},{4,199},{7,228},{9,265}... | collective-permute-start | bytes 49160 | tf_op jit(solution)/shard_map/ppermute | solution.py:400
  84.1 0.6 pad_add_fusion.place_ref
  84.7 3.3 %collective-permute-done.4.rows_ref = f32[4,1024]{1,0:T(4,128)S(1)} collective-permute-done((f32[4,1024]{1,0:T(4,128)}, f32[4,1024]{1,0:T(4,128)S(1)}, u32[]{:S(2)}, u32[]{:S(2)}) %collective-permute-start.4) | collective-permute-done | bytes 16416 | tf_op jit(solution)/shard_map/ppermute | solution.py:400
  88.1 0.6 copy-done.4
  88.7 2.3 %shard_map.108 = bf16[32,4,1024]{2,1,0:T(4,128)(2,1)} custom-call(s32[2]{0:T(128)} %pad_add_fusion.place_ref, f32[4,1024]{1,0:T(4,128)} %copy-done.4, bf16[128,1024]{1,0:T(8,128)(2,1)} %position_ref.1, f32[1,1024]{1,0:T(1,128)} %bitcast.21), custom_call_target="tpu_custom_call" | custom-call | flops 100000 | bytes 300000 | tf_op jit(solution)/shard_map/pallas_call | solution.py:208
  90.9 12.4 %all-to-all-start.2 = ((bf16[32,4,1024]{2,1,0:T(4,128)(2,1)}), bf16[32,4,1024]{2,1,0:T(4,128)(2,1)S(1)}, u32[]{:S(2)}, u32[]{:S(2)}) async-start(bf16[32,4,1024]{2,1,0:T(4,128)(2,1)} %shard_map.108), calls=%async_computation.2 | async-start | bytes 524288 | tf_op jit(solution)/shard_map/all_to_all | solution.py:402
  103.3 0.7 add_convert_fusion.edge_ref
  104.0 0.8 copy.11.source_ref
  104.8 6.4 %shard_map.109 = f32[16,8,8,256]{3,2,1,0:T(8,128)} custom-call(f32[4]{0:T(128)} %add_convert_fusion.edge_ref, f32[16,8,8,256]{3,2,1,0:T(8,128)} %fields_ref.3, bf16[13,8,8,256]{3,2,1,0:T(8,128)(2,1)} %source_ref.1, bf16[2,128,256]{2,1,0:T(8,128)(2,1)} %copy-done.2, bf16[2,128,256]{2,1,0:T(8,128)(2,1)} %collective-permute-done.1.y_high_ref.yh_ref, ...), custom_call_target="tpu_custom_call" | custom-call | flops 100000000 | bytes 4194304 | tf_op jit(solution)/shard_map/pallas_call | solution.py:336
  111.2 4.0 %all-to-all-done.2.normed_ref = bf16[32,4,1024]{2,1,0:T(4,128)(2,1)S(1)} async-done(((bf16[32,4,1024]{2,1,0:T(4,128)(2,1)}), bf16[32,4,1024]{2,1,0:T(4,128)(2,1)S(1)}, u32[]{:S(2)}, u32[]{:S(2)}) %all-to-all-start.2) | async-done | bytes 262176 | tf_op jit(solution)/shard_map/all_to_all | solution.py:402
  115.1 0.3 shard_map.110
  115.4 1.3 %convolution_convert_fusion = bf16[128,1408]{1,0:T(8,128)(2,1)} fusion(bf16[128,1024]{1,0:T(8,128)(2,1)S(1)} %shard_map.110, bf16[1024,1408]{1,0:T(8,128)(2,1)S(1)} %copy-done), kind=kOutput, calls=%fused_computation | convolution fusion | flops 369278976 | bytes 3506176 | tf_op jit(solution)/shard_map/dot_general | solution.py:410
  (9 shorter events, 0.0 us)
Async XLA Ops:
  0.6 114.8 %copy-start = (bf16[1024,1408]{1,0:T(8,128)(2,1)S(1)}, bf16[1024,1408]{1,0:T(8,128)(2,1)}, u32[]{:S(2)}) copy-start(bf16[1024,1408]{1,0:T(8,128)(2,1)} %param.14) | copy-start | bytes 8650756
  3.8 35.4 %all-to-all-start = ((bf16[32,16,512]{2,1,0:T(8,128)(2,1)}), bf16[32,16,512]{2,1,0:T(8,128)(2,1)S(1)}, u32[]{:S(2)}, u32[]{:S(2)}) async-start(bf16[32,16,512]{2,1,0:T(8,128)(2,1)} %shard_map.104), calls=%async_computation | async-start | bytes 1048576 | tf_op jit(solution)/shard_map/all_to_all | solution.py:377
  25.8 9.1 %collective-permute-start = (bf16[2,128,256]{2,1,0:T(8,128)(2,1)}, bf16[2,128,256]{2,1,0:T(8,128)(2,1)S(1)}, u32[]{:S(2)}, u32[]{:S(2)}) collective-permute-start(bf16[2,128,256]{2,1,0:T(8,128)(2,1)} %get-tuple-element.18), channel_id=1, source_target_pairs={{0,1},{1,2},{2,3},{3,4},{4,5},{5,6},{6,7},{7,8},{8,9},{9,10},{10,1... | collective-permute-start | bytes 393224 | tf_op jit(solution)/shard_map/ppermute | solution.py:353
  28.9 9.9 %collective-permute-start.1 = (bf16[2,128,256]{2,1,0:T(8,128)(2,1)}, bf16[2,128,256]{2,1,0:T(8,128)(2,1)}, u32[]{:S(2)}, u32[]{:S(2)}) collective-permute-start(bf16[2,128,256]{2,1,0:T(8,128)(2,1)} %get-tuple-element.19), channel_id=1, source_target_pairs={{1,0},{2,1},{3,2},{4,3},{5,4},{6,5},{7,6},{8,7},{9,8},{10,9},{11,1... | collective-permute-start | bytes 393224 | tf_op jit(solution)/shard_map/ppermute | solution.py:353
  34.9 22.4 %copy-start.2 = (bf16[2,128,256]{2,1,0:T(8,128)(2,1)}, bf16[2,128,256]{2,1,0:T(8,128)(2,1)S(1)}, u32[]{:S(2)}) copy-start(bf16[2,128,256]{2,1,0:T(8,128)(2,1)S(1)} %collective-permute-done.y_low_ref.yl_ref) | copy-start | bytes 393220
  39.2 0.8 copy-start.1
  44.7 34.3 %all-to-all-start.1 = ((bf16[64,4,1024]{2,1,0:T(4,128)(2,1)}), bf16[64,4,1024]{2,1,0:T(4,128)(2,1)S(1)}, u32[]{:S(2)}, u32[]{:S(2)}) async-start(bf16[64,4,1024]{2,1,0:T(4,128)(2,1)} %bitcast.20), calls=%async_computation.1 | async-start | bytes 1048576 | tf_op jit(solution)/shard_map/all_to_all | solution.py:388
  59.1 10.6 %collective-permute-start.2 = (bf16[288,256]{1,0:T(8,128)(2,1)}, bf16[288,256]{1,0:T(8,128)(2,1)S(1)}, u32[]{:S(2)}, u32[]{:S(2)}) collective-permute-start(bf16[288,256]{1,0:T(8,128)(2,1)} %get-tuple-element.24), channel_id=1, source_target_pairs={{0,32},{32,64},{64,96},{96,128},{128,160},{160,192},{192,224},{224... | collective-permute-start | bytes 442376 | tf_op jit(solution)/shard_map/ppermute | solution.py:353
  65.2 11.9 %collective-permute-start.3 = (bf16[288,256]{1,0:T(8,128)(2,1)}, bf16[288,256]{1,0:T(8,128)(2,1)}, u32[]{:S(2)}, u32[]{:S(2)}) collective-permute-start(bf16[288,256]{1,0:T(8,128)(2,1)} %get-tuple-element.25), channel_id=1, source_target_pairs={{32,0},{64,32},{96,64},{128,96},{160,128},{192,160},{224,192},{256... | collective-permute-start | bytes 442376 | tf_op jit(solution)/shard_map/ppermute | solution.py:353
  69.7 35.1 %copy-start.3 = (bf16[288,256]{1,0:T(8,128)(2,1)}, bf16[288,256]{1,0:T(8,128)(2,1)S(1)}, u32[]{:S(2)}) copy-start(bf16[288,256]{1,0:T(8,128)(2,1)S(1)} %collective-permute-done.2.xl_ref) | copy-start | bytes 442372
  82.2 5.9 %collective-permute-start.4 = (f32[4,1024]{1,0:T(4,128)}, f32[4,1024]{1,0:T(4,128)S(1)}, u32[]{:S(2)}, u32[]{:S(2)}) collective-permute-start(f32[4,1024]{1,0:T(4,128)} %convert_reduce_fusion), channel_id=1, source_target_pairs={{1,1},{2,34},{0,67},{3,96},{5,133},{6,166},{4,199},{7,228},{9,265}... | collective-permute-start | bytes 49160 | tf_op jit(solution)/shard_map/ppermute | solution.py:400
  88.1 0.6 copy-start.4
  90.9 24.2 %all-to-all-start.2 = ((bf16[32,4,1024]{2,1,0:T(4,128)(2,1)}), bf16[32,4,1024]{2,1,0:T(4,128)(2,1)S(1)}, u32[]{:S(2)}, u32[]{:S(2)}) async-start(bf16[32,4,1024]{2,1,0:T(4,128)(2,1)} %shard_map.108), calls=%async_computation.2 | async-start | bytes 524288 | tf_op jit(solution)/shard_map/all_to_all | solution.py:402

commit v5 on v4

--- a/solution.py
+++ b/solution.py
@@ -85,7 +85,7 @@
 
 
 VMEM = pl.BlockSpec(memory_space=pltpu.VMEM)
-SMALL = pltpu.CompilerParams(vmem_limit_bytes=16 << 20)
+ROOM = pltpu.CompilerParams(vmem_limit_bytes=16 << 20)
 
 
 def y_edge_kernel(fields_ref, first_ref, last_ref):
@@ -132,37 +132,51 @@
     )(fields, fields, y_low, y_high)
 
 
-EMBED_STEPS = 4
+def route(s, t):
+    z = ((t >> 2) - (s >> 2)) & 7
+    differ = (s ^ t) & 1
+    cross = ((s ^ t) >> 1) & 1
+    near = 1 + differ
+    m = z * 4 + near + cross * (2 * differ - 1)
+    mu = z * 4 + near + cross * (2 - 4 * differ)
+    return m, mu
+
+
+def arrived_from(t, mu):
+    y = ((t >> 2) - (mu >> 2)) & 7
+    cross = 1 - ((mu ^ (mu >> 1)) & 1)
+    differ = (mu & 1) ^ 1
+    return y * 4 + (((t >> 1) ^ cross) & 1) * 2 + ((t ^ differ) & 1)
 
 
 def embed_kernel(
-    member_ref, core_ref, patches_hbm, weight_hbm, out_hbm,
-    patches_ref, weight_ref, out_ref, patch_sem, in_sem, out_sem,
+    who_ref, patches_ref, weight_hbm, out_hbm, weight_ref, total_ref, out_ref, in_sem, out_sem
 ):
-    size = 1024 // EMBED_STEPS
-    arrive = pltpu.make_async_copy(patches_hbm, patches_ref, patch_sem)
-    arrive.start()
+    seq = who_ref[0]
     loads = []
-    for n in range(EMBED_STEPS):
-        columns = pl.ds(n * size, size)
-        load = pltpu.make_async_copy(
-            weight_hbm.at[core_ref[0], :, :, columns], weight_ref.at[:, :, columns], in_sem.at[n]
-        )
+    for b in range(2):
+        load = pltpu.make_async_copy(weight_hbm.at[seq & 1, b], weight_ref.at[b], in_sem.at[b])
         load.start()
         loads.append(load)
-    arrive.wait()
-    left = [patches_ref[:, b].reshape(256, 512) for b in range(2)]
+    size = 256
+    left = patches_ref[:, 0].reshape(256, 512)
+    loads[0].wait()
+    for n in range(4):
+        columns = pl.ds(n * size, size)
+        total_ref[:, columns] = jnp.dot(
+            left, weight_ref[0, :, columns], preferred_element_type=F32
+        )
+    left = patches_ref[:, 1].reshape(256, 512)
+    loads[1].wait()
     stores = []
-    for n in range(EMBED_STEPS):
+    for n in range(4):
         columns = pl.ds(n * size, size)
-        loads[n].wait()
-        total = jnp.dot(left[0], weight_ref[0, :, columns], preferred_element_type=F32)
-        total = total + jnp.dot(left[1], weight_ref[1, :, columns], preferred_element_type=F32)
-        total = total.reshape(16, 2, 2, 4, size).astype(BF16)
+        product = jnp.dot(left, weight_ref[1, :, columns], preferred_element_type=F32)
+        total = (total_ref[:, columns] + product).reshape(16, 2, 2, 4, size)
         for a in range(2):
-            for c in range(2):
-                for py in range(16):
-                    out_ref[a, member_ref[a * 32 + c * 16 + py], :, columns] = total[py, c, a]
+            for t in range(32):
+                member, _ = route((seq & 30) + a, t)
+                out_ref[a, member, :, columns] = total[t % 16, t // 16, a].astype(BF16)
         store = pltpu.make_async_copy(
             out_ref.at[:, :, :, columns], out_hbm.at[:, :, :, columns], out_sem.at[n]
         )
@@ -172,31 +186,31 @@
         store.wait()
 
 
-def embed(member, core, patches, weight):
-    smem = pl.BlockSpec(memory_space=pltpu.SMEM)
+def embed(who, patches, weight):
     anywhere = pl.BlockSpec(memory_space=pl.ANY)
     return pl.pallas_call(
         embed_kernel,
-        in_specs=[smem, smem, anywhere, anywhere],
+        in_specs=[pl.BlockSpec(memory_space=pltpu.SMEM), VMEM, anywhere],
         out_specs=anywhere,
-        out_shape=jax.ShapeDtypeStruct((2, 32, 4, 1024), BF16),
+        out_shape=pltpu.HBM((2, 32, 4, 1024), BF16),
         scratch_shapes=[
-            pltpu.VMEM((16, 2, 16, 512), BF16),
             pltpu.VMEM((2, 512, 1024), BF16),
+            pltpu.VMEM((256, 1024), F32),
             pltpu.VMEM((2, 32, 4, 1024), BF16),
-            pltpu.SemaphoreType.DMA,
-            pltpu.SemaphoreType.DMA((EMBED_STEPS,)),
-            pltpu.SemaphoreType.DMA((EMBED_STEPS,)),
+            pltpu.SemaphoreType.DMA((2,)),
+            pltpu.SemaphoreType.DMA((4,)),
         ],
+        compiler_params=pltpu.CompilerParams(vmem_limit_bytes=58 << 20),
         cost_estimate=pl.CostEstimate(flops=540000000, bytes_accessed=3 << 20, transcendentals=0),
-    )(member, core, patches, weight)
-
-
-def norm_kernel(place_ref, rows_ref, position_ref, gain_ref, out_ref):
+    )(who, patches, weight)
+
+
+def norm_kernel(who_ref, rows_ref, position_ref, gain_ref, out_ref):
+    part = arrived_from(who_ref[0], who_ref[1]) & 3
     block = position_ref[...].astype(F32).reshape(4, 4, 1024)
     hidden = rows_ref[...]
     for k in range(4):
-        hidden = hidden + jnp.where(place_ref[1] == k, block[k], 0.0)
+        hidden = hidden + jnp.where(part == k, block[k], 0.0)
     row_mean = jnp.mean(hidden, -1, keepdims=True)
     row_square = jnp.mean(hidden * hidden, -1, keepdims=True)
     variance = row_square - row_mean * row_mean
@@ -204,40 +218,43 @@
     out_ref[...] = jnp.broadcast_to(normed.astype(BF16)[None], (32, 4, 1024))
 
 
-def norm(rows, position, norm_gain, place):
+def norm(who, rows, position, norm_gain):
     return pl.pallas_call(
         norm_kernel,
         grid_spec=pltpu.PrefetchScalarGridSpec(
             num_scalar_prefetch=1,
             grid=(1,),
             in_specs=[
-                pl.BlockSpec((4, 1024), lambda n, place: (0, 0)),
-                pl.BlockSpec((16, 1024), lambda n, place: (place[0], 0)),
-                pl.BlockSpec((1, 1024), lambda n, place: (0, 0)),
+                pl.BlockSpec((4, 1024), lambda n, who: (0, 0)),
+                pl.BlockSpec((16, 1024), lambda n, who: (arrived_from(who[0], who[1]) >> 2, 0)),
+                pl.BlockSpec((1, 1024), lambda n, who: (0, 0)),
             ],
-            out_specs=pl.BlockSpec((32, 4, 1024), lambda n, place: (0, 0, 0)),
+            out_specs=pl.BlockSpec((32, 4, 1024), lambda n, who: (0, 0, 0)),
         ),
         out_shape=jax.ShapeDtypeStruct((32, 4, 1024), BF16),
+        compiler_params=ROOM,
         cost_estimate=pl.CostEstimate(flops=100000, bytes_accessed=300000, transcendentals=0),
-    )(jnp.stack([place // 4, place % 4]).astype(jnp.int32), rows, position, norm_gain.reshape(1, 1024))
-
-
-def arrange_kernel(source_ref, normed_ref, out_ref):
+    )(who, rows, position, norm_gain.reshape(1, 1024))
+
+
+def arrange_kernel(who_ref, normed_ref, out_ref):
     gathered = normed_ref[...].astype(F32).reshape(128, 1024).astype(BF16)
+    row = lax.broadcasted_iota(jnp.int32, (128, 128), 0)
     column = lax.broadcasted_iota(jnp.int32, (128, 128), 1)
-    order = jnp.where(column == source_ref[...], 1.0, 0.0).astype(BF16)
+    _, mu = route(row >> 2, who_ref[0])
+    order = jnp.where(column == mu * 4 + (row & 3), 1.0, 0.0).astype(BF16)
     out_ref[...] = jnp.dot(order, gathered, preferred_element_type=F32).astype(BF16)
 
 
-def arrange(source, normed):
+def arrange(who, normed):
     return pl.pallas_call(
         arrange_kernel,
-        in_specs=[VMEM, VMEM],
+        in_specs=[pl.BlockSpec(memory_space=pltpu.SMEM), VMEM],
         out_specs=VMEM,
         out_shape=jax.ShapeDtypeStruct((128, 1024), BF16),
-        compiler_params=SMALL,
+        compiler_params=ROOM,
         cost_estimate=pl.CostEstimate(flops=34000000, bytes_accessed=1 << 19, transcendentals=0),
-    )(source, normed)
+    )(who, normed)
 
 
 def advance_kernel(
@@ -353,19 +370,9 @@
     return lax.ppermute(value, axes, pairs)
 
 
-def route(s, t):
-    z = (t // 4 - s // 4) % 8
-    differ = (s ^ t) & 1
-    if ((s ^ t) >> 1) & 1:
-        return z * 4 + 3 * differ, z * 4 + 3 - 3 * differ
-    return z * 4 + 1 + differ, z * 4 + 1 + differ
-
-
-ROUTES = [[route(s, t) for t in range(32)] for s in range(32)]
-SWAP = [(s * 32 + ROUTES[s][t][0], t * 32 + ROUTES[s][t][1]) for s in range(32) for t in range(32)]
-MEMBER = [[ROUTES[2 * p + a][t][0] for a in range(2) for t in range(32)] for p in range(16)]
-SOURCE = [[ROUTES[s][t][1] * 4 + k for s in range(32) for k in range(4)] for t in range(32)]
-PLACE = [sorted(range(32), key=lambda s: ROUTES[s][t][1]) for t in range(32)]
+SWAP = [
+    (s * 32 + route(s, t)[0], t * 32 + route(s, t)[1]) for s in range(32) for t in range(32)
+]
 
 
 def on_device(fields, lagged_source, embed_weight, position, norm_gain, head_weight):
@@ -379,34 +386,32 @@
     y_first, y_last = y_edges(fields)
     y_low = along(y_last, ("mp",), 1)
     y_high = along(y_first, ("mp",), -1)
-    member = jnp.array(MEMBER, jnp.int32)[lax.axis_index("sq")]
-    patches, member, y_low, y_high = lax.optimization_barrier((patches, member, y_low, y_high))
+    who = jnp.stack([seq, mp]).astype(jnp.int32)
+    edges = jnp.stack([seq > 0, seq < 31, mp > 0, mp < 31]).astype(F32)
+    patches, who, edges, y_low, y_high = lax.optimization_barrier(
+        (patches, who, edges, y_low, y_high)
+    )
 
     weight = embed_weight.reshape(2, 2, 512, 1024)
     patches = patches.reshape(16, 2, 16, 512)
-    partial_sums = embed(member, core.astype(jnp.int32).reshape(1), patches, weight)
+    partial_sums = embed(who, patches, weight)
     pieces = lax.all_to_all(partial_sums.reshape(64, 4, 1024), ("core", "mp"), 0, 0, tiled=True)
 
     x_first, x_last = x_edges(fields, y_low, y_high)
     x_low = along(x_last, x_axes, 1)
     x_high = along(x_first, x_axes, -1)
-    source = jnp.array(SOURCE, jnp.int32)[seq].reshape(128, 1)
-    place = jnp.array(PLACE, jnp.int32)[seq, mp]
-    pieces, x_low, x_high, source, place = lax.optimization_barrier(
-        (pieces, x_low, x_high, source, place)
-    )
+    pieces, x_low, x_high = lax.optimization_barrier((pieces, x_low, x_high))
 
     rows = jnp.sum(pieces.astype(F32), 0)
     rows = lax.ppermute(rows, ALL, SWAP)
-    everyone = norm(rows, position, norm_gain, place)
+    everyone = norm(who, rows, position, norm_gain)
     normed = lax.all_to_all(everyone, "mp", 0, 0, tiled=True)
 
-    edges = jnp.stack([seq > 0, seq < 31, mp > 0, mp < 31]).astype(F32)
     edges, _ = lax.optimization_barrier((edges, everyone))
     fields_next = advance(edges, fields, lagged_source, y_low, y_high, x_low, x_high)
     normed, fields_next = lax.optimization_barrier((normed, fields_next))
 
-    left = arrange(source, normed)
+    left = arrange(who, normed)
     source_terms = jnp.dot(left, head_weight, preferred_element_type=F32).astype(BF16)
     return fields_next, source_terms
 

time: 118 us -> 114 us (0.966)
  local copies, waits for them, and re-layouts: 6 us -> 0.83 us
  waiting for transfers between devices: 23.5 us -> 27.6 us
  between operations: 3.13 us -> 0.8 us
  Pallas kernels: 21.1 us -> 19.9 us
    ppermute x4, waiting for transfers between devices: 13.9 us -> 16.6 us  [along(): return lax.ppermute(value, axes, pairs)]
    dynamic_slice x1 -> x0, local copies, waits for them, and re-layouts: 1.28 us -> none  [on_device(): place = jnp.array(PLACE, jnp.int32)[seq, mp]]
    squeeze x1 -> x0, local copies, waits for them, and re-layouts: 1.27 us -> none  [on_device(): member = jnp.array(MEMBER, jnp.int32)[lax.axis_index('sq')]]
    another operation x1 -> x0, local copies, waits for them, and re-layouts: 1.27 us -> none  [on_device(): source = jnp.array(SOURCE, jnp.int32)[seq].reshape(128, 1)]
  transfers between devices with their start and end apart: 8 -> 8, of which waited for: 7 -> 8; matrix products, arithmetic and copies ran while one was open for 5% -> 1% of each run, Pallas kernels for 9% -> 9%
where the time goes in v5:
time: 114 us; the launch traced here: 113 us
  starting transfers between devices  60 us (53%)
  waiting for transfers between devices  27.6 us (24%)
  Pallas kernels  19.9 us (17%)
  other arithmetic  2.43 us (2%)
  matrix products  1.33 us (1%)
    all_to_all x1, starting transfers between devices, on_device(): patches = lax.all_to_all(pack(fields), 'mp', 0, 0, tiled=True)  19.5 us
    ppermute x4, waiting for transfers between devices, along(): return lax.ppermute(value, axes, pairs)  16.6 us
    ppermute x4, starting transfers between devices, along(): return lax.ppermute(value, axes, pairs)  13.2 us
    all_to_all x1, starting transfers between devices, on_device(): lax.all_to_all(partial_sums.reshape(64, 4, 1024), ('core', 'mp'), 0, 0, t...  12.8 us
    all_to_all x1, starting transfers between devices, on_device(): normed = lax.all_to_all(everyone, 'mp', 0, 0, tiled=True)  12.4 us
    pallas_call x1, Pallas kernels, advance(): pl.pallas_call(advance_kernel, in_specs=[pl.BlockSpec(memory_space=pltpu....  6.4 us
    all_to_all x1, waiting for transfers between devices, on_device(): normed = lax.all_to_all(everyone, 'mp', 0, 0, tiled=True)  5.1 us
    pallas_call x1, Pallas kernels, embed(): pl.pallas_call(embed_kernel, in_specs=[pl.BlockSpec(memory_space=pltpu.SM...  3.89 us
  transfers between devices with their start and end apart: 8, of which 8 were waited for; matrix products, arithmetic and copies ran while one was open for 1% of the time, Pallas kernels for 9%

profile of v5, /device:TPU:15, one launch (start us, length us, event | category | flops | bytes accessed | tf_op | source)
XLA Modules:
  0.0 112.9 jit_solution(3431120534541139453)
XLA Ops:
  0.6 0.0 copy-start
  0.6 3.2 %shard_map.77 = bf16[32,16,512]{2,1,0:T(8,128)(2,1)} custom-call(f32[16,8,8,256]{3,2,1,0:T(8,128)} %fields_ref.3), custom_call_target="tpu_custom_call" | custom-call | flops 1000000 | bytes 2097152 | tf_op jit(solution)/shard_map/pallas_call | solution.py:72
  3.8 19.5 %all-to-all-start = ((bf16[32,16,512]{2,1,0:T(8,128)(2,1)}), bf16[32,16,512]{2,1,0:T(8,128)(2,1)S(1)}, u32[]{:S(2)}, u32[]{:S(2)}) async-start(bf16[32,16,512]{2,1,0:T(8,128)(2,1)} %shard_map.77), calls=%async_computation | async-start | bytes 1048576 | tf_op jit(solution)/shard_map/all_to_all | solution.py:384
  23.4 2.4 %shard_map.78 = (bf16[2,128,256]{2,1,0:T(8,128)(2,1)}, bf16[2,128,256]{2,1,0:T(8,128)(2,1)}) custom-call(f32[16,8,8,256]{3,2,1,0:T(8,128)} %fields_ref.3), custom_call_target="tpu_custom_call" | custom-call | flops 100000 | bytes 2097152 | tf_op jit(solution)/shard_map/pallas_call | solution.py:98
  25.8 3.1 %collective-permute-start = (bf16[2,128,256]{2,1,0:T(8,128)(2,1)}, bf16[2,128,256]{2,1,0:T(8,128)(2,1)S(1)}, u32[]{:S(2)}, u32[]{:S(2)}) collective-permute-start(bf16[2,128,256]{2,1,0:T(8,128)(2,1)} %get-tuple-element.17), channel_id=1, source_target_pairs={{0,1},{1,2},{2,3},{3,4},{4,5},{5,6},{6,7},{7,8},{8,9},{9,10},{10,1... | collective-permute-start | bytes 393224 | tf_op jit(solution)/shard_map/ppermute | solution.py:370
  28.9 2.2 %collective-permute-start.1 = (bf16[2,128,256]{2,1,0:T(8,128)(2,1)}, bf16[2,128,256]{2,1,0:T(8,128)(2,1)}, u32[]{:S(2)}, u32[]{:S(2)}) collective-permute-start(bf16[2,128,256]{2,1,0:T(8,128)(2,1)} %get-tuple-element.18), channel_id=1, source_target_pairs={{1,0},{2,1},{3,2},{4,3},{5,4},{6,5},{7,6},{8,7},{9,8},{10,9},{11,1... | collective-permute-start | bytes 393224 | tf_op jit(solution)/shard_map/ppermute | solution.py:370
  31.1 0.6 pad_add_fusion.who_ref
  31.7 0.6 add_convert_fusion.edge_ref
  32.3 2.6 %collective-permute-done.y_low_ref.yl_ref = bf16[2,128,256]{2,1,0:T(8,128)(2,1)S(1)} collective-permute-done((bf16[2,128,256]{2,1,0:T(8,128)(2,1)}, bf16[2,128,256]{2,1,0:T(8,128)(2,1)S(1)}, u32[]{:S(2)}, u32[]{:S(2)}) %collective-permute-start) | collective-permute-done | bytes 131104 | tf_op jit(solution)/shard_map/ppermute | solution.py:370
  34.9 3.9 %collective-permute-done.1.y_high_ref.yh_ref = bf16[2,128,256]{2,1,0:T(8,128)(2,1)} collective-permute-done((bf16[2,128,256]{2,1,0:T(8,128)(2,1)}, bf16[2,128,256]{2,1,0:T(8,128)(2,1)}, u32[]{:S(2)}, u32[]{:S(2)}) %collective-permute-start.1) | collective-permute-done | bytes 131104 | tf_op jit(solution)/shard_map/ppermute | solution.py:370
  38.8 0.4 all-to-all-done
  39.2 0.8 copy-done.4
  40.0 3.9 %shard_map.79 = bf16[2,32,4,1024]{3,2,1,0:T(4,128)(2,1)} custom-call(s32[2]{0:T(128)} %pad_add_fusion.who_ref, bf16[16,2,16,512]{3,2,1,0:T(8,128)(2,1)} %bitcast.14, bf16[2,2,512,1024]{3,2,1,0:T(8,128)(2,1)} %bitcast.13), custom_call_target="tpu_custom_call" | custom-call | flops 540000000 | bytes 3145728 | tf_op jit(solution)/shard_map/pallas_call | solution.py:191
  43.9 0.0 copy-start.1
  43.9 0.0 copy-start.3
  43.9 12.8 %all-to-all-start.1 = ((bf16[64,4,1024]{2,1,0:T(4,128)(2,1)}), bf16[64,4,1024]{2,1,0:T(4,128)(2,1)}, u32[]{:S(2)}, u32[]{:S(2)}) async-start(bf16[64,4,1024]{2,1,0:T(4,128)(2,1)} %bitcast.15), calls=%async_computation.1 | async-start | bytes 1048576 | tf_op jit(solution)/shard_map/all_to_all | solution.py:398
  56.7 1.9 %shard_map.80 = (bf16[288,256]{1,0:T(8,128)(2,1)}, bf16[288,256]{1,0:T(8,128)(2,1)}) custom-call(f32[16,8,8,256]{3,2,1,0:T(8,128)} %fields_ref.3, f32[16,8,8,256]{3,2,1,0:T(8,128)} %fields_ref.3, bf16[2,128,256]{2,1,0:T(8,128)(2,1)} %copy-done.5, bf16[2,128,256]{2,1,0:T(8,128)(2,1)} %collective-permute-done.1.y_high_ref.yh_ref), custom_call_target="tpu_custom_call" | custom-call | flops 100000 | bytes 1048576 | tf_op jit(solution)/shard_map/pallas_call | solution.py:119
  58.6 6.0 %collective-permute-start.2 = (bf16[288,256]{1,0:T(8,128)(2,1)}, bf16[288,256]{1,0:T(8,128)(2,1)S(1)}, u32[]{:S(2)}, u32[]{:S(2)}) collective-permute-start(bf16[288,256]{1,0:T(8,128)(2,1)} %get-tuple-element.23), channel_id=1, source_target_pairs={{0,32},{32,64},{64,96},{96,128},{128,160},{160,192},{192,224},{224... | collective-permute-start | bytes 442376 | tf_op jit(solution)/shard_map/ppermute | solution.py:370
  64.7 1.9 %collective-permute-start.3 = (bf16[288,256]{1,0:T(8,128)(2,1)}, bf16[288,256]{1,0:T(8,128)(2,1)S(1)}, u32[]{:S(2)}, u32[]{:S(2)}) collective-permute-start(bf16[288,256]{1,0:T(8,128)(2,1)} %get-tuple-element.24), channel_id=1, source_target_pairs={{32,0},{64,32},{96,64},{128,96},{160,128},{192,160},{224,192},{256... | collective-permute-start | bytes 442376 | tf_op jit(solution)/shard_map/ppermute | solution.py:370
  66.6 2.0 %collective-permute-done.2.xl_ref = bf16[288,256]{1,0:T(8,128)(2,1)S(1)} collective-permute-done((bf16[288,256]{1,0:T(8,128)(2,1)}, bf16[288,256]{1,0:T(8,128)(2,1)S(1)}, u32[]{:S(2)}, u32[]{:S(2)}) %collective-permute-start.2) | collective-permute-done | bytes 147488 | tf_op jit(solution)/shard_map/ppermute | solution.py:370
  68.6 8.1 %collective-permute-done.3.xh_ref = bf16[288,256]{1,0:T(8,128)(2,1)S(1)} collective-permute-done((bf16[288,256]{1,0:T(8,128)(2,1)}, bf16[288,256]{1,0:T(8,128)(2,1)S(1)}, u32[]{:S(2)}, u32[]{:S(2)}) %collective-permute-start.3) | collective-permute-done | bytes 147488 | tf_op jit(solution)/shard_map/ppermute | solution.py:370
  76.7 1.7 %all-to-all-done.1 = bf16[64,4,1024]{2,1,0:T(4,128)(2,1)} async-done(((bf16[64,4,1024]{2,1,0:T(4,128)(2,1)}), bf16[64,4,1024]{2,1,0:T(4,128)(2,1)}, u32[]{:S(2)}, u32[]{:S(2)}) %all-to-all-start.1) | async-done | bytes 524320 | tf_op jit(solution)/shard_map/all_to_all | solution.py:398
  78.4 1.3 %convert_reduce_fusion = f32[4,1024]{1,0:T(4,128)S(1)} fusion(bf16[64,4,1024]{2,1,0:T(4,128)(2,1)} %all-to-all-done.1), kind=kLoop, calls=%fused_computation.1 | loop fusion | flops 520192 | bytes 540672 | tf_op jit(solution)/shard_map/reduce_sum | solution.py:405
  79.7 1.9 %collective-permute-start.4 = (f32[4,1024]{1,0:T(4,128)S(1)}, f32[4,1024]{1,0:T(4,128)S(1)}, u32[]{:S(2)}, u32[]{:S(2)}) collective-permute-start(f32[4,1024]{1,0:T(4,128)S(1)} %convert_reduce_fusion), channel_id=1, source_target_pairs={{1,1},{2,34},{0,67},{3,96},{5,133},{6,166},{4,199},{7,228},{9,265}... | collective-permute-start | bytes 49160 | tf_op jit(solution)/shard_map/ppermute | solution.py:406
  81.6 3.8 %collective-permute-done.4.rows_ref = f32[4,1024]{1,0:T(4,128)S(1)} collective-permute-done((f32[4,1024]{1,0:T(4,128)S(1)}, f32[4,1024]{1,0:T(4,128)S(1)}, u32[]{:S(2)}, u32[]{:S(2)}) %collective-permute-start.4) | collective-permute-done | bytes 16416 | tf_op jit(solution)/shard_map/ppermute | solution.py:406
  85.4 0.0 copy-done.1
  85.4 1.4 %shard_map.81 = bf16[32,4,1024]{2,1,0:T(4,128)(2,1)} custom-call(s32[2]{0:T(128)S(1)} %copy-done.2, f32[4,1024]{1,0:T(4,128)S(1)} %collective-permute-done.4.rows_ref, bf16[128,1024]{1,0:T(8,128)(2,1)S(1)} %copy-done.1, f32[1,1024]{1,0:T(1,128)S(1)} %bitcast.12), custom_call_target="tpu_custom_call" | custom-call | flops 100000 | bytes 300000 | tf_op jit(solution)/shard_map/pallas_call | solution.py:222
  86.8 12.4 %all-to-all-start.2 = ((bf16[32,4,1024]{2,1,0:T(4,128)(2,1)}), bf16[32,4,1024]{2,1,0:T(4,128)(2,1)S(1)}, u32[]{:S(2)}, u32[]{:S(2)}) async-start(bf16[32,4,1024]{2,1,0:T(4,128)(2,1)} %shard_map.81), calls=%async_computation.2 | async-start | bytes 524288 | tf_op jit(solution)/shard_map/all_to_all | solution.py:408
  99.2 6.4 %shard_map.82 = f32[16,8,8,256]{3,2,1,0:T(8,128)} custom-call(f32[4]{0:T(128)} %add_convert_fusion.edge_ref, f32[16,8,8,256]{3,2,1,0:T(8,128)} %fields_ref.3, bf16[13,8,8,256]{3,2,1,0:T(8,128)(2,1)} %source_ref.1, bf16[2,128,256]{2,1,0:T(8,128)(2,1)} %copy-done.5, bf16[2,128,256]{2,1,0:T(8,128)(2,1)} %collective-permute-done.1.y_high_ref.yh_ref, ...), custom_call_target="tpu_custom_call" | custom-call | flops 100000000 | bytes 4194304 | tf_op jit(solution)/shard_map/pallas_call | solution.py:353
  105.6 5.1 %all-to-all-done.2.normed_ref = bf16[32,4,1024]{2,1,0:T(4,128)(2,1)S(1)} async-done(((bf16[32,4,1024]{2,1,0:T(4,128)(2,1)}), bf16[32,4,1024]{2,1,0:T(4,128)(2,1)S(1)}, u32[]{:S(2)}, u32[]{:S(2)}) %all-to-all-start.2) | async-done | bytes 262176 | tf_op jit(solution)/shard_map/all_to_all | solution.py:408
  110.7 0.8 shard_map.83
  111.5 1.3 %convolution_convert_fusion = bf16[128,1408]{1,0:T(8,128)(2,1)} fusion(bf16[128,1024]{1,0:T(8,128)(2,1)S(1)} %shard_map.83, bf16[1024,1408]{1,0:T(8,128)(2,1)S(1)} %copy-done), kind=kOutput, calls=%fused_computation | convolution fusion | flops 369278976 | bytes 3506176 | tf_op jit(solution)/shard_map/dot_general | solution.py:415
  (11 shorter events, 0.0 us)
Async XLA Ops:
  0.6 110.9 %copy-start = (bf16[1024,1408]{1,0:T(8,128)(2,1)S(1)}, bf16[1024,1408]{1,0:T(8,128)(2,1)}, u32[]{:S(2)}) copy-start(bf16[1024,1408]{1,0:T(8,128)(2,1)} %param.11) | copy-start | bytes 8650756
  3.8 35.4 %all-to-all-start = ((bf16[32,16,512]{2,1,0:T(8,128)(2,1)}), bf16[32,16,512]{2,1,0:T(8,128)(2,1)S(1)}, u32[]{:S(2)}, u32[]{:S(2)}) async-start(bf16[32,16,512]{2,1,0:T(8,128)(2,1)} %shard_map.77), calls=%async_computation | async-start | bytes 1048576 | tf_op jit(solution)/shard_map/all_to_all | solution.py:384
  25.8 9.1 %collective-permute-start = (bf16[2,128,256]{2,1,0:T(8,128)(2,1)}, bf16[2,128,256]{2,1,0:T(8,128)(2,1)S(1)}, u32[]{:S(2)}, u32[]{:S(2)}) collective-permute-start(bf16[2,128,256]{2,1,0:T(8,128)(2,1)} %get-tuple-element.17), channel_id=1, source_target_pairs={{0,1},{1,2},{2,3},{3,4},{4,5},{5,6},{6,7},{7,8},{8,9},{9,10},{10,1... | collective-permute-start | bytes 393224 | tf_op jit(solution)/shard_map/ppermute | solution.py:370
  28.9 9.9 %collective-permute-start.1 = (bf16[2,128,256]{2,1,0:T(8,128)(2,1)}, bf16[2,128,256]{2,1,0:T(8,128)(2,1)}, u32[]{:S(2)}, u32[]{:S(2)}) collective-permute-start(bf16[2,128,256]{2,1,0:T(8,128)(2,1)} %get-tuple-element.18), channel_id=1, source_target_pairs={{1,0},{2,1},{3,2},{4,3},{5,4},{6,5},{7,6},{8,7},{9,8},{10,9},{11,1... | collective-permute-start | bytes 393224 | tf_op jit(solution)/shard_map/ppermute | solution.py:370
  34.9 21.8 %copy-start.5 = (bf16[2,128,256]{2,1,0:T(8,128)(2,1)}, bf16[2,128,256]{2,1,0:T(8,128)(2,1)S(1)}, u32[]{:S(2)}) copy-start(bf16[2,128,256]{2,1,0:T(8,128)(2,1)S(1)} %collective-permute-done.y_low_ref.yl_ref) | copy-start | bytes 393220
  39.2 0.8 copy-start.4
  43.9 41.5 %copy-start.1 = (bf16[128,1024]{1,0:T(8,128)(2,1)S(1)}, bf16[128,1024]{1,0:T(8,128)(2,1)}, u32[]{:S(2)}) copy-start(bf16[128,1024]{1,0:T(8,128)(2,1)} %position_ref.1) | copy-start | bytes 786436
  43.9 41.5 %copy-start.2 = (s32[2]{0:T(128)S(1)}, s32[2]{0:T(128)}, u32[]{:S(2)}) copy-start(s32[2]{0:T(128)} %pad_add_fusion.who_ref) | copy-start | bytes 28
  43.9 41.5 %copy-start.3 = (f32[1024]{0:T(1024)S(1)}, f32[1024]{0:T(1024)}, u32[]{:S(2)}) copy-start(f32[1024]{0:T(1024)} %param.10) | copy-start | bytes 12292
  43.9 34.5 %all-to-all-start.1 = ((bf16[64,4,1024]{2,1,0:T(4,128)(2,1)}), bf16[64,4,1024]{2,1,0:T(4,128)(2,1)}, u32[]{:S(2)}, u32[]{:S(2)}) async-start(bf16[64,4,1024]{2,1,0:T(4,128)(2,1)} %bitcast.15), calls=%async_computation.1 | async-start | bytes 1048576 | tf_op jit(solution)/shard_map/all_to_all | solution.py:398
  58.6 10.0 %collective-permute-start.2 = (bf16[288,256]{1,0:T(8,128)(2,1)}, bf16[288,256]{1,0:T(8,128)(2,1)S(1)}, u32[]{:S(2)}, u32[]{:S(2)}) collective-permute-start(bf16[288,256]{1,0:T(8,128)(2,1)} %get-tuple-element.23), channel_id=1, source_target_pairs={{0,32},{32,64},{64,96},{96,128},{128,160},{160,192},{192,224},{224... | collective-permute-start | bytes 442376 | tf_op jit(solution)/shard_map/ppermute | solution.py:370
  64.7 12.0 %collective-permute-start.3 = (bf16[288,256]{1,0:T(8,128)(2,1)}, bf16[288,256]{1,0:T(8,128)(2,1)S(1)}, u32[]{:S(2)}, u32[]{:S(2)}) collective-permute-start(bf16[288,256]{1,0:T(8,128)(2,1)} %get-tuple-element.24), channel_id=1, source_target_pairs={{32,0},{64,32},{96,64},{128,96},{160,128},{192,160},{224,192},{256... | collective-permute-start | bytes 442376 | tf_op jit(solution)/shard_map/ppermute | solution.py:370
  68.6 30.6 %copy-start.6 = (bf16[288,256]{1,0:T(8,128)(2,1)}, bf16[288,256]{1,0:T(8,128)(2,1)S(1)}, u32[]{:S(2)}) copy-start(bf16[288,256]{1,0:T(8,128)(2,1)S(1)} %collective-permute-done.2.xl_ref) | copy-start | bytes 442372
  76.7 22.5 %copy-start.7 = (bf16[288,256]{1,0:T(8,128)(2,1)}, bf16[288,256]{1,0:T(8,128)(2,1)S(1)}, u32[]{:S(2)}) copy-start(bf16[288,256]{1,0:T(8,128)(2,1)S(1)} %collective-permute-done.3.xh_ref) | copy-start | bytes 442372
  79.7 5.7 %collective-permute-start.4 = (f32[4,1024]{1,0:T(4,128)S(1)}, f32[4,1024]{1,0:T(4,128)S(1)}, u32[]{:S(2)}, u32[]{:S(2)}) collective-permute-start(f32[4,1024]{1,0:T(4,128)S(1)} %convert_reduce_fusion), channel_id=1, source_target_pairs={{1,1},{2,34},{0,67},{3,96},{5,133},{6,166},{4,199},{7,228},{9,265}... | collective-permute-start | bytes 49160 | tf_op jit(solution)/shard_map/ppermute | solution.py:406
  86.8 24.0 %all-to-all-start.2 = ((bf16[32,4,1024]{2,1,0:T(4,128)(2,1)}), bf16[32,4,1024]{2,1,0:T(4,128)(2,1)S(1)}, u32[]{:S(2)}, u32[]{:S(2)}) async-start(bf16[32,4,1024]{2,1,0:T(4,128)(2,1)} %shard_map.81), calls=%async_computation.2 | async-start | bytes 524288 | tf_op jit(solution)/shard_map/all_to_all | solution.py:408

commit v6 on v5

--- a/solution.py
+++ b/solution.py
@@ -149,30 +149,16 @@
     return y * 4 + (((t >> 1) ^ cross) & 1) * 2 + ((t ^ differ) & 1)
 
 
-def embed_kernel(
-    who_ref, patches_ref, weight_hbm, out_hbm, weight_ref, total_ref, out_ref, in_sem, out_sem
-):
+def embed_kernel(who_ref, patches_ref, weight_ref, out_hbm, out_ref, out_sem):
     seq = who_ref[0]
-    loads = []
-    for b in range(2):
-        load = pltpu.make_async_copy(weight_hbm.at[seq & 1, b], weight_ref.at[b], in_sem.at[b])
-        load.start()
-        loads.append(load)
+    left = [patches_ref[:, b].reshape(256, 512) for b in range(2)]
     size = 256
-    left = patches_ref[:, 0].reshape(256, 512)
-    loads[0].wait()
-    for n in range(4):
-        columns = pl.ds(n * size, size)
-        total_ref[:, columns] = jnp.dot(
-            left, weight_ref[0, :, columns], preferred_element_type=F32
-        )
-    left = patches_ref[:, 1].reshape(256, 512)
-    loads[1].wait()
     stores = []
     for n in range(4):
         columns = pl.ds(n * size, size)
-        product = jnp.dot(left, weight_ref[1, :, columns], preferred_element_type=F32)
-        total = (total_ref[:, columns] + product).reshape(16, 2, 2, 4, size)
+        total = jnp.dot(left[0], weight_ref[0, :, columns], preferred_element_type=F32)
+        total = total + jnp.dot(left[1], weight_ref[1, :, columns], preferred_element_type=F32)
+        total = total.reshape(16, 2, 2, 4, size)
         for a in range(2):
             for t in range(32):
                 member, _ = route((seq & 30) + a, t)
@@ -187,20 +173,13 @@
 
 
 def embed(who, patches, weight):
-    anywhere = pl.BlockSpec(memory_space=pl.ANY)
     return pl.pallas_call(
         embed_kernel,
-        in_specs=[pl.BlockSpec(memory_space=pltpu.SMEM), VMEM, anywhere],
-        out_specs=anywhere,
+        in_specs=[pl.BlockSpec(memory_space=pltpu.SMEM), VMEM, VMEM],
+        out_specs=pl.BlockSpec(memory_space=pl.ANY),
         out_shape=pltpu.HBM((2, 32, 4, 1024), BF16),
-        scratch_shapes=[
-            pltpu.VMEM((2, 512, 1024), BF16),
-            pltpu.VMEM((256, 1024), F32),
-            pltpu.VMEM((2, 32, 4, 1024), BF16),
-            pltpu.SemaphoreType.DMA((2,)),
-            pltpu.SemaphoreType.DMA((4,)),
-        ],
-        compiler_params=pltpu.CompilerParams(vmem_limit_bytes=58 << 20),
+        scratch_shapes=[pltpu.VMEM((2, 32, 4, 1024), BF16), pltpu.SemaphoreType.DMA((4,))],
+        compiler_params=ROOM,
         cost_estimate=pl.CostEstimate(flops=540000000, bytes_accessed=3 << 20, transcendentals=0),
     )(who, patches, weight)
 
@@ -237,24 +216,41 @@
     )(who, rows, position, norm_gain.reshape(1, 1024))
 
 
-def arrange_kernel(who_ref, normed_ref, out_ref):
+def head_kernel(who_ref, normed_ref, weight_ref, out_hbm, out_ref, out_sem):
     gathered = normed_ref[...].astype(F32).reshape(128, 1024).astype(BF16)
     row = lax.broadcasted_iota(jnp.int32, (128, 128), 0)
     column = lax.broadcasted_iota(jnp.int32, (128, 128), 1)
     _, mu = route(row >> 2, who_ref[0])
     order = jnp.where(column == mu * 4 + (row & 3), 1.0, 0.0).astype(BF16)
-    out_ref[...] = jnp.dot(order, gathered, preferred_element_type=F32).astype(BF16)
-
-
-def arrange(who, normed):
-    return pl.pallas_call(
-        arrange_kernel,
-        in_specs=[pl.BlockSpec(memory_space=pltpu.SMEM), VMEM],
-        out_specs=VMEM,
-        out_shape=jax.ShapeDtypeStruct((128, 1024), BF16),
+    left = jnp.dot(order, gathered, preferred_element_type=F32).astype(BF16)
+    stores = []
+    for n, (start, size) in enumerate(HEAD_COLUMNS):
+        columns = pl.ds(start, size)
+        product = jnp.dot(left, weight_ref[:, columns], preferred_element_type=F32)
+        out_ref[:, columns] = product.astype(BF16)
+        store = pltpu.make_async_copy(out_ref.at[:, columns], out_hbm.at[:, columns], out_sem.at[n])
+        store.start()
+        stores.append(store)
+    for store in stores:
+        store.wait()
+
+
+HEAD_COLUMNS = ((0, 512), (512, 512), (1024, 384))
+
+
+def head(who, normed, head_weight):
+    return pl.pallas_call(
+        head_kernel,
+        in_specs=[pl.BlockSpec(memory_space=pltpu.SMEM), VMEM, VMEM],
+        out_specs=pl.BlockSpec(memory_space=pl.ANY),
+        out_shape=jax.ShapeDtypeStruct((128, 1408), BF16),
+        scratch_shapes=[
+            pltpu.VMEM((128, 1408), BF16),
+            pltpu.SemaphoreType.DMA((len(HEAD_COLUMNS),)),
+        ],
         compiler_params=ROOM,
-        cost_estimate=pl.CostEstimate(flops=34000000, bytes_accessed=1 << 19, transcendentals=0),
-    )(who, normed)
+        cost_estimate=pl.CostEstimate(flops=370000000, bytes_accessed=4 << 20, transcendentals=0),
+    )(who, normed, head_weight)
 
 
 def advance_kernel(
@@ -388,11 +384,11 @@
     y_high = along(y_first, ("mp",), -1)
     who = jnp.stack([seq, mp]).astype(jnp.int32)
     edges = jnp.stack([seq > 0, seq < 31, mp > 0, mp < 31]).astype(F32)
-    patches, who, edges, y_low, y_high = lax.optimization_barrier(
-        (patches, who, edges, y_low, y_high)
+    weight = lax.dynamic_slice_in_dim(embed_weight, core * 1024, 1024, 0).reshape(2, 512, 1024)
+    patches, who, edges, weight, y_low, y_high = lax.optimization_barrier(
+        (patches, who, edges, weight, y_low, y_high)
     )
 
-    weight = embed_weight.reshape(2, 2, 512, 1024)
     patches = patches.reshape(16, 2, 16, 512)
     partial_sums = embed(who, patches, weight)
     pieces = lax.all_to_all(partial_sums.reshape(64, 4, 1024), ("core", "mp"), 0, 0, tiled=True)
@@ -411,9 +407,7 @@
     fields_next = advance(edges, fields, lagged_source, y_low, y_high, x_low, x_high)
     normed, fields_next = lax.optimization_barrier((normed, fields_next))
 
-    left = arrange(who, normed)
-    source_terms = jnp.dot(left, head_weight, preferred_element_type=F32).astype(BF16)
-    return fields_next, source_terms
+    return fields_next, head(who, normed, head_weight)
 
 
 def solution(mesh):

time: 114 us -> 110 us (0.965)
  waiting for transfers between devices: 27.6 us -> 25.5 us
  matrix products: 1.33 us -> 0 us
    pallas_call x1, Pallas kernels: 3.89 us -> 2.04 us  [embed(): pl.pallas_call(embed_kernel, in_specs=[pl.BlockSpec(memory_space=pltpu.SM...]
    dynamic_slice x0 -> x1, local copies, waits for them, and re-layouts: none -> 1.77 us  [on_device(): lax.dynamic_slice_in_dim(embed_weight, core * 1024, 1024, 0)]
    dot_general x1 -> x0, matrix products: 1.33 us -> none  [on_device(): jnp.dot(left, head_weight, preferred_element_type=F32).astype(BF16)]
    ppermute x4, waiting for transfers between devices: 16.6 us -> 15.4 us  [along(): return lax.ppermute(value, axes, pairs)]
  transfers between devices with their start and end apart: 8 -> 8, of which waited for: 8 -> 8; matrix products, arithmetic and copies ran while one was open for 1% -> 2% of each run, Pallas kernels for 9% -> 10%
where the time goes in v6:
time: 110 us
  starting transfers between devices  60.6 us (55%)
  waiting for transfers between devices  25.5 us (23%)
  Pallas kernels  19 us (17%)
  other arithmetic  1.98 us (2%)
  local copies, waits for them, and re-layouts  1.79 us (2%)
    all_to_all x1, starting transfers between devices, on_device(): patches = lax.all_to_all(pack(fields), 'mp', 0, 0, tiled=True)  19.5 us
    ppermute x4, waiting for transfers between devices, along(): return lax.ppermute(value, axes, pairs)  15.4 us
    ppermute x4, starting transfers between devices, along(): return lax.ppermute(value, axes, pairs)  13.5 us
    all_to_all x1, starting transfers between devices, on_device(): normed = lax.all_to_all(everyone, 'mp', 0, 0, tiled=True)  13 us
    all_to_all x1, starting transfers between devices, on_device(): lax.all_to_all(partial_sums.reshape(64, 4, 1024), ('core', 'mp'), 0, 0, t...  12.6 us
    pallas_call x1, Pallas kernels, advance(): pl.pallas_call(advance_kernel, in_specs=[pl.BlockSpec(memory_space=pltpu....  6.4 us
    all_to_all x1, waiting for transfers between devices, on_device(): normed = lax.all_to_all(everyone, 'mp', 0, 0, tiled=True)  4.57 us
    ppermute x1, waiting for transfers between devices, on_device(): rows = lax.ppermute(rows, ALL, SWAP)  3.77 us
  transfers between devices with their start and end apart: 8, of which 8 were waited for; matrix products, arithmetic and copies ran while one was open for 2% of the time, Pallas kernels for 10%

profile of v6, /device:TPU:15, one launch (start us, length us, event | category | flops | bytes accessed | tf_op | source)
XLA Modules:
  0.0 109.7 jit_solution(17513677996134634911)
XLA Ops:
  0.6 3.0 %shard_map.77 = bf16[32,16,512]{2,1,0:T(8,128)(2,1)} custom-call(f32[16,8,8,256]{3,2,1,0:T(8,128)} %fields_ref.3), custom_call_target="tpu_custom_call" | custom-call | flops 1000000 | bytes 2097152 | tf_op jit(solution)/shard_map/pallas_call | solution.py:72
  3.7 19.5 %all-to-all-start = ((bf16[32,16,512]{2,1,0:T(8,128)(2,1)}), bf16[32,16,512]{2,1,0:T(8,128)(2,1)S(1)}, u32[]{:S(2)}, u32[]{:S(2)}) async-start(bf16[32,16,512]{2,1,0:T(8,128)(2,1)} %shard_map.77), calls=%async_computation | async-start | bytes 1048576 | tf_op jit(solution)/shard_map/all_to_all | solution.py:380
  23.2 2.4 %shard_map.78 = (bf16[2,128,256]{2,1,0:T(8,128)(2,1)}, bf16[2,128,256]{2,1,0:T(8,128)(2,1)}) custom-call(f32[16,8,8,256]{3,2,1,0:T(8,128)} %fields_ref.3), custom_call_target="tpu_custom_call" | custom-call | flops 100000 | bytes 2097152 | tf_op jit(solution)/shard_map/pallas_call | solution.py:98
  25.6 3.1 %collective-permute-start = (bf16[2,128,256]{2,1,0:T(8,128)(2,1)}, bf16[2,128,256]{2,1,0:T(8,128)(2,1)S(1)}, u32[]{:S(2)}, u32[]{:S(2)}) collective-permute-start(bf16[2,128,256]{2,1,0:T(8,128)(2,1)} %get-tuple-element.18), channel_id=1, source_target_pairs={{0,1},{1,2},{2,3},{3,4},{4,5},{5,6},{6,7},{7,8},{8,9},{9,10},{10,1... | collective-permute-start | bytes 393224 | tf_op jit(solution)/shard_map/ppermute | solution.py:366
  28.7 2.2 %collective-permute-start.1 = (bf16[2,128,256]{2,1,0:T(8,128)(2,1)}, bf16[2,128,256]{2,1,0:T(8,128)(2,1)S(1)}, u32[]{:S(2)}, u32[]{:S(2)}) collective-permute-start(bf16[2,128,256]{2,1,0:T(8,128)(2,1)} %get-tuple-element.19), channel_id=1, source_target_pairs={{1,0},{2,1},{3,2},{4,3},{5,4},{6,5},{7,6},{8,7},{9,8},{10,9},{11,1... | collective-permute-start | bytes 393224 | tf_op jit(solution)/shard_map/ppermute | solution.py:366
  30.9 1.8 %constant_dynamic-slice_fusion = bf16[1024,1024]{1,0:T(8,128)(2,1)S(1)} fusion(bf16[2048,1024]{1,0:T(8,128)(2,1)} %param.8, s32[]{:T(128)S(6)} %select_n.3), kind=kLoop, calls=%fused_computation.3 | loop fusion | bytes 4194308 | tf_op jit(solution)/shard_map/dynamic_slice | solution.py:387
  32.7 0.1 pad_add_fusion.who_ref
  32.8 0.6 add_convert_fusion.edge_ref
  33.4 1.3 %collective-permute-done.y_low_ref.yl_ref = bf16[2,128,256]{2,1,0:T(8,128)(2,1)S(1)} collective-permute-done((bf16[2,128,256]{2,1,0:T(8,128)(2,1)}, bf16[2,128,256]{2,1,0:T(8,128)(2,1)S(1)}, u32[]{:S(2)}, u32[]{:S(2)}) %collective-permute-start) | collective-permute-done | bytes 131104 | tf_op jit(solution)/shard_map/ppermute | solution.py:366
  34.7 3.8 %collective-permute-done.1.y_high_ref.yh_ref = bf16[2,128,256]{2,1,0:T(8,128)(2,1)S(1)} collective-permute-done((bf16[2,128,256]{2,1,0:T(8,128)(2,1)}, bf16[2,128,256]{2,1,0:T(8,128)(2,1)S(1)}, u32[]{:S(2)}, u32[]{:S(2)}) %collective-permute-start.1) | collective-permute-done | bytes 131104 | tf_op jit(solution)/shard_map/ppermute | solution.py:366
  38.5 0.5 all-to-all-done
  39.0 2.0 %shard_map.79 = bf16[2,32,4,1024]{3,2,1,0:T(4,128)(2,1)} custom-call(s32[2]{0:T(128)S(1)} %pad_add_fusion.who_ref, bf16[16,2,16,512]{3,2,1,0:T(8,128)(2,1)S(1)} %bitcast.11, bf16[2,512,1024]{2,1,0:T(8,128)(2,1)S(1)} %bitcast.10), custom_call_target="tpu_custom_call" | custom-call | flops 540000000 | bytes 3145728 | tf_op jit(solution)/shard_map/pallas_call | solution.py:176
  41.1 12.6 %all-to-all-start.1 = ((bf16[64,4,1024]{2,1,0:T(4,128)(2,1)}), bf16[64,4,1024]{2,1,0:T(4,128)(2,1)}, u32[]{:S(2)}, u32[]{:S(2)}) async-start(bf16[64,4,1024]{2,1,0:T(4,128)(2,1)} %bitcast.13), calls=%async_computation.1 | async-start | bytes 1048576 | tf_op jit(solution)/shard_map/all_to_all | solution.py:394
  53.7 0.0 copy-done.3
  53.7 0.0 copy-done.4
  53.7 1.9 %shard_map.80 = (bf16[288,256]{1,0:T(8,128)(2,1)}, bf16[288,256]{1,0:T(8,128)(2,1)}) custom-call(f32[16,8,8,256]{3,2,1,0:T(8,128)} %fields_ref.3, f32[16,8,8,256]{3,2,1,0:T(8,128)} %fields_ref.3, bf16[2,128,256]{2,1,0:T(8,128)(2,1)} %copy-done.3, bf16[2,128,256]{2,1,0:T(8,128)(2,1)} %copy-done.4), custom_call_target="tpu_custom_call" | custom-call | flops 100000 | bytes 1048576 | tf_op jit(solution)/shard_map/pallas_call | solution.py:119
  55.6 6.3 %collective-permute-start.2 = (bf16[288,256]{1,0:T(8,128)(2,1)}, bf16[288,256]{1,0:T(8,128)(2,1)S(1)}, u32[]{:S(2)}, u32[]{:S(2)}) collective-permute-start(bf16[288,256]{1,0:T(8,128)(2,1)} %get-tuple-element.25), channel_id=1, source_target_pairs={{0,32},{32,64},{64,96},{96,128},{128,160},{160,192},{192,224},{224... | collective-permute-start | bytes 442376 | tf_op jit(solution)/shard_map/ppermute | solution.py:366
  61.9 1.9 %collective-permute-start.3 = (bf16[288,256]{1,0:T(8,128)(2,1)}, bf16[288,256]{1,0:T(8,128)(2,1)S(1)}, u32[]{:S(2)}, u32[]{:S(2)}) collective-permute-start(bf16[288,256]{1,0:T(8,128)(2,1)} %get-tuple-element.26), channel_id=1, source_target_pairs={{32,0},{64,32},{96,64},{128,96},{160,128},{192,160},{224,192},{256... | collective-permute-start | bytes 442376 | tf_op jit(solution)/shard_map/ppermute | solution.py:366
  63.8 1.7 %collective-permute-done.2.xl_ref = bf16[288,256]{1,0:T(8,128)(2,1)S(1)} collective-permute-done((bf16[288,256]{1,0:T(8,128)(2,1)}, bf16[288,256]{1,0:T(8,128)(2,1)S(1)}, u32[]{:S(2)}, u32[]{:S(2)}) %collective-permute-start.2) | collective-permute-done | bytes 147488 | tf_op jit(solution)/shard_map/ppermute | solution.py:366
  65.5 8.5 %collective-permute-done.3.xh_ref = bf16[288,256]{1,0:T(8,128)(2,1)S(1)} collective-permute-done((bf16[288,256]{1,0:T(8,128)(2,1)}, bf16[288,256]{1,0:T(8,128)(2,1)S(1)}, u32[]{:S(2)}, u32[]{:S(2)}) %collective-permute-start.3) | collective-permute-done | bytes 147488 | tf_op jit(solution)/shard_map/ppermute | solution.py:366
  74.0 1.3 %all-to-all-done.1 = bf16[64,4,1024]{2,1,0:T(4,128)(2,1)} async-done(((bf16[64,4,1024]{2,1,0:T(4,128)(2,1)}), bf16[64,4,1024]{2,1,0:T(4,128)(2,1)}, u32[]{:S(2)}, u32[]{:S(2)}) %all-to-all-start.1) | async-done | bytes 524320 | tf_op jit(solution)/shard_map/all_to_all | solution.py:394
  75.4 1.3 %convert_reduce_fusion = f32[4,1024]{1,0:T(4,128)S(1)} fusion(bf16[64,4,1024]{2,1,0:T(4,128)(2,1)} %all-to-all-done.1), kind=kLoop, calls=%fused_computation | loop fusion | flops 520192 | bytes 540672 | tf_op jit(solution)/shard_map/reduce_sum | solution.py:401
  76.7 1.9 %collective-permute-start.4 = (f32[4,1024]{1,0:T(4,128)S(1)}, f32[4,1024]{1,0:T(4,128)S(1)}, u32[]{:S(2)}, u32[]{:S(2)}) collective-permute-start(f32[4,1024]{1,0:T(4,128)S(1)} %convert_reduce_fusion), channel_id=1, source_target_pairs={{1,1},{2,34},{0,67},{3,96},{5,133},{6,166},{4,199},{7,228},{9,265}... | collective-permute-start | bytes 49160 | tf_op jit(solution)/shard_map/ppermute | solution.py:402
  78.6 3.8 %collective-permute-done.4.rows_ref = f32[4,1024]{1,0:T(4,128)S(1)} collective-permute-done((f32[4,1024]{1,0:T(4,128)S(1)}, f32[4,1024]{1,0:T(4,128)S(1)}, u32[]{:S(2)}, u32[]{:S(2)}) %collective-permute-start.4) | collective-permute-done | bytes 16416 | tf_op jit(solution)/shard_map/ppermute | solution.py:402
  82.3 0.0 copy-done.1
  82.4 1.4 %shard_map.81 = bf16[32,4,1024]{2,1,0:T(4,128)(2,1)} custom-call(s32[2]{0:T(128)S(1)} %pad_add_fusion.who_ref, f32[4,1024]{1,0:T(4,128)S(1)} %collective-permute-done.4.rows_ref, bf16[128,1024]{1,0:T(8,128)(2,1)S(1)} %copy-done.1, f32[1,1024]{1,0:T(1,128)S(1)} %bitcast.12), custom_call_target="tpu_custom_call" | custom-call | flops 100000 | bytes 300000 | tf_op jit(solution)/shard_map/pallas_call | solution.py:201
  83.7 13.0 %all-to-all-start.2 = ((bf16[32,4,1024]{2,1,0:T(4,128)(2,1)}), bf16[32,4,1024]{2,1,0:T(4,128)(2,1)S(1)}, u32[]{:S(2)}, u32[]{:S(2)}) async-start(bf16[32,4,1024]{2,1,0:T(4,128)(2,1)} %shard_map.81), calls=%async_computation.2 | async-start | bytes 524288 | tf_op jit(solution)/shard_map/all_to_all | solution.py:404
  96.8 0.0 copy-done.5
  96.8 0.0 copy-done.6
  96.8 6.4 %shard_map.82 = f32[16,8,8,256]{3,2,1,0:T(8,128)} custom-call(f32[4]{0:T(128)} %add_convert_fusion.edge_ref, f32[16,8,8,256]{3,2,1,0:T(8,128)} %fields_ref.3, bf16[13,8,8,256]{3,2,1,0:T(8,128)(2,1)} %source_ref.1, bf16[2,128,256]{2,1,0:T(8,128)(2,1)} %copy-done.3, bf16[2,128,256]{2,1,0:T(8,128)(2,1)} %copy-done.4, bf16[288,256]{1,0:T(8,128)(2,1)} %copy-done.5, ...), custom_call_target="tpu_custom_call" | custom-call | flops 100000000 | bytes 4194304 | tf_op jit(solution)/shard_map/pallas_call | solution.py:349
  103.2 4.6 %all-to-all-done.2.normed_ref = bf16[32,4,1024]{2,1,0:T(4,128)(2,1)S(1)} async-done(((bf16[32,4,1024]{2,1,0:T(4,128)(2,1)}), bf16[32,4,1024]{2,1,0:T(4,128)(2,1)S(1)}, u32[]{:S(2)}, u32[]{:S(2)}) %all-to-all-start.2) | async-done | bytes 262176 | tf_op jit(solution)/shard_map/all_to_all | solution.py:404
  107.8 1.9 %shard_map.83 = bf16[128,1408]{1,0:T(8,128)(2,1)} custom-call(s32[2]{0:T(128)S(1)} %pad_add_fusion.who_ref, bf16[32,4,1024]{2,1,0:T(4,128)(2,1)S(1)} %all-to-all-done.2.normed_ref, bf16[1024,1408]{1,0:T(8,128)(2,1)S(1)} %copy-done), custom_call_target="tpu_custom_call" | custom-call | flops 370000000 | bytes 4194304 | tf_op jit(solution)/shard_map/pallas_call | solution.py:242
  (9 shorter events, 0.0 us)
Async XLA Ops:
  3.7 35.3 %all-to-all-start = ((bf16[32,16,512]{2,1,0:T(8,128)(2,1)}), bf16[32,16,512]{2,1,0:T(8,128)(2,1)S(1)}, u32[]{:S(2)}, u32[]{:S(2)}) async-start(bf16[32,16,512]{2,1,0:T(8,128)(2,1)} %shard_map.77), calls=%async_computation | async-start | bytes 1048576 | tf_op jit(solution)/shard_map/all_to_all | solution.py:380
  25.6 9.1 %collective-permute-start = (bf16[2,128,256]{2,1,0:T(8,128)(2,1)}, bf16[2,128,256]{2,1,0:T(8,128)(2,1)S(1)}, u32[]{:S(2)}, u32[]{:S(2)}) collective-permute-start(bf16[2,128,256]{2,1,0:T(8,128)(2,1)} %get-tuple-element.18), channel_id=1, source_target_pairs={{0,1},{1,2},{2,3},{3,4},{4,5},{5,6},{6,7},{7,8},{8,9},{9,10},{10,1... | collective-permute-start | bytes 393224 | tf_op jit(solution)/shard_map/ppermute | solution.py:366
  28.7 9.8 %collective-permute-start.1 = (bf16[2,128,256]{2,1,0:T(8,128)(2,1)}, bf16[2,128,256]{2,1,0:T(8,128)(2,1)S(1)}, u32[]{:S(2)}, u32[]{:S(2)}) collective-permute-start(bf16[2,128,256]{2,1,0:T(8,128)(2,1)} %get-tuple-element.19), channel_id=1, source_target_pairs={{1,0},{2,1},{3,2},{4,3},{5,4},{6,5},{7,6},{8,7},{9,8},{10,9},{11,1... | collective-permute-start | bytes 393224 | tf_op jit(solution)/shard_map/ppermute | solution.py:366
  34.7 19.0 %copy-start.3 = (bf16[2,128,256]{2,1,0:T(8,128)(2,1)}, bf16[2,128,256]{2,1,0:T(8,128)(2,1)S(1)}, u32[]{:S(2)}) copy-start(bf16[2,128,256]{2,1,0:T(8,128)(2,1)S(1)} %collective-permute-done.y_low_ref.yl_ref) | copy-start | bytes 393220
  38.5 15.2 %copy-start.4 = (bf16[2,128,256]{2,1,0:T(8,128)(2,1)}, bf16[2,128,256]{2,1,0:T(8,128)(2,1)S(1)}, u32[]{:S(2)}) copy-start(bf16[2,128,256]{2,1,0:T(8,128)(2,1)S(1)} %collective-permute-done.1.y_high_ref.yh_ref) | copy-start | bytes 393220
  39.0 43.3 %copy-start.1 = (bf16[128,1024]{1,0:T(8,128)(2,1)S(1)}, bf16[128,1024]{1,0:T(8,128)(2,1)}, u32[]{:S(2)}) copy-start(bf16[128,1024]{1,0:T(8,128)(2,1)} %position_ref.1) | copy-start | bytes 786436
  39.0 43.3 %copy-start.2 = (f32[1024]{0:T(1024)S(1)}, f32[1024]{0:T(1024)}, u32[]{:S(2)}) copy-start(f32[1024]{0:T(1024)} %param.10) | copy-start | bytes 12292
  41.1 34.3 %all-to-all-start.1 = ((bf16[64,4,1024]{2,1,0:T(4,128)(2,1)}), bf16[64,4,1024]{2,1,0:T(4,128)(2,1)}, u32[]{:S(2)}, u32[]{:S(2)}) async-start(bf16[64,4,1024]{2,1,0:T(4,128)(2,1)} %bitcast.13), calls=%async_computation.1 | async-start | bytes 1048576 | tf_op jit(solution)/shard_map/all_to_all | solution.py:394
  55.6 52.2 %copy-start = (bf16[1024,1408]{1,0:T(8,128)(2,1)S(1)}, bf16[1024,1408]{1,0:T(8,128)(2,1)}, u32[]{:S(2)}) copy-start(bf16[1024,1408]{1,0:T(8,128)(2,1)} %weight_ref.1) | copy-start | bytes 8650756
  55.6 10.0 %collective-permute-start.2 = (bf16[288,256]{1,0:T(8,128)(2,1)}, bf16[288,256]{1,0:T(8,128)(2,1)S(1)}, u32[]{:S(2)}, u32[]{:S(2)}) collective-permute-start(bf16[288,256]{1,0:T(8,128)(2,1)} %get-tuple-element.25), channel_id=1, source_target_pairs={{0,32},{32,64},{64,96},{96,128},{128,160},{160,192},{192,224},{224... | collective-permute-start | bytes 442376 | tf_op jit(solution)/shard_map/ppermute | solution.py:366
  61.9 12.1 %collective-permute-start.3 = (bf16[288,256]{1,0:T(8,128)(2,1)}, bf16[288,256]{1,0:T(8,128)(2,1)S(1)}, u32[]{:S(2)}, u32[]{:S(2)}) collective-permute-start(bf16[288,256]{1,0:T(8,128)(2,1)} %get-tuple-element.26), channel_id=1, source_target_pairs={{32,0},{64,32},{96,64},{128,96},{160,128},{192,160},{224,192},{256... | collective-permute-start | bytes 442376 | tf_op jit(solution)/shard_map/ppermute | solution.py:366
  65.5 31.2 %copy-start.5 = (bf16[288,256]{1,0:T(8,128)(2,1)}, bf16[288,256]{1,0:T(8,128)(2,1)S(1)}, u32[]{:S(2)}) copy-start(bf16[288,256]{1,0:T(8,128)(2,1)S(1)} %collective-permute-done.2.xl_ref) | copy-start | bytes 442372
  74.0 22.8 %copy-start.6 = (bf16[288,256]{1,0:T(8,128)(2,1)}, bf16[288,256]{1,0:T(8,128)(2,1)S(1)}, u32[]{:S(2)}) copy-start(bf16[288,256]{1,0:T(8,128)(2,1)S(1)} %collective-permute-done.3.xh_ref) | copy-start | bytes 442372
  76.7 5.7 %collective-permute-start.4 = (f32[4,1024]{1,0:T(4,128)S(1)}, f32[4,1024]{1,0:T(4,128)S(1)}, u32[]{:S(2)}, u32[]{:S(2)}) collective-permute-start(f32[4,1024]{1,0:T(4,128)S(1)} %convert_reduce_fusion), channel_id=1, source_target_pairs={{1,1},{2,34},{0,67},{3,96},{5,133},{6,166},{4,199},{7,228},{9,265}... | collective-permute-start | bytes 49160 | tf_op jit(solution)/shard_map/ppermute | solution.py:402
  83.7 24.0 %all-to-all-start.2 = ((bf16[32,4,1024]{2,1,0:T(4,128)(2,1)}), bf16[32,4,1024]{2,1,0:T(4,128)(2,1)S(1)}, u32[]{:S(2)}, u32[]{:S(2)}) async-start(bf16[32,4,1024]{2,1,0:T(4,128)(2,1)} %shard_map.81), calls=%async_computation.2 | async-start | bytes 524288 | tf_op jit(solution)/shard_map/all_to_all | solution.py:404

commit v7 on v6

--- a/solution.py
+++ b/solution.py
@@ -149,8 +149,9 @@
     return y * 4 + (((t >> 1) ^ cross) & 1) * 2 + ((t ^ differ) & 1)
 
 
-def embed_kernel(who_ref, patches_ref, weight_ref, out_hbm, out_ref, out_sem):
+def embed_kernel(who_ref, patches_ref, weight_ref, keep_ref, send_hbm, send_ref, out_sem):
     seq = who_ref[0]
+    other = (seq & 1) == 1
     left = [patches_ref[:, b].reshape(256, 512) for b in range(2)]
     size = 256
     stores = []
@@ -158,13 +159,14 @@
         columns = pl.ds(n * size, size)
         total = jnp.dot(left[0], weight_ref[0, :, columns], preferred_element_type=F32)
         total = total + jnp.dot(left[1], weight_ref[1, :, columns], preferred_element_type=F32)
-        total = total.reshape(16, 2, 2, 4, size)
-        for a in range(2):
-            for t in range(32):
-                member, _ = route((seq & 30) + a, t)
-                out_ref[a, member, :, columns] = total[t % 16, t // 16, a].astype(BF16)
+        total = total.reshape(16, 2, 8, size)
+        for t in range(32):
+            rows = total[t % 16, t // 16]
+            rows = jnp.where(other, pltpu.roll(rows, 4, 0), rows)
+            keep_ref[route(seq, t)[0], :, columns] = rows[0:4]
+            send_ref[route(seq ^ 1, t)[0], :, columns] = rows[4:8].astype(BF16)
         store = pltpu.make_async_copy(
-            out_ref.at[:, :, :, columns], out_hbm.at[:, :, :, columns], out_sem.at[n]
+            send_ref.at[:, :, columns], send_hbm.at[:, :, columns], out_sem.at[n]
         )
         store.start()
         stores.append(store)
@@ -176,9 +178,12 @@
     return pl.pallas_call(
         embed_kernel,
         in_specs=[pl.BlockSpec(memory_space=pltpu.SMEM), VMEM, VMEM],
-        out_specs=pl.BlockSpec(memory_space=pl.ANY),
-        out_shape=pltpu.HBM((2, 32, 4, 1024), BF16),
-        scratch_shapes=[pltpu.VMEM((2, 32, 4, 1024), BF16), pltpu.SemaphoreType.DMA((4,))],
+        out_specs=[VMEM, pl.BlockSpec(memory_space=pl.ANY)],
+        out_shape=[
+            jax.ShapeDtypeStruct((32, 4, 1024), F32),
+            pltpu.HBM((32, 4, 1024), BF16),
+        ],
+        scratch_shapes=[pltpu.VMEM((32, 4, 1024), BF16), pltpu.SemaphoreType.DMA((4,))],
         compiler_params=ROOM,
         cost_estimate=pl.CostEstimate(flops=540000000, bytes_accessed=3 << 20, transcendentals=0),
     )(who, patches, weight)
@@ -390,8 +395,10 @@
     )
 
     patches = patches.reshape(16, 2, 16, 512)
-    partial_sums = embed(who, patches, weight)
-    pieces = lax.all_to_all(partial_sums.reshape(64, 4, 1024), ("core", "mp"), 0, 0, tiled=True)
+    keep, send = embed(who, patches, weight)
+    theirs = lax.ppermute(send, "core", [(0, 1), (1, 0)])
+    partial_sums = (keep + theirs.astype(F32)).astype(BF16)
+    pieces = lax.all_to_all(partial_sums, "mp", 0, 0, tiled=True)
 
     x_first, x_last = x_edges(fields, y_low, y_high)
     x_low = along(x_last, x_axes, 1)

time: 110 us -> 114 us (1.036)
  starting transfers between devices: 60.6 us -> 63.8 us
    ppermute x0 -> x1, starting transfers between devices: none -> 4.74 us  [on_device(): theirs = lax.ppermute(send, 'core', [(0, 1), (1, 0)])]
    all_to_all x1, starting transfers between devices: 12.6 us -> 9.4 us  [on_device(): pieces = lax.all_to_all(partial_sums, 'mp', 0, 0, tiled=True)]
    ppermute x0 -> x1, waiting for transfers between devices: none -> 1.35 us  [on_device(): theirs = lax.ppermute(send, 'core', [(0, 1), (1, 0)])]
    all_to_all x1, waiting for transfers between devices: 1.33 us -> 0.01 us  [on_device(): pieces = lax.all_to_all(partial_sums, 'mp', 0, 0, tiled=True)]
    all_to_all x1, starting transfers between devices: 13 us -> 14.3 us  [on_device(): normed = lax.all_to_all(everyone, 'mp', 0, 0, tiled=True)]
    reduce_sum x1, other arithmetic: 1.28 us -> 0.12 us  [on_device(): rows = jnp.sum(pieces.astype(F32), 0)]
  transfers between devices with their start and end apart: 8 -> 9, of which waited for: 8 -> 8; matrix products, arithmetic and copies ran while one was open for 2% -> 2% of each run, Pallas kernels for 10% -> 10%
where the time goes in v7:
time: 114 us; the launch traced here: 113 us
  starting transfers between devices  63.8 us (56%)
  waiting for transfers between devices  24.9 us (22%)
  Pallas kernels  19.2 us (17%)
  local copies, waits for them, and re-layouts  2.6 us (2%)
  other arithmetic  1.71 us (2%)
    all_to_all x1, starting transfers between devices, on_device(): patches = lax.all_to_all(pack(fields), 'mp', 0, 0, tiled=True)  19.5 us
    ppermute x4, waiting for transfers between devices, along(): return lax.ppermute(value, axes, pairs)  15.5 us
    all_to_all x1, starting transfers between devices, on_device(): normed = lax.all_to_all(everyone, 'mp', 0, 0, tiled=True)  14.3 us
    ppermute x4, starting transfers between devices, along(): return lax.ppermute(value, axes, pairs)  13.9 us
    all_to_all x1, starting transfers between devices, on_device(): pieces = lax.all_to_all(partial_sums, 'mp', 0, 0, tiled=True)  9.4 us
    pallas_call x1, Pallas kernels, advance(): pl.pallas_call(advance_kernel, in_specs=[pl.BlockSpec(memory_space=pltpu....  6.4 us
    ppermute x1, starting transfers between devices, on_device(): theirs = lax.ppermute(send, 'core', [(0, 1), (1, 0)])  4.74 us
    all_to_all x1, waiting for transfers between devices, on_device(): normed = lax.all_to_all(everyone, 'mp', 0, 0, tiled=True)  3.77 us
  transfers between devices with their start and end apart: 9, of which 8 were waited for; matrix products, arithmetic and copies ran while one was open for 2% of the time, Pallas kernels for 10%

profile of v7, /device:TPU:15, one launch (start us, length us, event | category | flops | bytes accessed | tf_op | source)
XLA Modules:
  0.0 113.0 jit_solution(5792050662477161188)
XLA Ops:
  0.6 3.0 %shard_map.77 = bf16[32,16,512]{2,1,0:T(8,128)(2,1)} custom-call(f32[16,8,8,256]{3,2,1,0:T(8,128)} %fields_ref.3), custom_call_target="tpu_custom_call" | custom-call | flops 1000000 | bytes 2097152 | tf_op jit(solution)/shard_map/pallas_call | solution.py:72
  3.7 19.5 %all-to-all-start = ((bf16[32,16,512]{2,1,0:T(8,128)(2,1)}), bf16[32,16,512]{2,1,0:T(8,128)(2,1)S(1)}, u32[]{:S(2)}, u32[]{:S(2)}) async-start(bf16[32,16,512]{2,1,0:T(8,128)(2,1)} %shard_map.77), calls=%async_computation | async-start | bytes 1048576 | tf_op jit(solution)/shard_map/all_to_all | solution.py:385
  23.2 2.4 %shard_map.78 = (bf16[2,128,256]{2,1,0:T(8,128)(2,1)}, bf16[2,128,256]{2,1,0:T(8,128)(2,1)}) custom-call(f32[16,8,8,256]{3,2,1,0:T(8,128)} %fields_ref.3), custom_call_target="tpu_custom_call" | custom-call | flops 100000 | bytes 2097152 | tf_op jit(solution)/shard_map/pallas_call | solution.py:98
  25.6 3.1 %collective-permute-start = (bf16[2,128,256]{2,1,0:T(8,128)(2,1)}, bf16[2,128,256]{2,1,0:T(8,128)(2,1)S(1)}, u32[]{:S(2)}, u32[]{:S(2)}) collective-permute-start(bf16[2,128,256]{2,1,0:T(8,128)(2,1)} %get-tuple-element.20), channel_id=1, source_target_pairs={{0,1},{1,2},{2,3},{3,4},{4,5},{5,6},{6,7},{7,8},{8,9},{9,10},{10,1... | collective-permute-start | bytes 393224 | tf_op jit(solution)/shard_map/ppermute | solution.py:371
  28.7 2.2 %collective-permute-start.1 = (bf16[2,128,256]{2,1,0:T(8,128)(2,1)}, bf16[2,128,256]{2,1,0:T(8,128)(2,1)S(1)}, u32[]{:S(2)}, u32[]{:S(2)}) collective-permute-start(bf16[2,128,256]{2,1,0:T(8,128)(2,1)} %get-tuple-element.21), channel_id=1, source_target_pairs={{1,0},{2,1},{3,2},{4,3},{5,4},{6,5},{7,6},{8,7},{9,8},{10,9},{11,1... | collective-permute-start | bytes 393224 | tf_op jit(solution)/shard_map/ppermute | solution.py:371
  30.9 1.8 %constant_dynamic-slice_fusion = bf16[1024,1024]{1,0:T(8,128)(2,1)S(1)} fusion(bf16[2048,1024]{1,0:T(8,128)(2,1)} %param.8, s32[]{:T(128)S(6)} %select_n.3), kind=kLoop, calls=%fused_computation.4 | loop fusion | bytes 4194308 | tf_op jit(solution)/shard_map/dynamic_slice | solution.py:392
  32.7 0.1 pad_add_fusion.who_ref
  32.8 0.6 add_convert_fusion.1.edge_ref
  33.4 1.3 %collective-permute-done.y_low_ref.yl_ref = bf16[2,128,256]{2,1,0:T(8,128)(2,1)S(1)} collective-permute-done((bf16[2,128,256]{2,1,0:T(8,128)(2,1)}, bf16[2,128,256]{2,1,0:T(8,128)(2,1)S(1)}, u32[]{:S(2)}, u32[]{:S(2)}) %collective-permute-start) | collective-permute-done | bytes 131104 | tf_op jit(solution)/shard_map/ppermute | solution.py:371
  34.7 3.8 %collective-permute-done.1.y_high_ref.yh_ref = bf16[2,128,256]{2,1,0:T(8,128)(2,1)S(1)} collective-permute-done((bf16[2,128,256]{2,1,0:T(8,128)(2,1)}, bf16[2,128,256]{2,1,0:T(8,128)(2,1)S(1)}, u32[]{:S(2)}, u32[]{:S(2)}) %collective-permute-start.1) | collective-permute-done | bytes 131104 | tf_op jit(solution)/shard_map/ppermute | solution.py:371
  38.5 0.5 all-to-all-done
  39.0 0.2 copy-done.4
  39.2 2.0 %shard_map.79 = (f32[32,4,1024]{2,1,0:T(4,128)S(1)}, bf16[32,4,1024]{2,1,0:T(4,128)(2,1)}) custom-call(s32[2]{0:T(128)S(1)} %pad_add_fusion.who_ref, bf16[16,2,16,512]{3,2,1,0:T(8,128)(2,1)S(1)} %bitcast.10, bf16[2,512,1024]{2,1,0:T(8,128)(2,1)S(1)} %bitcast.9), custom_call_target="tpu_custom_call" | custom-call | flops 540000000 | bytes 3145728 | tf_op jit(solution)/shard_map/pallas_call | solution.py:178
  41.2 4.7 %collective-permute-start.2 = (bf16[32,4,1024]{2,1,0:T(4,128)(2,1)}, bf16[32,4,1024]{2,1,0:T(4,128)(2,1)S(1)}, u32[]{:S(2)}, u32[]{:S(2)}) collective-permute-start(bf16[32,4,1024]{2,1,0:T(4,128)(2,1)} %get-tuple-element.26), channel_id=1, source_target_pairs={{0,32},{32,0},{1,33},{33,1},{2,34},{34,2},{3,35},{35,3},{4,36},{36... | collective-permute-start | bytes 786440 | tf_op jit(solution)/shard_map/ppermute | solution.py:399
  45.9 1.4 %collective-permute-done.2 = bf16[32,4,1024]{2,1,0:T(4,128)(2,1)S(1)} collective-permute-done((bf16[32,4,1024]{2,1,0:T(4,128)(2,1)}, bf16[32,4,1024]{2,1,0:T(4,128)(2,1)S(1)}, u32[]{:S(2)}, u32[]{:S(2)}) %collective-permute-start.2) | collective-permute-done | bytes 262176 | tf_op jit(solution)/shard_map/ppermute | solution.py:399
  47.3 0.9 add_convert_fusion
  48.2 9.4 %all-to-all-start.1 = ((bf16[32,4,1024]{2,1,0:T(4,128)(2,1)}), bf16[32,4,1024]{2,1,0:T(4,128)(2,1)S(1)}, u32[]{:S(2)}, u32[]{:S(2)}) async-start(bf16[32,4,1024]{2,1,0:T(4,128)(2,1)} %add_convert_fusion), calls=%async_computation.1 | async-start | bytes 524288 | tf_op jit(solution)/shard_map/all_to_all | solution.py:401
  57.6 0.0 copy-start
  57.6 2.0 %shard_map.80 = (bf16[288,256]{1,0:T(8,128)(2,1)}, bf16[288,256]{1,0:T(8,128)(2,1)}) custom-call(f32[16,8,8,256]{3,2,1,0:T(8,128)} %fields_ref.3, f32[16,8,8,256]{3,2,1,0:T(8,128)} %fields_ref.3, bf16[2,128,256]{2,1,0:T(8,128)(2,1)} %copy-done.3, bf16[2,128,256]{2,1,0:T(8,128)(2,1)} %copy-done.4), custom_call_target="tpu_custom_call" | custom-call | flops 100000 | bytes 1048576 | tf_op jit(solution)/shard_map/pallas_call | solution.py:119
  59.6 6.7 %collective-permute-start.3 = (bf16[288,256]{1,0:T(8,128)(2,1)}, bf16[288,256]{1,0:T(8,128)(2,1)S(1)}, u32[]{:S(2)}, u32[]{:S(2)}) collective-permute-start(bf16[288,256]{1,0:T(8,128)(2,1)} %get-tuple-element.29), channel_id=1, source_target_pairs={{0,32},{32,64},{64,96},{96,128},{128,160},{160,192},{192,224},{224... | collective-permute-start | bytes 442376 | tf_op jit(solution)/shard_map/ppermute | solution.py:371
  66.3 1.9 %collective-permute-start.4 = (bf16[288,256]{1,0:T(8,128)(2,1)}, bf16[288,256]{1,0:T(8,128)(2,1)}, u32[]{:S(2)}, u32[]{:S(2)}) collective-permute-start(bf16[288,256]{1,0:T(8,128)(2,1)} %get-tuple-element.30), channel_id=1, source_target_pairs={{32,0},{64,32},{96,64},{128,96},{160,128},{192,160},{224,192},{256... | collective-permute-start | bytes 442376 | tf_op jit(solution)/shard_map/ppermute | solution.py:371
  68.3 1.3 %collective-permute-done.3.xl_ref = bf16[288,256]{1,0:T(8,128)(2,1)S(1)} collective-permute-done((bf16[288,256]{1,0:T(8,128)(2,1)}, bf16[288,256]{1,0:T(8,128)(2,1)S(1)}, u32[]{:S(2)}, u32[]{:S(2)}) %collective-permute-start.3) | collective-permute-done | bytes 147488 | tf_op jit(solution)/shard_map/ppermute | solution.py:371
  69.6 0.7 copy-done.5
  70.3 9.1 %collective-permute-done.4.xh_ref = bf16[288,256]{1,0:T(8,128)(2,1)} collective-permute-done((bf16[288,256]{1,0:T(8,128)(2,1)}, bf16[288,256]{1,0:T(8,128)(2,1)}, u32[]{:S(2)}, u32[]{:S(2)}) %collective-permute-start.4) | collective-permute-done | bytes 147488 | tf_op jit(solution)/shard_map/ppermute | solution.py:371
  79.3 0.1 convert_reduce_fusion
  79.5 1.9 %collective-permute-start.5 = (f32[4,1024]{1,0:T(4,128)S(1)}, f32[4,1024]{1,0:T(4,128)S(1)}, u32[]{:S(2)}, u32[]{:S(2)}) collective-permute-start(f32[4,1024]{1,0:T(4,128)S(1)} %convert_reduce_fusion), channel_id=1, source_target_pairs={{1,1},{2,34},{0,67},{3,96},{5,133},{6,166},{4,199},{7,228},{9,265}... | collective-permute-start | bytes 49160 | tf_op jit(solution)/shard_map/ppermute | solution.py:409
  81.4 3.8 %collective-permute-done.5.rows_ref = f32[4,1024]{1,0:T(4,128)S(1)} collective-permute-done((f32[4,1024]{1,0:T(4,128)S(1)}, f32[4,1024]{1,0:T(4,128)S(1)}, u32[]{:S(2)}, u32[]{:S(2)}) %collective-permute-start.5) | collective-permute-done | bytes 16416 | tf_op jit(solution)/shard_map/ppermute | solution.py:409
  85.2 1.4 %shard_map.81 = bf16[32,4,1024]{2,1,0:T(4,128)(2,1)} custom-call(s32[2]{0:T(128)S(1)} %pad_add_fusion.who_ref, f32[4,1024]{1,0:T(4,128)S(1)} %collective-permute-done.5.rows_ref, bf16[128,1024]{1,0:T(8,128)(2,1)S(1)} %copy-done.1, f32[1,1024]{1,0:T(1,128)S(1)} %bitcast.11), custom_call_target="tpu_custom_call" | custom-call | flops 100000 | bytes 300000 | tf_op jit(solution)/shard_map/pallas_call | solution.py:206
  86.5 14.3 %all-to-all-start.2 = ((bf16[32,4,1024]{2,1,0:T(4,128)(2,1)}), bf16[32,4,1024]{2,1,0:T(4,128)(2,1)S(1)}, u32[]{:S(2)}, u32[]{:S(2)}) async-start(bf16[32,4,1024]{2,1,0:T(4,128)(2,1)} %shard_map.81), calls=%async_computation.2 | async-start | bytes 524288 | tf_op jit(solution)/shard_map/all_to_all | solution.py:411
  100.9 6.4 %shard_map.82 = f32[16,8,8,256]{3,2,1,0:T(8,128)} custom-call(f32[4]{0:T(128)} %add_convert_fusion.1.edge_ref, f32[16,8,8,256]{3,2,1,0:T(8,128)} %fields_ref.3, bf16[13,8,8,256]{3,2,1,0:T(8,128)(2,1)} %source_ref.1, bf16[2,128,256]{2,1,0:T(8,128)(2,1)} %copy-done.3, bf16[2,128,256]{2,1,0:T(8,128)(2,1)} %copy-done.4, bf16[288,256]{1,0:T(8,128)(2,1)} %copy-done.5, ...), custom_call_target="tpu_custom_call" | custom-call | flops 100000000 | bytes 4194304 | tf_op jit(solution)/shard_map/pallas_call | solution.py:354
  107.3 3.8 %all-to-all-done.2.normed_ref = bf16[32,4,1024]{2,1,0:T(4,128)(2,1)S(1)} async-done(((bf16[32,4,1024]{2,1,0:T(4,128)(2,1)}), bf16[32,4,1024]{2,1,0:T(4,128)(2,1)S(1)}, u32[]{:S(2)}, u32[]{:S(2)}) %all-to-all-start.2) | async-done | bytes 262176 | tf_op jit(solution)/shard_map/all_to_all | solution.py:411
  111.0 1.9 %shard_map.83 = bf16[128,1408]{1,0:T(8,128)(2,1)} custom-call(s32[2]{0:T(128)S(1)} %pad_add_fusion.who_ref, bf16[32,4,1024]{2,1,0:T(4,128)(2,1)S(1)} %all-to-all-done.2.normed_ref, bf16[1024,1408]{1,0:T(8,128)(2,1)S(1)} %copy-done), custom_call_target="tpu_custom_call" | custom-call | flops 370000000 | bytes 4194304 | tf_op jit(solution)/shard_map/pallas_call | solution.py:247
  (10 shorter events, 0.0 us)
Async XLA Ops:
  3.7 35.3 %all-to-all-start = ((bf16[32,16,512]{2,1,0:T(8,128)(2,1)}), bf16[32,16,512]{2,1,0:T(8,128)(2,1)S(1)}, u32[]{:S(2)}, u32[]{:S(2)}) async-start(bf16[32,16,512]{2,1,0:T(8,128)(2,1)} %shard_map.77), calls=%async_computation | async-start | bytes 1048576 | tf_op jit(solution)/shard_map/all_to_all | solution.py:385
  25.6 9.1 %collective-permute-start = (bf16[2,128,256]{2,1,0:T(8,128)(2,1)}, bf16[2,128,256]{2,1,0:T(8,128)(2,1)S(1)}, u32[]{:S(2)}, u32[]{:S(2)}) collective-permute-start(bf16[2,128,256]{2,1,0:T(8,128)(2,1)} %get-tuple-element.20), channel_id=1, source_target_pairs={{0,1},{1,2},{2,3},{3,4},{4,5},{5,6},{6,7},{7,8},{8,9},{9,10},{10,1... | collective-permute-start | bytes 393224 | tf_op jit(solution)/shard_map/ppermute | solution.py:371
  28.7 9.8 %collective-permute-start.1 = (bf16[2,128,256]{2,1,0:T(8,128)(2,1)}, bf16[2,128,256]{2,1,0:T(8,128)(2,1)S(1)}, u32[]{:S(2)}, u32[]{:S(2)}) collective-permute-start(bf16[2,128,256]{2,1,0:T(8,128)(2,1)} %get-tuple-element.21), channel_id=1, source_target_pairs={{1,0},{2,1},{3,2},{4,3},{5,4},{6,5},{7,6},{8,7},{9,8},{10,9},{11,1... | collective-permute-start | bytes 393224 | tf_op jit(solution)/shard_map/ppermute | solution.py:371
  34.7 22.8 %copy-start.3 = (bf16[2,128,256]{2,1,0:T(8,128)(2,1)}, bf16[2,128,256]{2,1,0:T(8,128)(2,1)S(1)}, u32[]{:S(2)}) copy-start(bf16[2,128,256]{2,1,0:T(8,128)(2,1)S(1)} %collective-permute-done.y_low_ref.yl_ref) | copy-start | bytes 393220
  38.5 0.7 copy-start.4
  39.2 46.0 %copy-start.1 = (bf16[128,1024]{1,0:T(8,128)(2,1)S(1)}, bf16[128,1024]{1,0:T(8,128)(2,1)}, u32[]{:S(2)}) copy-start(bf16[128,1024]{1,0:T(8,128)(2,1)} %position_ref.1) | copy-start | bytes 786436
  39.2 46.0 %copy-start.2 = (f32[1024]{0:T(1024)S(1)}, f32[1024]{0:T(1024)}, u32[]{:S(2)}) copy-start(f32[1024]{0:T(1024)} %param.10) | copy-start | bytes 12292
  41.2 6.1 %collective-permute-start.2 = (bf16[32,4,1024]{2,1,0:T(4,128)(2,1)}, bf16[32,4,1024]{2,1,0:T(4,128)(2,1)S(1)}, u32[]{:S(2)}, u32[]{:S(2)}) collective-permute-start(bf16[32,4,1024]{2,1,0:T(4,128)(2,1)} %get-tuple-element.26), channel_id=1, source_target_pairs={{0,32},{32,0},{1,33},{33,1},{2,34},{34,2},{3,35},{35,3},{4,36},{36... | collective-permute-start | bytes 786440 | tf_op jit(solution)/shard_map/ppermute | solution.py:399
  48.2 31.2 %all-to-all-start.1 = ((bf16[32,4,1024]{2,1,0:T(4,128)(2,1)}), bf16[32,4,1024]{2,1,0:T(4,128)(2,1)S(1)}, u32[]{:S(2)}, u32[]{:S(2)}) async-start(bf16[32,4,1024]{2,1,0:T(4,128)(2,1)} %add_convert_fusion), calls=%async_computation.1 | async-start | bytes 524288 | tf_op jit(solution)/shard_map/all_to_all | solution.py:401
  57.6 53.5 %copy-start = (bf16[1024,1408]{1,0:T(8,128)(2,1)S(1)}, bf16[1024,1408]{1,0:T(8,128)(2,1)}, u32[]{:S(2)}) copy-start(bf16[1024,1408]{1,0:T(8,128)(2,1)} %weight_ref.1) | copy-start | bytes 8650756
  59.6 10.0 %collective-permute-start.3 = (bf16[288,256]{1,0:T(8,128)(2,1)}, bf16[288,256]{1,0:T(8,128)(2,1)S(1)}, u32[]{:S(2)}, u32[]{:S(2)}) collective-permute-start(bf16[288,256]{1,0:T(8,128)(2,1)} %get-tuple-element.29), channel_id=1, source_target_pairs={{0,32},{32,64},{64,96},{96,128},{128,160},{160,192},{192,224},{224... | collective-permute-start | bytes 442376 | tf_op jit(solution)/shard_map/ppermute | solution.py:371
  66.3 13.0 %collective-permute-start.4 = (bf16[288,256]{1,0:T(8,128)(2,1)}, bf16[288,256]{1,0:T(8,128)(2,1)}, u32[]{:S(2)}, u32[]{:S(2)}) collective-permute-start(bf16[288,256]{1,0:T(8,128)(2,1)} %get-tuple-element.30), channel_id=1, source_target_pairs={{32,0},{64,32},{96,64},{128,96},{160,128},{192,160},{224,192},{256... | collective-permute-start | bytes 442376 | tf_op jit(solution)/shard_map/ppermute | solution.py:371
  69.6 0.7 copy-start.5
  79.5 5.7 %collective-permute-start.5 = (f32[4,1024]{1,0:T(4,128)S(1)}, f32[4,1024]{1,0:T(4,128)S(1)}, u32[]{:S(2)}, u32[]{:S(2)}) collective-permute-start(f32[4,1024]{1,0:T(4,128)S(1)} %convert_reduce_fusion), channel_id=1, source_target_pairs={{1,1},{2,34},{0,67},{3,96},{5,133},{6,166},{4,199},{7,228},{9,265}... | collective-permute-start | bytes 49160 | tf_op jit(solution)/shard_map/ppermute | solution.py:409
  86.5 24.5 %all-to-all-start.2 = ((bf16[32,4,1024]{2,1,0:T(4,128)(2,1)}), bf16[32,4,1024]{2,1,0:T(4,128)(2,1)S(1)}, u32[]{:S(2)}, u32[]{:S(2)}) async-start(bf16[32,4,1024]{2,1,0:T(4,128)(2,1)} %shard_map.81), calls=%async_computation.2 | async-start | bytes 524288 | tf_op jit(solution)/shard_map/all_to_all | solution.py:411

commit v8 on v7

--- a/solution.py
+++ b/solution.py
@@ -401,15 +401,15 @@
     pieces = lax.all_to_all(partial_sums, "mp", 0, 0, tiled=True)
 
     x_first, x_last = x_edges(fields, y_low, y_high)
-    x_low = along(x_last, x_axes, 1)
-    x_high = along(x_first, x_axes, -1)
-    pieces, x_low, x_high = lax.optimization_barrier((pieces, x_low, x_high))
+    pieces, x_first, x_last = lax.optimization_barrier((pieces, x_first, x_last))
 
     rows = jnp.sum(pieces.astype(F32), 0)
     rows = lax.ppermute(rows, ALL, SWAP)
     everyone = norm(who, rows, position, norm_gain)
     normed = lax.all_to_all(everyone, "mp", 0, 0, tiled=True)
 
+    x_low = along(x_last, x_axes, 1)
+    x_high = along(x_first, x_axes, -1)
     edges, _ = lax.optimization_barrier((edges, everyone))
     fields_next = advance(edges, fields, lagged_source, y_low, y_high, x_low, x_high)
     normed, fields_next = lax.optimization_barrier((normed, fields_next))

time: 114 us -> 117 us (1.026)
  waiting for transfers between devices: 24.9 us -> 28.4 us
    all_to_all x1, waiting for transfers between devices: 0.01 us -> 9.09 us  [on_device(): pieces = lax.all_to_all(partial_sums, 'mp', 0, 0, tiled=True)]
    all_to_all x1, waiting for transfers between devices: 3.77 us -> 0.01 us  [on_device(): normed = lax.all_to_all(everyone, 'mp', 0, 0, tiled=True)]
    all_to_all x1, starting transfers between devices: 14.3 us -> 10.7 us  [on_device(): normed = lax.all_to_all(everyone, 'mp', 0, 0, tiled=True)]
    ppermute x1, waiting for transfers between devices: 3.77 us -> 1.29 us  [on_device(): rows = lax.ppermute(rows, ALL, SWAP)]
    ppermute x1, starting transfers between devices: 1.91 us -> 4.39 us  [on_device(): rows = lax.ppermute(rows, ALL, SWAP)]
  transfers between devices with their start and end apart: 9 -> 9, of which waited for: 8 -> 8; matrix products, arithmetic and copies ran while one was open for 2% -> 2% of each run, Pallas kernels for 10% -> 9%
where the time goes in v8:
time: 117 us; the launch traced here: 115 us
  starting transfers between devices  63.1 us (54%)
  waiting for transfers between devices  28.4 us (24%)
  Pallas kernels  19.1 us (16%)
  local copies, waits for them, and re-layouts  2.46 us (2%)
  other arithmetic  1.65 us (1%)
    all_to_all x1, starting transfers between devices, on_device(): patches = lax.all_to_all(pack(fields), 'mp', 0, 0, tiled=True)  19.5 us
    ppermute x4, waiting for transfers between devices, along(): return lax.ppermute(value, axes, pairs)  16.2 us
    ppermute x4, starting transfers between devices, along(): return lax.ppermute(value, axes, pairs)  14.9 us
    all_to_all x1, starting transfers between devices, on_device(): normed = lax.all_to_all(everyone, 'mp', 0, 0, tiled=True)  10.7 us
    all_to_all x1, waiting for transfers between devices, on_device(): pieces = lax.all_to_all(partial_sums, 'mp', 0, 0, tiled=True)  9.09 us
    all_to_all x1, starting transfers between devices, on_device(): pieces = lax.all_to_all(partial_sums, 'mp', 0, 0, tiled=True)  8.77 us
    pallas_call x1, Pallas kernels, advance(): pl.pallas_call(advance_kernel, in_specs=[pl.BlockSpec(memory_space=pltpu....  6.39 us
    ppermute x1, starting transfers between devices, on_device(): theirs = lax.ppermute(send, 'core', [(0, 1), (1, 0)])  4.88 us
  transfers between devices with their start and end apart: 9, of which 8 were waited for; matrix products, arithmetic and copies ran while one was open for 2% of the time, Pallas kernels for 9%

profile of v8, /device:TPU:15, one launch (start us, length us, event | category | flops | bytes accessed | tf_op | source)
XLA Modules:
  0.0 115.5 jit_solution(367666079452480503)
XLA Ops:
  0.6 3.0 %shard_map.77 = bf16[32,16,512]{2,1,0:T(8,128)(2,1)} custom-call(f32[16,8,8,256]{3,2,1,0:T(8,128)} %fields_ref.3), custom_call_target="tpu_custom_call" | custom-call | flops 1000000 | bytes 2097152 | tf_op jit(solution)/shard_map/pallas_call | solution.py:72
  3.7 19.5 %all-to-all-start = ((bf16[32,16,512]{2,1,0:T(8,128)(2,1)}), bf16[32,16,512]{2,1,0:T(8,128)(2,1)S(1)}, u32[]{:S(2)}, u32[]{:S(2)}) async-start(bf16[32,16,512]{2,1,0:T(8,128)(2,1)} %shard_map.77), calls=%async_computation | async-start | bytes 1048576 | tf_op jit(solution)/shard_map/all_to_all | solution.py:385
  23.2 2.4 %shard_map.78 = (bf16[2,128,256]{2,1,0:T(8,128)(2,1)}, bf16[2,128,256]{2,1,0:T(8,128)(2,1)}) custom-call(f32[16,8,8,256]{3,2,1,0:T(8,128)} %fields_ref.3), custom_call_target="tpu_custom_call" | custom-call | flops 100000 | bytes 2097152 | tf_op jit(solution)/shard_map/pallas_call | solution.py:98
  25.6 3.1 %collective-permute-start = (bf16[2,128,256]{2,1,0:T(8,128)(2,1)}, bf16[2,128,256]{2,1,0:T(8,128)(2,1)S(1)}, u32[]{:S(2)}, u32[]{:S(2)}) collective-permute-start(bf16[2,128,256]{2,1,0:T(8,128)(2,1)} %get-tuple-element.20), channel_id=1, source_target_pairs={{0,1},{1,2},{2,3},{3,4},{4,5},{5,6},{6,7},{7,8},{8,9},{9,10},{10,1... | collective-permute-start | bytes 393224 | tf_op jit(solution)/shard_map/ppermute | solution.py:371
  28.7 2.2 %collective-permute-start.1 = (bf16[2,128,256]{2,1,0:T(8,128)(2,1)}, bf16[2,128,256]{2,1,0:T(8,128)(2,1)S(1)}, u32[]{:S(2)}, u32[]{:S(2)}) collective-permute-start(bf16[2,128,256]{2,1,0:T(8,128)(2,1)} %get-tuple-element.21), channel_id=1, source_target_pairs={{1,0},{2,1},{3,2},{4,3},{5,4},{6,5},{7,6},{8,7},{9,8},{10,9},{11,1... | collective-permute-start | bytes 393224 | tf_op jit(solution)/shard_map/ppermute | solution.py:371
  30.9 1.8 %constant_dynamic-slice_fusion = bf16[1024,1024]{1,0:T(8,128)(2,1)S(1)} fusion(bf16[2048,1024]{1,0:T(8,128)(2,1)} %param.8, s32[]{:T(128)S(6)} %select_n.3), kind=kLoop, calls=%fused_computation.4 | loop fusion | bytes 4194308 | tf_op jit(solution)/shard_map/dynamic_slice | solution.py:392
  32.7 0.1 pad_add_fusion.who_ref
  32.8 0.6 add_convert_fusion.1.edge_ref
  33.3 1.4 %collective-permute-done.y_low_ref.yl_ref = bf16[2,128,256]{2,1,0:T(8,128)(2,1)S(1)} collective-permute-done((bf16[2,128,256]{2,1,0:T(8,128)(2,1)}, bf16[2,128,256]{2,1,0:T(8,128)(2,1)S(1)}, u32[]{:S(2)}, u32[]{:S(2)}) %collective-permute-start) | collective-permute-done | bytes 131104 | tf_op jit(solution)/shard_map/ppermute | solution.py:371
  34.7 3.8 %collective-permute-done.1.y_high_ref.yh_ref = bf16[2,128,256]{2,1,0:T(8,128)(2,1)S(1)} collective-permute-done((bf16[2,128,256]{2,1,0:T(8,128)(2,1)}, bf16[2,128,256]{2,1,0:T(8,128)(2,1)S(1)}, u32[]{:S(2)}, u32[]{:S(2)}) %collective-permute-start.1) | collective-permute-done | bytes 131104 | tf_op jit(solution)/shard_map/ppermute | solution.py:371
  38.5 0.5 all-to-all-done
  39.0 2.0 %shard_map.79 = (f32[32,4,1024]{2,1,0:T(4,128)S(1)}, bf16[32,4,1024]{2,1,0:T(4,128)(2,1)}) custom-call(s32[2]{0:T(128)S(1)} %pad_add_fusion.who_ref, bf16[16,2,16,512]{3,2,1,0:T(8,128)(2,1)S(1)} %bitcast.10, bf16[2,512,1024]{2,1,0:T(8,128)(2,1)S(1)} %bitcast.9), custom_call_target="tpu_custom_call" | custom-call | flops 540000000 | bytes 3145728 | tf_op jit(solution)/shard_map/pallas_call | solution.py:178
  41.0 4.9 %collective-permute-start.2 = (bf16[32,4,1024]{2,1,0:T(4,128)(2,1)}, bf16[32,4,1024]{2,1,0:T(4,128)(2,1)S(1)}, u32[]{:S(2)}, u32[]{:S(2)}) collective-permute-start(bf16[32,4,1024]{2,1,0:T(4,128)(2,1)} %get-tuple-element.26), channel_id=1, source_target_pairs={{0,32},{32,0},{1,33},{33,1},{2,34},{34,2},{3,35},{35,3},{4,36},{36... | collective-permute-start | bytes 786440 | tf_op jit(solution)/shard_map/ppermute | solution.py:399
  45.9 1.4 %collective-permute-done.2 = bf16[32,4,1024]{2,1,0:T(4,128)(2,1)S(1)} collective-permute-done((bf16[32,4,1024]{2,1,0:T(4,128)(2,1)}, bf16[32,4,1024]{2,1,0:T(4,128)(2,1)S(1)}, u32[]{:S(2)}, u32[]{:S(2)}) %collective-permute-start.2) | collective-permute-done | bytes 262176 | tf_op jit(solution)/shard_map/ppermute | solution.py:399
  47.3 0.9 add_convert_fusion
  48.1 8.8 %all-to-all-start.1 = ((bf16[32,4,1024]{2,1,0:T(4,128)(2,1)}), bf16[32,4,1024]{2,1,0:T(4,128)(2,1)S(1)}, u32[]{:S(2)}, u32[]{:S(2)}) async-start(bf16[32,4,1024]{2,1,0:T(4,128)(2,1)} %add_convert_fusion), calls=%async_computation.1 | async-start | bytes 524288 | tf_op jit(solution)/shard_map/all_to_all | solution.py:401
  56.9 0.0 copy-start
  56.9 2.0 %shard_map.80 = (bf16[288,256]{1,0:T(8,128)(2,1)}, bf16[288,256]{1,0:T(8,128)(2,1)}) custom-call(f32[16,8,8,256]{3,2,1,0:T(8,128)} %fields_ref.3, f32[16,8,8,256]{3,2,1,0:T(8,128)} %fields_ref.3, bf16[2,128,256]{2,1,0:T(8,128)(2,1)} %copy-done.3, bf16[2,128,256]{2,1,0:T(8,128)(2,1)} %copy-done.4), custom_call_target="tpu_custom_call" | custom-call | flops 100000 | bytes 1048576 | tf_op jit(solution)/shard_map/pallas_call | solution.py:119
  59.0 9.1 %all-to-all-done.1 = bf16[32,4,1024]{2,1,0:T(4,128)(2,1)S(1)} async-done(((bf16[32,4,1024]{2,1,0:T(4,128)(2,1)}), bf16[32,4,1024]{2,1,0:T(4,128)(2,1)S(1)}, u32[]{:S(2)}, u32[]{:S(2)}) %all-to-all-start.1) | async-done | bytes 262176 | tf_op jit(solution)/shard_map/all_to_all | solution.py:401
  68.0 0.1 convert_reduce_fusion
  68.2 4.4 %collective-permute-start.3 = (f32[4,1024]{1,0:T(4,128)S(1)}, f32[4,1024]{1,0:T(4,128)S(1)}, u32[]{:S(2)}, u32[]{:S(2)}) collective-permute-start(f32[4,1024]{1,0:T(4,128)S(1)} %convert_reduce_fusion), channel_id=1, source_target_pairs={{1,1},{2,34},{0,67},{3,96},{5,133},{6,166},{4,199},{7,228},{9,265}... | collective-permute-start | bytes 49160 | tf_op jit(solution)/shard_map/ppermute | solution.py:407
  72.6 1.3 %collective-permute-done.3.rows_ref = f32[4,1024]{1,0:T(4,128)S(1)} collective-permute-done((f32[4,1024]{1,0:T(4,128)S(1)}, f32[4,1024]{1,0:T(4,128)S(1)}, u32[]{:S(2)}, u32[]{:S(2)}) %collective-permute-start.3) | collective-permute-done | bytes 16416 | tf_op jit(solution)/shard_map/ppermute | solution.py:407
  73.9 1.4 %shard_map.81 = bf16[32,4,1024]{2,1,0:T(4,128)(2,1)} custom-call(s32[2]{0:T(128)S(1)} %pad_add_fusion.who_ref, f32[4,1024]{1,0:T(4,128)S(1)} %collective-permute-done.3.rows_ref, bf16[128,1024]{1,0:T(8,128)(2,1)S(1)} %copy-done.1, f32[1,1024]{1,0:T(1,128)S(1)} %bitcast.11), custom_call_target="tpu_custom_call" | custom-call | flops 100000 | bytes 300000 | tf_op jit(solution)/shard_map/pallas_call | solution.py:206
  75.2 10.7 %all-to-all-start.2 = ((bf16[32,4,1024]{2,1,0:T(4,128)(2,1)}), bf16[32,4,1024]{2,1,0:T(4,128)(2,1)S(1)}, u32[]{:S(2)}, u32[]{:S(2)}) async-start(bf16[32,4,1024]{2,1,0:T(4,128)(2,1)} %shard_map.81), calls=%async_computation.2 | async-start | bytes 524288 | tf_op jit(solution)/shard_map/all_to_all | solution.py:409
  85.9 7.7 %collective-permute-start.4 = (bf16[288,256]{1,0:T(8,128)(2,1)}, bf16[288,256]{1,0:T(8,128)(2,1)S(1)}, u32[]{:S(2)}, u32[]{:S(2)}) collective-permute-start(bf16[288,256]{1,0:T(8,128)(2,1)} %get-tuple-element.34), channel_id=1, source_target_pairs={{0,32},{32,64},{64,96},{96,128},{128,160},{160,192},{192,224},{224... | collective-permute-start | bytes 442376 | tf_op jit(solution)/shard_map/ppermute | solution.py:371
  93.6 1.9 %collective-permute-start.5 = (bf16[288,256]{1,0:T(8,128)(2,1)}, bf16[288,256]{1,0:T(8,128)(2,1)S(1)}, u32[]{:S(2)}, u32[]{:S(2)}) collective-permute-start(bf16[288,256]{1,0:T(8,128)(2,1)} %get-tuple-element.35), channel_id=1, source_target_pairs={{32,0},{64,32},{96,64},{128,96},{160,128},{192,160},{224,192},{256... | collective-permute-start | bytes 442376 | tf_op jit(solution)/shard_map/ppermute | solution.py:371
  95.5 1.3 %collective-permute-done.4.xl_ref = bf16[288,256]{1,0:T(8,128)(2,1)S(1)} collective-permute-done((bf16[288,256]{1,0:T(8,128)(2,1)}, bf16[288,256]{1,0:T(8,128)(2,1)S(1)}, u32[]{:S(2)}, u32[]{:S(2)}) %collective-permute-start.4) | collective-permute-done | bytes 147488 | tf_op jit(solution)/shard_map/ppermute | solution.py:371
  96.9 9.6 %collective-permute-done.5.xh_ref = bf16[288,256]{1,0:T(8,128)(2,1)S(1)} collective-permute-done((bf16[288,256]{1,0:T(8,128)(2,1)}, bf16[288,256]{1,0:T(8,128)(2,1)S(1)}, u32[]{:S(2)}, u32[]{:S(2)}) %collective-permute-start.5) | collective-permute-done | bytes 147488 | tf_op jit(solution)/shard_map/ppermute | solution.py:371
  106.5 0.7 copy-done.6
  107.2 6.4 %shard_map.82 = f32[16,8,8,256]{3,2,1,0:T(8,128)} custom-call(f32[4]{0:T(128)} %add_convert_fusion.1.edge_ref, f32[16,8,8,256]{3,2,1,0:T(8,128)} %fields_ref.3, bf16[13,8,8,256]{3,2,1,0:T(8,128)(2,1)} %source_ref.1, bf16[2,128,256]{2,1,0:T(8,128)(2,1)} %copy-done.3, bf16[2,128,256]{2,1,0:T(8,128)(2,1)} %copy-done.4, bf16[288,256]{1,0:T(8,128)(2,1)} %copy-done.5, ...), custom_call_target="tpu_custom_call" | custom-call | flops 100000000 | bytes 4194304 | tf_op jit(solution)/shard_map/pallas_call | solution.py:354
  113.6 0.0 all-to-all-done.2.normed_ref
  113.6 1.9 %shard_map.83 = bf16[128,1408]{1,0:T(8,128)(2,1)} custom-call(s32[2]{0:T(128)S(1)} %pad_add_fusion.who_ref, bf16[32,4,1024]{2,1,0:T(4,128)(2,1)S(1)} %all-to-all-done.2.normed_ref, bf16[1024,1408]{1,0:T(8,128)(2,1)S(1)} %copy-done), custom_call_target="tpu_custom_call" | custom-call | flops 370000000 | bytes 4194304 | tf_op jit(solution)/shard_map/pallas_call | solution.py:247
  (12 shorter events, 0.0 us)
Async XLA Ops:
  3.7 35.3 %all-to-all-start = ((bf16[32,16,512]{2,1,0:T(8,128)(2,1)}), bf16[32,16,512]{2,1,0:T(8,128)(2,1)S(1)}, u32[]{:S(2)}, u32[]{:S(2)}) async-start(bf16[32,16,512]{2,1,0:T(8,128)(2,1)} %shard_map.77), calls=%async_computation | async-start | bytes 1048576 | tf_op jit(solution)/shard_map/all_to_all | solution.py:385
  25.6 9.1 %collective-permute-start = (bf16[2,128,256]{2,1,0:T(8,128)(2,1)}, bf16[2,128,256]{2,1,0:T(8,128)(2,1)S(1)}, u32[]{:S(2)}, u32[]{:S(2)}) collective-permute-start(bf16[2,128,256]{2,1,0:T(8,128)(2,1)} %get-tuple-element.20), channel_id=1, source_target_pairs={{0,1},{1,2},{2,3},{3,4},{4,5},{5,6},{6,7},{7,8},{8,9},{9,10},{10,1... | collective-permute-start | bytes 393224 | tf_op jit(solution)/shard_map/ppermute | solution.py:371
  28.7 9.8 %collective-permute-start.1 = (bf16[2,128,256]{2,1,0:T(8,128)(2,1)}, bf16[2,128,256]{2,1,0:T(8,128)(2,1)S(1)}, u32[]{:S(2)}, u32[]{:S(2)}) collective-permute-start(bf16[2,128,256]{2,1,0:T(8,128)(2,1)} %get-tuple-element.21), channel_id=1, source_target_pairs={{1,0},{2,1},{3,2},{4,3},{5,4},{6,5},{7,6},{8,7},{9,8},{10,9},{11,1... | collective-permute-start | bytes 393224 | tf_op jit(solution)/shard_map/ppermute | solution.py:371
  34.7 22.2 %copy-start.3 = (bf16[2,128,256]{2,1,0:T(8,128)(2,1)}, bf16[2,128,256]{2,1,0:T(8,128)(2,1)S(1)}, u32[]{:S(2)}) copy-start(bf16[2,128,256]{2,1,0:T(8,128)(2,1)S(1)} %collective-permute-done.y_low_ref.yl_ref) | copy-start | bytes 393220
  38.5 9.6 %copy-start.4 = (bf16[2,128,256]{2,1,0:T(8,128)(2,1)}, bf16[2,128,256]{2,1,0:T(8,128)(2,1)S(1)}, u32[]{:S(2)}) copy-start(bf16[2,128,256]{2,1,0:T(8,128)(2,1)S(1)} %collective-permute-done.1.y_high_ref.yh_ref) | copy-start | bytes 393220
  39.0 34.8 %copy-start.1 = (bf16[128,1024]{1,0:T(8,128)(2,1)S(1)}, bf16[128,1024]{1,0:T(8,128)(2,1)}, u32[]{:S(2)}) copy-start(bf16[128,1024]{1,0:T(8,128)(2,1)} %position_ref.1) | copy-start | bytes 786436
  39.0 34.8 %copy-start.2 = (f32[1024]{0:T(1024)S(1)}, f32[1024]{0:T(1024)}, u32[]{:S(2)}) copy-start(f32[1024]{0:T(1024)} %param.10) | copy-start | bytes 12292
  41.0 6.2 %collective-permute-start.2 = (bf16[32,4,1024]{2,1,0:T(4,128)(2,1)}, bf16[32,4,1024]{2,1,0:T(4,128)(2,1)S(1)}, u32[]{:S(2)}, u32[]{:S(2)}) collective-permute-start(bf16[32,4,1024]{2,1,0:T(4,128)(2,1)} %get-tuple-element.26), channel_id=1, source_target_pairs={{0,32},{32,0},{1,33},{33,1},{2,34},{34,2},{3,35},{35,3},{4,36},{36... | collective-permute-start | bytes 786440 | tf_op jit(solution)/shard_map/ppermute | solution.py:399
  48.1 19.9 %all-to-all-start.1 = ((bf16[32,4,1024]{2,1,0:T(4,128)(2,1)}), bf16[32,4,1024]{2,1,0:T(4,128)(2,1)S(1)}, u32[]{:S(2)}, u32[]{:S(2)}) async-start(bf16[32,4,1024]{2,1,0:T(4,128)(2,1)} %add_convert_fusion), calls=%async_computation.1 | async-start | bytes 524288 | tf_op jit(solution)/shard_map/all_to_all | solution.py:401
  56.9 56.7 %copy-start = (bf16[1024,1408]{1,0:T(8,128)(2,1)S(1)}, bf16[1024,1408]{1,0:T(8,128)(2,1)}, u32[]{:S(2)}) copy-start(bf16[1024,1408]{1,0:T(8,128)(2,1)} %weight_ref.1) | copy-start | bytes 8650756
  68.2 5.7 %collective-permute-start.3 = (f32[4,1024]{1,0:T(4,128)S(1)}, f32[4,1024]{1,0:T(4,128)S(1)}, u32[]{:S(2)}, u32[]{:S(2)}) collective-permute-start(f32[4,1024]{1,0:T(4,128)S(1)} %convert_reduce_fusion), channel_id=1, source_target_pairs={{1,1},{2,34},{0,67},{3,96},{5,133},{6,166},{4,199},{7,228},{9,265}... | collective-permute-start | bytes 49160 | tf_op jit(solution)/shard_map/ppermute | solution.py:407
  75.2 38.3 %all-to-all-start.2 = ((bf16[32,4,1024]{2,1,0:T(4,128)(2,1)}), bf16[32,4,1024]{2,1,0:T(4,128)(2,1)S(1)}, u32[]{:S(2)}, u32[]{:S(2)}) async-start(bf16[32,4,1024]{2,1,0:T(4,128)(2,1)} %shard_map.81), calls=%async_computation.2 | async-start | bytes 524288 | tf_op jit(solution)/shard_map/all_to_all | solution.py:409
  85.9 10.9 %collective-permute-start.4 = (bf16[288,256]{1,0:T(8,128)(2,1)}, bf16[288,256]{1,0:T(8,128)(2,1)S(1)}, u32[]{:S(2)}, u32[]{:S(2)}) collective-permute-start(bf16[288,256]{1,0:T(8,128)(2,1)} %get-tuple-element.34), channel_id=1, source_target_pairs={{0,32},{32,64},{64,96},{96,128},{128,160},{160,192},{192,224},{224... | collective-permute-start | bytes 442376 | tf_op jit(solution)/shard_map/ppermute | solution.py:371
  93.6 12.9 %collective-permute-start.5 = (bf16[288,256]{1,0:T(8,128)(2,1)}, bf16[288,256]{1,0:T(8,128)(2,1)S(1)}, u32[]{:S(2)}, u32[]{:S(2)}) collective-permute-start(bf16[288,256]{1,0:T(8,128)(2,1)} %get-tuple-element.35), channel_id=1, source_target_pairs={{32,0},{64,32},{96,64},{128,96},{160,128},{192,160},{224,192},{256... | collective-permute-start | bytes 442376 | tf_op jit(solution)/shard_map/ppermute | solution.py:371
  96.9 9.6 %copy-start.5 = (bf16[288,256]{1,0:T(8,128)(2,1)}, bf16[288,256]{1,0:T(8,128)(2,1)S(1)}, u32[]{:S(2)}) copy-start(bf16[288,256]{1,0:T(8,128)(2,1)S(1)} %collective-permute-done.4.xl_ref) | copy-start | bytes 442372
  106.5 0.7 copy-start.6

commit v9 on v7

--- a/solution.py
+++ b/solution.py
@@ -390,8 +390,9 @@
     who = jnp.stack([seq, mp]).astype(jnp.int32)
     edges = jnp.stack([seq > 0, seq < 31, mp > 0, mp < 31]).astype(F32)
     weight = lax.dynamic_slice_in_dim(embed_weight, core * 1024, 1024, 0).reshape(2, 512, 1024)
-    patches, who, edges, weight, y_low, y_high = lax.optimization_barrier(
-        (patches, who, edges, weight, y_low, y_high)
+    x_first, x_last = x_edges(fields, y_low, y_high)
+    patches, who, edges, weight, x_first, x_last = lax.optimization_barrier(
+        (patches, who, edges, weight, x_first, x_last)
     )
 
     patches = patches.reshape(16, 2, 16, 512)
@@ -400,13 +401,12 @@
     partial_sums = (keep + theirs.astype(F32)).astype(BF16)
     pieces = lax.all_to_all(partial_sums, "mp", 0, 0, tiled=True)
 
-    x_first, x_last = x_edges(fields, y_low, y_high)
     x_low = along(x_last, x_axes, 1)
     x_high = along(x_first, x_axes, -1)
-    pieces, x_low, x_high = lax.optimization_barrier((pieces, x_low, x_high))
 
     rows = jnp.sum(pieces.astype(F32), 0)
     rows = lax.ppermute(rows, ALL, SWAP)
+    rows, x_low, x_high = lax.optimization_barrier((rows, x_low, x_high))
     everyone = norm(who, rows, position, norm_gain)
     normed = lax.all_to_all(everyone, "mp", 0, 0, tiled=True)
 

time: 114 us -> 109 us (0.956)
  the two profiles are of different devices: /device:TPU:15 before, /device:TPU:64 now
where the time goes in v9:
time: 109 us
  starting transfers between devices  66 us (61%)
  Pallas kernels  19 us (17%)
  waiting for transfers between devices  19 us (17%)
  local copies, waits for them, and re-layouts  2.44 us (2%)
  other arithmetic  1.7 us (2%)
    all_to_all x1, starting transfers between devices, on_device(): patches = lax.all_to_all(pack(fields), 'mp', 0, 0, tiled=True)  19.9 us
    ppermute x4, starting transfers between devices, along(): return lax.ppermute(value, axes, pairs)  16.6 us
    all_to_all x1, starting transfers between devices, on_device(): normed = lax.all_to_all(everyone, 'mp', 0, 0, tiled=True)  14.1 us
    all_to_all x1, starting transfers between devices, on_device(): pieces = lax.all_to_all(partial_sums, 'mp', 0, 0, tiled=True)  10 us
    ppermute x4, waiting for transfers between devices, along(): return lax.ppermute(value, axes, pairs)  7.43 us
    pallas_call x1, Pallas kernels, advance(): pl.pallas_call(advance_kernel, in_specs=[pl.BlockSpec(memory_space=pltpu....  6.4 us
    all_to_all x1, waiting for transfers between devices, on_device(): normed = lax.all_to_all(everyone, 'mp', 0, 0, tiled=True)  5.54 us
    ppermute x1, starting transfers between devices, on_device(): rows = lax.ppermute(rows, ALL, SWAP)  3.49 us
  transfers between devices with their start and end apart: 9, of which 7 were waited for; matrix products, arithmetic and copies ran while one was open for 2% of the time, Pallas kernels for 10%

profile of v9, /device:TPU:64, one launch (start us, length us, event | category | flops | bytes accessed | tf_op | source)
XLA Modules:
  0.0 108.9 jit_solution(1400720814972443255)
XLA Ops:
  0.6 3.0 %shard_map.77 = bf16[32,16,512]{2,1,0:T(8,128)(2,1)} custom-call(f32[16,8,8,256]{3,2,1,0:T(8,128)} %fields_ref.3), custom_call_target="tpu_custom_call" | custom-call | flops 1000000 | bytes 2097152 | tf_op jit(solution)/shard_map/pallas_call | solution.py:72
  3.7 19.9 %all-to-all-start = ((bf16[32,16,512]{2,1,0:T(8,128)(2,1)}), bf16[32,16,512]{2,1,0:T(8,128)(2,1)S(1)}, u32[]{:S(2)}, u32[]{:S(2)}) async-start(bf16[32,16,512]{2,1,0:T(8,128)(2,1)} %shard_map.77), calls=%async_computation | async-start | bytes 1048576 | tf_op jit(solution)/shard_map/all_to_all | solution.py:385
  23.5 2.4 %shard_map.78 = (bf16[2,128,256]{2,1,0:T(8,128)(2,1)}, bf16[2,128,256]{2,1,0:T(8,128)(2,1)}) custom-call(f32[16,8,8,256]{3,2,1,0:T(8,128)} %fields_ref.3), custom_call_target="tpu_custom_call" | custom-call | flops 100000 | bytes 2097152 | tf_op jit(solution)/shard_map/pallas_call | solution.py:98
  25.9 3.7 %collective-permute-start = (bf16[2,128,256]{2,1,0:T(8,128)(2,1)}, bf16[2,128,256]{2,1,0:T(8,128)(2,1)S(1)}, u32[]{:S(2)}, u32[]{:S(2)}) collective-permute-start(bf16[2,128,256]{2,1,0:T(8,128)(2,1)} %get-tuple-element.20), channel_id=1, source_target_pairs={{0,1},{1,2},{2,3},{3,4},{4,5},{5,6},{6,7},{7,8},{8,9},{9,10},{10,1... | collective-permute-start | bytes 393224 | tf_op jit(solution)/shard_map/ppermute | solution.py:371
  29.6 1.3 %collective-permute-start.1 = (bf16[2,128,256]{2,1,0:T(8,128)(2,1)}, bf16[2,128,256]{2,1,0:T(8,128)(2,1)S(1)}, u32[]{:S(2)}, u32[]{:S(2)}) collective-permute-start(bf16[2,128,256]{2,1,0:T(8,128)(2,1)} %get-tuple-element.21), channel_id=1, source_target_pairs={{1,0},{2,1},{3,2},{4,3},{5,4},{6,5},{7,6},{8,7},{9,8},{10,9},{11,1... | collective-permute-start | bytes 393224 | tf_op jit(solution)/shard_map/ppermute | solution.py:371
  30.9 1.8 %constant_dynamic-slice_fusion = bf16[1024,1024]{1,0:T(8,128)(2,1)S(1)} fusion(bf16[2048,1024]{1,0:T(8,128)(2,1)} %param.8, s32[]{:T(128)S(6)} %select_n.3), kind=kLoop, calls=%fused_computation.4 | loop fusion | bytes 4194308 | tf_op jit(solution)/shard_map/dynamic_slice | solution.py:392
  32.7 0.1 pad_add_fusion.who_ref
  32.8 0.7 add_convert_fusion.1.edge_ref
  33.4 1.3 %collective-permute-done.y_low_ref.yl_ref = bf16[2,128,256]{2,1,0:T(8,128)(2,1)S(1)} collective-permute-done((bf16[2,128,256]{2,1,0:T(8,128)(2,1)}, bf16[2,128,256]{2,1,0:T(8,128)(2,1)S(1)}, u32[]{:S(2)}, u32[]{:S(2)}) %collective-permute-start) | collective-permute-done | bytes 131104 | tf_op jit(solution)/shard_map/ppermute | solution.py:371
  34.8 6.1 %collective-permute-done.1.y_high_ref.yh_ref = bf16[2,128,256]{2,1,0:T(8,128)(2,1)S(1)} collective-permute-done((bf16[2,128,256]{2,1,0:T(8,128)(2,1)}, bf16[2,128,256]{2,1,0:T(8,128)(2,1)S(1)}, u32[]{:S(2)}, u32[]{:S(2)}) %collective-permute-start.1) | collective-permute-done | bytes 131104 | tf_op jit(solution)/shard_map/ppermute | solution.py:371
  40.9 0.0 copy-done.3
  40.9 0.7 copy-done.4
  41.5 1.9 %shard_map.79 = (bf16[288,256]{1,0:T(8,128)(2,1)}, bf16[288,256]{1,0:T(8,128)(2,1)}) custom-call(f32[16,8,8,256]{3,2,1,0:T(8,128)} %fields_ref.3, f32[16,8,8,256]{3,2,1,0:T(8,128)} %fields_ref.3, bf16[2,128,256]{2,1,0:T(8,128)(2,1)} %copy-done.3, bf16[2,128,256]{2,1,0:T(8,128)(2,1)} %copy-done.4), custom_call_target="tpu_custom_call" | custom-call | flops 100000 | bytes 1048576 | tf_op jit(solution)/shard_map/pallas_call | solution.py:119
  43.4 0.2 all-to-all-done
  43.6 2.0 %shard_map.80 = (f32[32,4,1024]{2,1,0:T(4,128)S(1)}, bf16[32,4,1024]{2,1,0:T(4,128)(2,1)}) custom-call(s32[2]{0:T(128)S(1)} %pad_add_fusion.who_ref, bf16[16,2,16,512]{3,2,1,0:T(8,128)(2,1)S(1)} %bitcast.10, bf16[2,512,1024]{2,1,0:T(8,128)(2,1)S(1)} %bitcast.9), custom_call_target="tpu_custom_call" | custom-call | flops 540000000 | bytes 3145728 | tf_op jit(solution)/shard_map/pallas_call | solution.py:178
  45.6 1.9 %collective-permute-start.2 = (bf16[32,4,1024]{2,1,0:T(4,128)(2,1)}, bf16[32,4,1024]{2,1,0:T(4,128)(2,1)S(1)}, u32[]{:S(2)}, u32[]{:S(2)}) collective-permute-start(bf16[32,4,1024]{2,1,0:T(4,128)(2,1)} %get-tuple-element.28), channel_id=1, source_target_pairs={{0,32},{32,0},{1,33},{33,1},{2,34},{34,2},{3,35},{35,3},{4,36},{36... | collective-permute-start | bytes 786440 | tf_op jit(solution)/shard_map/ppermute | solution.py:400
  47.6 1.7 %collective-permute-done.2 = bf16[32,4,1024]{2,1,0:T(4,128)(2,1)S(1)} collective-permute-done((bf16[32,4,1024]{2,1,0:T(4,128)(2,1)}, bf16[32,4,1024]{2,1,0:T(4,128)(2,1)S(1)}, u32[]{:S(2)}, u32[]{:S(2)}) %collective-permute-start.2) | collective-permute-done | bytes 262176 | tf_op jit(solution)/shard_map/ppermute | solution.py:400
  49.3 0.9 add_convert_fusion
  50.1 10.0 %all-to-all-start.1 = ((bf16[32,4,1024]{2,1,0:T(4,128)(2,1)}), bf16[32,4,1024]{2,1,0:T(4,128)(2,1)S(1)}, u32[]{:S(2)}, u32[]{:S(2)}) async-start(bf16[32,4,1024]{2,1,0:T(4,128)(2,1)} %add_convert_fusion), calls=%async_computation.1 | async-start | bytes 524288 | tf_op jit(solution)/shard_map/all_to_all | solution.py:402
  60.2 1.9 %collective-permute-start.4 = (bf16[288,256]{1,0:T(8,128)(2,1)}, bf16[288,256]{1,0:T(8,128)(2,1)}, u32[]{:S(2)}, u32[]{:S(2)}) collective-permute-start(bf16[288,256]{1,0:T(8,128)(2,1)} %get-tuple-element.29), channel_id=1, source_target_pairs={{0,32},{32,64},{64,96},{96,128},{128,160},{160,192},{192,224},{224... | collective-permute-start | bytes 442376 | tf_op jit(solution)/shard_map/ppermute | solution.py:371
  62.1 9.7 %collective-permute-start.5 = (bf16[288,256]{1,0:T(8,128)(2,1)}, bf16[288,256]{1,0:T(8,128)(2,1)}, u32[]{:S(2)}, u32[]{:S(2)}) collective-permute-start(bf16[288,256]{1,0:T(8,128)(2,1)} %get-tuple-element.30), channel_id=1, source_target_pairs={{32,0},{64,32},{96,64},{128,96},{160,128},{192,160},{224,192},{256... | collective-permute-start | bytes 442376 | tf_op jit(solution)/shard_map/ppermute | solution.py:371
  71.8 1.4 %all-to-all-done.1 = bf16[32,4,1024]{2,1,0:T(4,128)(2,1)S(1)} async-done(((bf16[32,4,1024]{2,1,0:T(4,128)(2,1)}), bf16[32,4,1024]{2,1,0:T(4,128)(2,1)S(1)}, u32[]{:S(2)}, u32[]{:S(2)}) %all-to-all-start.1) | async-done | bytes 262176 | tf_op jit(solution)/shard_map/all_to_all | solution.py:402
  73.1 0.1 convert_reduce_fusion
  73.3 3.5 %collective-permute-start.3 = (f32[4,1024]{1,0:T(4,128)S(1)}, f32[4,1024]{1,0:T(4,128)S(1)}, u32[]{:S(2)}, u32[]{:S(2)}) collective-permute-start(f32[4,1024]{1,0:T(4,128)S(1)} %convert_reduce_fusion), channel_id=1, source_target_pairs={{1,1},{2,34},{0,67},{3,96},{5,133},{6,166},{4,199},{7,228},{9,265}... | collective-permute-start | bytes 49160 | tf_op jit(solution)/shard_map/ppermute | solution.py:408
  76.8 0.0 collective-permute-done.4.xl_ref
  76.8 0.0 collective-permute-done.5.xh_ref
  76.8 2.7 %collective-permute-done.3.rows_ref = f32[4,1024]{1,0:T(4,128)S(1)} collective-permute-done((f32[4,1024]{1,0:T(4,128)S(1)}, f32[4,1024]{1,0:T(4,128)S(1)}, u32[]{:S(2)}, u32[]{:S(2)}) %collective-permute-start.3) | collective-permute-done | bytes 16416 | tf_op jit(solution)/shard_map/ppermute | solution.py:408
  79.5 1.4 %shard_map.81 = bf16[32,4,1024]{2,1,0:T(4,128)(2,1)} custom-call(s32[2]{0:T(128)S(1)} %pad_add_fusion.who_ref, f32[4,1024]{1,0:T(4,128)S(1)} %collective-permute-done.3.rows_ref, bf16[128,1024]{1,0:T(8,128)(2,1)S(1)} %copy-done.1, f32[1,1024]{1,0:T(1,128)S(1)} %bitcast.11), custom_call_target="tpu_custom_call" | custom-call | flops 100000 | bytes 300000 | tf_op jit(solution)/shard_map/pallas_call | solution.py:206
  80.9 14.1 %all-to-all-start.2 = ((bf16[32,4,1024]{2,1,0:T(4,128)(2,1)}), bf16[32,4,1024]{2,1,0:T(4,128)(2,1)S(1)}, u32[]{:S(2)}, u32[]{:S(2)}) async-start(bf16[32,4,1024]{2,1,0:T(4,128)(2,1)} %shard_map.81), calls=%async_computation.2 | async-start | bytes 524288 | tf_op jit(solution)/shard_map/all_to_all | solution.py:411
  95.0 6.4 %shard_map.82 = f32[16,8,8,256]{3,2,1,0:T(8,128)} custom-call(f32[4]{0:T(128)} %add_convert_fusion.1.edge_ref, f32[16,8,8,256]{3,2,1,0:T(8,128)} %fields_ref.3, bf16[13,8,8,256]{3,2,1,0:T(8,128)(2,1)} %source_ref.1, bf16[2,128,256]{2,1,0:T(8,128)(2,1)} %copy-done.3, bf16[2,128,256]{2,1,0:T(8,128)(2,1)} %copy-done.4, ...), custom_call_target="tpu_custom_call" | custom-call | flops 100000000 | bytes 4194304 | tf_op jit(solution)/shard_map/pallas_call | solution.py:354
  101.4 5.5 %all-to-all-done.2.normed_ref = bf16[32,4,1024]{2,1,0:T(4,128)(2,1)S(1)} async-done(((bf16[32,4,1024]{2,1,0:T(4,128)(2,1)}), bf16[32,4,1024]{2,1,0:T(4,128)(2,1)S(1)}, u32[]{:S(2)}, u32[]{:S(2)}) %all-to-all-start.2) | async-done | bytes 262176 | tf_op jit(solution)/shard_map/all_to_all | solution.py:411
  107.0 1.9 %shard_map.83 = bf16[128,1408]{1,0:T(8,128)(2,1)} custom-call(s32[2]{0:T(128)S(1)} %pad_add_fusion.who_ref, bf16[32,4,1024]{2,1,0:T(4,128)(2,1)S(1)} %all-to-all-done.2.normed_ref, bf16[1024,1408]{1,0:T(8,128)(2,1)S(1)} %copy-done), custom_call_target="tpu_custom_call" | custom-call | flops 370000000 | bytes 4194304 | tf_op jit(solution)/shard_map/pallas_call | solution.py:247
  (8 shorter events, 0.0 us)
Async XLA Ops:
  3.7 40.0 %all-to-all-start = ((bf16[32,16,512]{2,1,0:T(8,128)(2,1)}), bf16[32,16,512]{2,1,0:T(8,128)(2,1)S(1)}, u32[]{:S(2)}, u32[]{:S(2)}) async-start(bf16[32,16,512]{2,1,0:T(8,128)(2,1)} %shard_map.77), calls=%async_computation | async-start | bytes 1048576 | tf_op jit(solution)/shard_map/all_to_all | solution.py:385
  25.9 8.9 %collective-permute-start = (bf16[2,128,256]{2,1,0:T(8,128)(2,1)}, bf16[2,128,256]{2,1,0:T(8,128)(2,1)S(1)}, u32[]{:S(2)}, u32[]{:S(2)}) collective-permute-start(bf16[2,128,256]{2,1,0:T(8,128)(2,1)} %get-tuple-element.20), channel_id=1, source_target_pairs={{0,1},{1,2},{2,3},{3,4},{4,5},{5,6},{6,7},{7,8},{8,9},{9,10},{10,1... | collective-permute-start | bytes 393224 | tf_op jit(solution)/shard_map/ppermute | solution.py:371
  29.6 11.2 %collective-permute-start.1 = (bf16[2,128,256]{2,1,0:T(8,128)(2,1)}, bf16[2,128,256]{2,1,0:T(8,128)(2,1)S(1)}, u32[]{:S(2)}, u32[]{:S(2)}) collective-permute-start(bf16[2,128,256]{2,1,0:T(8,128)(2,1)} %get-tuple-element.21), channel_id=1, source_target_pairs={{1,0},{2,1},{3,2},{4,3},{5,4},{6,5},{7,6},{8,7},{9,8},{10,9},{11,1... | collective-permute-start | bytes 393224 | tf_op jit(solution)/shard_map/ppermute | solution.py:371
  33.4 46.1 %copy-start.1 = (bf16[128,1024]{1,0:T(8,128)(2,1)S(1)}, bf16[128,1024]{1,0:T(8,128)(2,1)}, u32[]{:S(2)}) copy-start(bf16[128,1024]{1,0:T(8,128)(2,1)} %position_ref.1) | copy-start | bytes 786436
  33.4 46.1 %copy-start.2 = (f32[1024]{0:T(1024)S(1)}, f32[1024]{0:T(1024)}, u32[]{:S(2)}) copy-start(f32[1024]{0:T(1024)} %param.10) | copy-start | bytes 12292
  34.8 6.1 %copy-start.3 = (bf16[2,128,256]{2,1,0:T(8,128)(2,1)}, bf16[2,128,256]{2,1,0:T(8,128)(2,1)S(1)}, u32[]{:S(2)}) copy-start(bf16[2,128,256]{2,1,0:T(8,128)(2,1)S(1)} %collective-permute-done.y_low_ref.yl_ref) | copy-start | bytes 393220
  40.9 0.7 copy-start.4
  45.6 3.6 %collective-permute-start.2 = (bf16[32,4,1024]{2,1,0:T(4,128)(2,1)}, bf16[32,4,1024]{2,1,0:T(4,128)(2,1)S(1)}, u32[]{:S(2)}, u32[]{:S(2)}) collective-permute-start(bf16[32,4,1024]{2,1,0:T(4,128)(2,1)} %get-tuple-element.28), channel_id=1, source_target_pairs={{0,32},{32,0},{1,33},{33,1},{2,34},{34,2},{3,35},{35,3},{4,36},{36... | collective-permute-start | bytes 786440 | tf_op jit(solution)/shard_map/ppermute | solution.py:400
  49.3 57.7 %copy-start = (bf16[1024,1408]{1,0:T(8,128)(2,1)S(1)}, bf16[1024,1408]{1,0:T(8,128)(2,1)}, u32[]{:S(2)}) copy-start(bf16[1024,1408]{1,0:T(8,128)(2,1)} %weight_ref.1) | copy-start | bytes 8650756
  50.1 23.0 %all-to-all-start.1 = ((bf16[32,4,1024]{2,1,0:T(4,128)(2,1)}), bf16[32,4,1024]{2,1,0:T(4,128)(2,1)S(1)}, u32[]{:S(2)}, u32[]{:S(2)}) async-start(bf16[32,4,1024]{2,1,0:T(4,128)(2,1)} %add_convert_fusion), calls=%async_computation.1 | async-start | bytes 524288 | tf_op jit(solution)/shard_map/all_to_all | solution.py:402
  60.2 16.6 %collective-permute-start.4 = (bf16[288,256]{1,0:T(8,128)(2,1)}, bf16[288,256]{1,0:T(8,128)(2,1)}, u32[]{:S(2)}, u32[]{:S(2)}) collective-permute-start(bf16[288,256]{1,0:T(8,128)(2,1)} %get-tuple-element.29), channel_id=1, source_target_pairs={{0,32},{32,64},{64,96},{96,128},{128,160},{160,192},{192,224},{224... | collective-permute-start | bytes 442376 | tf_op jit(solution)/shard_map/ppermute | solution.py:371
  62.1 14.7 %collective-permute-start.5 = (bf16[288,256]{1,0:T(8,128)(2,1)}, bf16[288,256]{1,0:T(8,128)(2,1)}, u32[]{:S(2)}, u32[]{:S(2)}) collective-permute-start(bf16[288,256]{1,0:T(8,128)(2,1)} %get-tuple-element.30), channel_id=1, source_target_pairs={{32,0},{64,32},{96,64},{128,96},{160,128},{192,160},{224,192},{256... | collective-permute-start | bytes 442376 | tf_op jit(solution)/shard_map/ppermute | solution.py:371
  73.3 6.3 %collective-permute-start.3 = (f32[4,1024]{1,0:T(4,128)S(1)}, f32[4,1024]{1,0:T(4,128)S(1)}, u32[]{:S(2)}, u32[]{:S(2)}) collective-permute-start(f32[4,1024]{1,0:T(4,128)S(1)} %convert_reduce_fusion), channel_id=1, source_target_pairs={{1,1},{2,34},{0,67},{3,96},{5,133},{6,166},{4,199},{7,228},{9,265}... | collective-permute-start | bytes 49160 | tf_op jit(solution)/shard_map/ppermute | solution.py:408
  80.9 26.1 %all-to-all-start.2 = ((bf16[32,4,1024]{2,1,0:T(4,128)(2,1)}), bf16[32,4,1024]{2,1,0:T(4,128)(2,1)S(1)}, u32[]{:S(2)}, u32[]{:S(2)}) async-start(bf16[32,4,1024]{2,1,0:T(4,128)(2,1)} %shard_map.81), calls=%async_computation.2 | async-start | bytes 524288 | tf_op jit(solution)/shard_map/all_to_all | solution.py:411

commit v10 on v7

--- a/solution.py
+++ b/solution.py
@@ -403,10 +403,10 @@
     x_first, x_last = x_edges(fields, y_low, y_high)
     x_low = along(x_last, x_axes, 1)
     x_high = along(x_first, x_axes, -1)
-    pieces, x_low, x_high = lax.optimization_barrier((pieces, x_low, x_high))
 
     rows = jnp.sum(pieces.astype(F32), 0)
     rows = lax.ppermute(rows, ALL, SWAP)
+    rows, x_low, x_high = lax.optimization_barrier((rows, x_low, x_high))
     everyone = norm(who, rows, position, norm_gain)
     normed = lax.all_to_all(everyone, "mp", 0, 0, tiled=True)
 

time: 114 us -> 109 us (0.956)
  the two profiles are of different devices: /device:TPU:15 before, /device:TPU:64 now
where the time goes in v10:
time: 109 us; the launch traced here: 108 us
  starting transfers between devices  64.1 us (59%)
  waiting for transfers between devices  20.9 us (19%)
  Pallas kernels  19.1 us (18%)
  local copies, waits for them, and re-layouts  1.79 us (2%)
  other arithmetic  1.63 us (1%)
    all_to_all x1, starting transfers between devices, on_device(): patches = lax.all_to_all(pack(fields), 'mp', 0, 0, tiled=True)  19.9 us
    ppermute x4, starting transfers between devices, along(): return lax.ppermute(value, axes, pairs)  16.6 us
    all_to_all x1, starting transfers between devices, on_device(): normed = lax.all_to_all(everyone, 'mp', 0, 0, tiled=True)  15.5 us
    ppermute x4, waiting for transfers between devices, along(): return lax.ppermute(value, axes, pairs)  7.6 us
    all_to_all x1, starting transfers between devices, on_device(): pieces = lax.all_to_all(partial_sums, 'mp', 0, 0, tiled=True)  7.41 us
    pallas_call x1, Pallas kernels, advance(): pl.pallas_call(advance_kernel, in_specs=[pl.BlockSpec(memory_space=pltpu....  6.4 us
    all_to_all x1, waiting for transfers between devices, on_device(): normed = lax.all_to_all(everyone, 'mp', 0, 0, tiled=True)  5.54 us
    ppermute x1, waiting for transfers between devices, on_device(): rows = lax.ppermute(rows, ALL, SWAP)  3.26 us
  transfers between devices with their start and end apart: 9, of which 7 were waited for; matrix products, arithmetic and copies ran while one was open for 2% of the time, Pallas kernels for 10%

profile of v10, /device:TPU:64, one launch (start us, length us, event | category | flops | bytes accessed | tf_op | source)
XLA Modules:
  0.0 108.3 jit_solution(16209879757432854408)
XLA Ops:
  0.6 3.0 %shard_map.77 = bf16[32,16,512]{2,1,0:T(8,128)(2,1)} custom-call(f32[16,8,8,256]{3,2,1,0:T(8,128)} %fields_ref.3), custom_call_target="tpu_custom_call" | custom-call | flops 1000000 | bytes 2097152 | tf_op jit(solution)/shard_map/pallas_call | solution.py:72
  3.7 19.9 %all-to-all-start = ((bf16[32,16,512]{2,1,0:T(8,128)(2,1)}), bf16[32,16,512]{2,1,0:T(8,128)(2,1)S(1)}, u32[]{:S(2)}, u32[]{:S(2)}) async-start(bf16[32,16,512]{2,1,0:T(8,128)(2,1)} %shard_map.77), calls=%async_computation | async-start | bytes 1048576 | tf_op jit(solution)/shard_map/all_to_all | solution.py:385
  23.5 2.4 %shard_map.78 = (bf16[2,128,256]{2,1,0:T(8,128)(2,1)}, bf16[2,128,256]{2,1,0:T(8,128)(2,1)}) custom-call(f32[16,8,8,256]{3,2,1,0:T(8,128)} %fields_ref.3), custom_call_target="tpu_custom_call" | custom-call | flops 100000 | bytes 2097152 | tf_op jit(solution)/shard_map/pallas_call | solution.py:98
  25.9 3.7 %collective-permute-start = (bf16[2,128,256]{2,1,0:T(8,128)(2,1)}, bf16[2,128,256]{2,1,0:T(8,128)(2,1)S(1)}, u32[]{:S(2)}, u32[]{:S(2)}) collective-permute-start(bf16[2,128,256]{2,1,0:T(8,128)(2,1)} %get-tuple-element.20), channel_id=1, source_target_pairs={{0,1},{1,2},{2,3},{3,4},{4,5},{5,6},{6,7},{7,8},{8,9},{9,10},{10,1... | collective-permute-start | bytes 393224 | tf_op jit(solution)/shard_map/ppermute | solution.py:371
  29.6 1.3 %collective-permute-start.1 = (bf16[2,128,256]{2,1,0:T(8,128)(2,1)}, bf16[2,128,256]{2,1,0:T(8,128)(2,1)S(1)}, u32[]{:S(2)}, u32[]{:S(2)}) collective-permute-start(bf16[2,128,256]{2,1,0:T(8,128)(2,1)} %get-tuple-element.21), channel_id=1, source_target_pairs={{1,0},{2,1},{3,2},{4,3},{5,4},{6,5},{7,6},{8,7},{9,8},{10,9},{11,1... | collective-permute-start | bytes 393224 | tf_op jit(solution)/shard_map/ppermute | solution.py:371
  30.9 1.8 %constant_dynamic-slice_fusion = bf16[1024,1024]{1,0:T(8,128)(2,1)S(1)} fusion(bf16[2048,1024]{1,0:T(8,128)(2,1)} %param.8, s32[]{:T(128)S(6)} %select_n.3), kind=kLoop, calls=%fused_computation.4 | loop fusion | bytes 4194308 | tf_op jit(solution)/shard_map/dynamic_slice | solution.py:392
  32.7 0.1 pad_add_fusion.who_ref
  32.8 0.6 add_convert_fusion.1.edge_ref
  33.4 1.4 %collective-permute-done.y_low_ref.yl_ref = bf16[2,128,256]{2,1,0:T(8,128)(2,1)S(1)} collective-permute-done((bf16[2,128,256]{2,1,0:T(8,128)(2,1)}, bf16[2,128,256]{2,1,0:T(8,128)(2,1)S(1)}, u32[]{:S(2)}, u32[]{:S(2)}) %collective-permute-start) | collective-permute-done | bytes 131104 | tf_op jit(solution)/shard_map/ppermute | solution.py:371
  34.8 6.1 %collective-permute-done.1.y_high_ref.yh_ref = bf16[2,128,256]{2,1,0:T(8,128)(2,1)S(1)} collective-permute-done((bf16[2,128,256]{2,1,0:T(8,128)(2,1)}, bf16[2,128,256]{2,1,0:T(8,128)(2,1)S(1)}, u32[]{:S(2)}, u32[]{:S(2)}) %collective-permute-start.1) | collective-permute-done | bytes 131104 | tf_op jit(solution)/shard_map/ppermute | solution.py:371
  40.9 2.7 %all-to-all-done = bf16[32,16,512]{2,1,0:T(8,128)(2,1)S(1)} async-done(((bf16[32,16,512]{2,1,0:T(8,128)(2,1)}), bf16[32,16,512]{2,1,0:T(8,128)(2,1)S(1)}, u32[]{:S(2)}, u32[]{:S(2)}) %all-to-all-start) | async-done | bytes 524320 | tf_op jit(solution)/shard_map/all_to_all | solution.py:385
  43.6 2.0 %shard_map.79 = (f32[32,4,1024]{2,1,0:T(4,128)S(1)}, bf16[32,4,1024]{2,1,0:T(4,128)(2,1)}) custom-call(s32[2]{0:T(128)S(1)} %pad_add_fusion.who_ref, bf16[16,2,16,512]{3,2,1,0:T(8,128)(2,1)S(1)} %bitcast.10, bf16[2,512,1024]{2,1,0:T(8,128)(2,1)S(1)} %bitcast.9), custom_call_target="tpu_custom_call" | custom-call | flops 540000000 | bytes 3145728 | tf_op jit(solution)/shard_map/pallas_call | solution.py:178
  45.6 1.9 %collective-permute-start.2 = (bf16[32,4,1024]{2,1,0:T(4,128)(2,1)}, bf16[32,4,1024]{2,1,0:T(4,128)(2,1)S(1)}, u32[]{:S(2)}, u32[]{:S(2)}) collective-permute-start(bf16[32,4,1024]{2,1,0:T(4,128)(2,1)} %get-tuple-element.26), channel_id=1, source_target_pairs={{0,32},{32,0},{1,33},{33,1},{2,34},{34,2},{3,35},{35,3},{4,36},{36... | collective-permute-start | bytes 786440 | tf_op jit(solution)/shard_map/ppermute | solution.py:399
  47.6 1.7 %collective-permute-done.2 = bf16[32,4,1024]{2,1,0:T(4,128)(2,1)S(1)} collective-permute-done((bf16[32,4,1024]{2,1,0:T(4,128)(2,1)}, bf16[32,4,1024]{2,1,0:T(4,128)(2,1)S(1)}, u32[]{:S(2)}, u32[]{:S(2)}) %collective-permute-start.2) | collective-permute-done | bytes 262176 | tf_op jit(solution)/shard_map/ppermute | solution.py:399
  49.3 0.9 add_convert_fusion
  50.2 7.4 %all-to-all-start.1 = ((bf16[32,4,1024]{2,1,0:T(4,128)(2,1)}), bf16[32,4,1024]{2,1,0:T(4,128)(2,1)S(1)}, u32[]{:S(2)}, u32[]{:S(2)}) async-start(bf16[32,4,1024]{2,1,0:T(4,128)(2,1)} %add_convert_fusion), calls=%async_computation.1 | async-start | bytes 524288 | tf_op jit(solution)/shard_map/all_to_all | solution.py:401
  57.6 0.0 copy-start
  57.6 2.0 %shard_map.80 = (bf16[288,256]{1,0:T(8,128)(2,1)}, bf16[288,256]{1,0:T(8,128)(2,1)}) custom-call(f32[16,8,8,256]{3,2,1,0:T(8,128)} %fields_ref.3, f32[16,8,8,256]{3,2,1,0:T(8,128)} %fields_ref.3, bf16[2,128,256]{2,1,0:T(8,128)(2,1)} %copy-done.3, bf16[2,128,256]{2,1,0:T(8,128)(2,1)} %copy-done.4), custom_call_target="tpu_custom_call" | custom-call | flops 100000 | bytes 1048576 | tf_op jit(solution)/shard_map/pallas_call | solution.py:119
  59.6 1.9 %collective-permute-start.4 = (bf16[288,256]{1,0:T(8,128)(2,1)}, bf16[288,256]{1,0:T(8,128)(2,1)}, u32[]{:S(2)}, u32[]{:S(2)}) collective-permute-start(bf16[288,256]{1,0:T(8,128)(2,1)} %get-tuple-element.29), channel_id=1, source_target_pairs={{0,32},{32,64},{64,96},{96,128},{128,160},{160,192},{192,224},{224... | collective-permute-start | bytes 442376 | tf_op jit(solution)/shard_map/ppermute | solution.py:371
  61.5 9.7 %collective-permute-start.5 = (bf16[288,256]{1,0:T(8,128)(2,1)}, bf16[288,256]{1,0:T(8,128)(2,1)}, u32[]{:S(2)}, u32[]{:S(2)}) collective-permute-start(bf16[288,256]{1,0:T(8,128)(2,1)} %get-tuple-element.30), channel_id=1, source_target_pairs={{32,0},{64,32},{96,64},{128,96},{160,128},{192,160},{224,192},{256... | collective-permute-start | bytes 442376 | tf_op jit(solution)/shard_map/ppermute | solution.py:371
  71.2 0.0 all-to-all-done.1
  71.2 0.1 convert_reduce_fusion
  71.3 2.9 %collective-permute-start.3 = (f32[4,1024]{1,0:T(4,128)S(1)}, f32[4,1024]{1,0:T(4,128)S(1)}, u32[]{:S(2)}, u32[]{:S(2)}) collective-permute-start(f32[4,1024]{1,0:T(4,128)S(1)} %convert_reduce_fusion), channel_id=1, source_target_pairs={{1,1},{2,34},{0,67},{3,96},{5,133},{6,166},{4,199},{7,228},{9,265}... | collective-permute-start | bytes 49160 | tf_op jit(solution)/shard_map/ppermute | solution.py:408
  74.2 0.0 collective-permute-done.4.xl_ref
  74.3 0.1 collective-permute-done.5.xh_ref
  74.3 3.3 %collective-permute-done.3.rows_ref = f32[4,1024]{1,0:T(4,128)S(1)} collective-permute-done((f32[4,1024]{1,0:T(4,128)S(1)}, f32[4,1024]{1,0:T(4,128)S(1)}, u32[]{:S(2)}, u32[]{:S(2)}) %collective-permute-start.3) | collective-permute-done | bytes 16416 | tf_op jit(solution)/shard_map/ppermute | solution.py:408
  77.6 0.0 copy-done.2
  77.6 1.4 %shard_map.81 = bf16[32,4,1024]{2,1,0:T(4,128)(2,1)} custom-call(s32[2]{0:T(128)S(1)} %pad_add_fusion.who_ref, f32[4,1024]{1,0:T(4,128)S(1)} %collective-permute-done.3.rows_ref, bf16[128,1024]{1,0:T(8,128)(2,1)S(1)} %copy-done.1, f32[1,1024]{1,0:T(1,128)S(1)} %bitcast.11), custom_call_target="tpu_custom_call" | custom-call | flops 100000 | bytes 300000 | tf_op jit(solution)/shard_map/pallas_call | solution.py:206
  79.0 15.5 %all-to-all-start.2 = ((bf16[32,4,1024]{2,1,0:T(4,128)(2,1)}), bf16[32,4,1024]{2,1,0:T(4,128)(2,1)S(1)}, u32[]{:S(2)}, u32[]{:S(2)}) async-start(bf16[32,4,1024]{2,1,0:T(4,128)(2,1)} %shard_map.81), calls=%async_computation.2 | async-start | bytes 524288 | tf_op jit(solution)/shard_map/all_to_all | solution.py:411
  94.4 6.4 %shard_map.82 = f32[16,8,8,256]{3,2,1,0:T(8,128)} custom-call(f32[4]{0:T(128)} %add_convert_fusion.1.edge_ref, f32[16,8,8,256]{3,2,1,0:T(8,128)} %fields_ref.3, bf16[13,8,8,256]{3,2,1,0:T(8,128)(2,1)} %source_ref.1, bf16[2,128,256]{2,1,0:T(8,128)(2,1)} %copy-done.3, bf16[2,128,256]{2,1,0:T(8,128)(2,1)} %copy-done.4, ...), custom_call_target="tpu_custom_call" | custom-call | flops 100000000 | bytes 4194304 | tf_op jit(solution)/shard_map/pallas_call | solution.py:354
  100.8 5.5 %all-to-all-done.2.normed_ref = bf16[32,4,1024]{2,1,0:T(4,128)(2,1)S(1)} async-done(((bf16[32,4,1024]{2,1,0:T(4,128)(2,1)}), bf16[32,4,1024]{2,1,0:T(4,128)(2,1)S(1)}, u32[]{:S(2)}, u32[]{:S(2)}) %all-to-all-start.2) | async-done | bytes 262176 | tf_op jit(solution)/shard_map/all_to_all | solution.py:411
  106.4 1.9 %shard_map.83 = bf16[128,1408]{1,0:T(8,128)(2,1)} custom-call(s32[2]{0:T(128)S(1)} %pad_add_fusion.who_ref, bf16[32,4,1024]{2,1,0:T(4,128)(2,1)S(1)} %all-to-all-done.2.normed_ref, bf16[1024,1408]{1,0:T(8,128)(2,1)S(1)} %copy-done), custom_call_target="tpu_custom_call" | custom-call | flops 370000000 | bytes 4194304 | tf_op jit(solution)/shard_map/pallas_call | solution.py:247
  (8 shorter events, 0.0 us)
Async XLA Ops:
  3.7 40.0 %all-to-all-start = ((bf16[32,16,512]{2,1,0:T(8,128)(2,1)}), bf16[32,16,512]{2,1,0:T(8,128)(2,1)S(1)}, u32[]{:S(2)}, u32[]{:S(2)}) async-start(bf16[32,16,512]{2,1,0:T(8,128)(2,1)} %shard_map.77), calls=%async_computation | async-start | bytes 1048576 | tf_op jit(solution)/shard_map/all_to_all | solution.py:385
  25.9 8.9 %collective-permute-start = (bf16[2,128,256]{2,1,0:T(8,128)(2,1)}, bf16[2,128,256]{2,1,0:T(8,128)(2,1)S(1)}, u32[]{:S(2)}, u32[]{:S(2)}) collective-permute-start(bf16[2,128,256]{2,1,0:T(8,128)(2,1)} %get-tuple-element.20), channel_id=1, source_target_pairs={{0,1},{1,2},{2,3},{3,4},{4,5},{5,6},{6,7},{7,8},{8,9},{9,10},{10,1... | collective-permute-start | bytes 393224 | tf_op jit(solution)/shard_map/ppermute | solution.py:371
  29.6 11.2 %collective-permute-start.1 = (bf16[2,128,256]{2,1,0:T(8,128)(2,1)}, bf16[2,128,256]{2,1,0:T(8,128)(2,1)S(1)}, u32[]{:S(2)}, u32[]{:S(2)}) collective-permute-start(bf16[2,128,256]{2,1,0:T(8,128)(2,1)} %get-tuple-element.21), channel_id=1, source_target_pairs={{1,0},{2,1},{3,2},{4,3},{5,4},{6,5},{7,6},{8,7},{9,8},{10,9},{11,1... | collective-permute-start | bytes 393224 | tf_op jit(solution)/shard_map/ppermute | solution.py:371
  34.8 22.8 %copy-start.3 = (bf16[2,128,256]{2,1,0:T(8,128)(2,1)}, bf16[2,128,256]{2,1,0:T(8,128)(2,1)S(1)}, u32[]{:S(2)}) copy-start(bf16[2,128,256]{2,1,0:T(8,128)(2,1)S(1)} %collective-permute-done.y_low_ref.yl_ref) | copy-start | bytes 393220
  40.9 2.7 %copy-start.4 = (bf16[2,128,256]{2,1,0:T(8,128)(2,1)}, bf16[2,128,256]{2,1,0:T(8,128)(2,1)S(1)}, u32[]{:S(2)}) copy-start(bf16[2,128,256]{2,1,0:T(8,128)(2,1)S(1)} %collective-permute-done.1.y_high_ref.yh_ref) | copy-start | bytes 393220
  43.6 34.0 %copy-start.1 = (bf16[128,1024]{1,0:T(8,128)(2,1)S(1)}, bf16[128,1024]{1,0:T(8,128)(2,1)}, u32[]{:S(2)}) copy-start(bf16[128,1024]{1,0:T(8,128)(2,1)} %position_ref.1) | copy-start | bytes 786436
  43.6 34.0 %copy-start.2 = (f32[1024]{0:T(1024)S(1)}, f32[1024]{0:T(1024)}, u32[]{:S(2)}) copy-start(f32[1024]{0:T(1024)} %param.10) | copy-start | bytes 12292
  45.6 3.6 %collective-permute-start.2 = (bf16[32,4,1024]{2,1,0:T(4,128)(2,1)}, bf16[32,4,1024]{2,1,0:T(4,128)(2,1)S(1)}, u32[]{:S(2)}, u32[]{:S(2)}) collective-permute-start(bf16[32,4,1024]{2,1,0:T(4,128)(2,1)} %get-tuple-element.26), channel_id=1, source_target_pairs={{0,32},{32,0},{1,33},{33,1},{2,34},{34,2},{3,35},{35,3},{4,36},{36... | collective-permute-start | bytes 786440 | tf_op jit(solution)/shard_map/ppermute | solution.py:399
  50.2 21.0 %all-to-all-start.1 = ((bf16[32,4,1024]{2,1,0:T(4,128)(2,1)}), bf16[32,4,1024]{2,1,0:T(4,128)(2,1)S(1)}, u32[]{:S(2)}, u32[]{:S(2)}) async-start(bf16[32,4,1024]{2,1,0:T(4,128)(2,1)} %add_convert_fusion), calls=%async_computation.1 | async-start | bytes 524288 | tf_op jit(solution)/shard_map/all_to_all | solution.py:401
  57.6 48.8 %copy-start = (bf16[1024,1408]{1,0:T(8,128)(2,1)S(1)}, bf16[1024,1408]{1,0:T(8,128)(2,1)}, u32[]{:S(2)}) copy-start(bf16[1024,1408]{1,0:T(8,128)(2,1)} %weight_ref.1) | copy-start | bytes 8650756
  59.6 14.6 %collective-permute-start.4 = (bf16[288,256]{1,0:T(8,128)(2,1)}, bf16[288,256]{1,0:T(8,128)(2,1)}, u32[]{:S(2)}, u32[]{:S(2)}) collective-permute-start(bf16[288,256]{1,0:T(8,128)(2,1)} %get-tuple-element.29), channel_id=1, source_target_pairs={{0,32},{32,64},{64,96},{96,128},{128,160},{160,192},{192,224},{224... | collective-permute-start | bytes 442376 | tf_op jit(solution)/shard_map/ppermute | solution.py:371
  61.5 12.8 %collective-permute-start.5 = (bf16[288,256]{1,0:T(8,128)(2,1)}, bf16[288,256]{1,0:T(8,128)(2,1)}, u32[]{:S(2)}, u32[]{:S(2)}) collective-permute-start(bf16[288,256]{1,0:T(8,128)(2,1)} %get-tuple-element.30), channel_id=1, source_target_pairs={{32,0},{64,32},{96,64},{128,96},{160,128},{192,160},{224,192},{256... | collective-permute-start | bytes 442376 | tf_op jit(solution)/shard_map/ppermute | solution.py:371
  71.3 6.3 %collective-permute-start.3 = (f32[4,1024]{1,0:T(4,128)S(1)}, f32[4,1024]{1,0:T(4,128)S(1)}, u32[]{:S(2)}, u32[]{:S(2)}) collective-permute-start(f32[4,1024]{1,0:T(4,128)S(1)} %convert_reduce_fusion), channel_id=1, source_target_pairs={{1,1},{2,34},{0,67},{3,96},{5,133},{6,166},{4,199},{7,228},{9,265}... | collective-permute-start | bytes 49160 | tf_op jit(solution)/shard_map/ppermute | solution.py:408
  79.0 27.4 %all-to-all-start.2 = ((bf16[32,4,1024]{2,1,0:T(4,128)(2,1)}), bf16[32,4,1024]{2,1,0:T(4,128)(2,1)S(1)}, u32[]{:S(2)}, u32[]{:S(2)}) async-start(bf16[32,4,1024]{2,1,0:T(4,128)(2,1)} %shard_map.81), calls=%async_computation.2 | async-start | bytes 524288 | tf_op jit(solution)/shard_map/all_to_all | solution.py:411

commit v11 on v10

--- a/solution.py
+++ b/solution.py
@@ -401,12 +401,17 @@
     pieces = lax.all_to_all(partial_sums, "mp", 0, 0, tiled=True)
 
     x_first, x_last = x_edges(fields, y_low, y_high)
-    x_low = along(x_last, x_axes, 1)
-    x_high = along(x_first, x_axes, -1)
+    first_core = core == 0
+    far = [(i, i + 1) for i in range(1, 31, 2)]
+    far = far + [(j, i) for i, j in far]
+    from_far = lax.ppermute(jnp.where(first_core, x_first, x_last), x_axes, far)
+    from_near = lax.ppermute(jnp.where(first_core, x_last, x_first), "core", [(0, 1), (1, 0)])
 
     rows = jnp.sum(pieces.astype(F32), 0)
     rows = lax.ppermute(rows, ALL, SWAP)
-    rows, x_low, x_high = lax.optimization_barrier((rows, x_low, x_high))
+    rows, from_far, from_near = lax.optimization_barrier((rows, from_far, from_near))
+    x_low = jnp.where(first_core, from_far, from_near)
+    x_high = jnp.where(first_core, from_near, from_far)
     everyone = norm(who, rows, position, norm_gain)
     normed = lax.all_to_all(everyone, "mp", 0, 0, tiled=True)
 

time: 109 us -> 108 us (level)
  the two profiles are of different devices: /device:TPU:64 before, /device:TPU:15 now
where the time goes in v11:
time: 108 us; the launch traced here: 106 us
  starting transfers between devices  62.1 us (58%)
  Pallas kernels  19.1 us (18%)
  waiting for transfers between devices  16.8 us (16%)
  other arithmetic  5.28 us (5%)
  local copies, waits for them, and re-layouts  1.79 us (2%)
    all_to_all x1, starting transfers between devices, on_device(): patches = lax.all_to_all(pack(fields), 'mp', 0, 0, tiled=True)  19.5 us
    all_to_all x1, starting transfers between devices, on_device(): normed = lax.all_to_all(everyone, 'mp', 0, 0, tiled=True)  11.8 us
    all_to_all x1, starting transfers between devices, on_device(): pieces = lax.all_to_all(partial_sums, 'mp', 0, 0, tiled=True)  8.74 us
    ppermute x1, waiting for transfers between devices, on_device(): from_far = lax.ppermute(jnp.where(first_core, x_first, x_last), x_axes, far)  6.86 us
    pallas_call x1, Pallas kernels, advance(): pl.pallas_call(advance_kernel, in_specs=[pl.BlockSpec(memory_space=pltpu....  6.45 us
    ppermute x1, starting transfers between devices, on_device(): from_far = lax.ppermute(jnp.where(first_core, x_first, x_last), x_axes, far)  5.8 us
    ppermute x2, starting transfers between devices, along(): return lax.ppermute(value, axes, pairs)  5.27 us
    ppermute x2, waiting for transfers between devices, along(): return lax.ppermute(value, axes, pairs)  5.12 us
  transfers between devices with their start and end apart: 9, of which 6 were waited for; matrix products, arithmetic and copies ran while one was open for 6% of the time, Pallas kernels for 10%

profile of v11, /device:TPU:15, one launch (start us, length us, event | category | flops | bytes accessed | tf_op | source)
XLA Modules:
  0.0 105.8 jit_solution(7277572654002548765)
XLA Ops:
  0.6 3.0 %shard_map.77 = bf16[32,16,512]{2,1,0:T(8,128)(2,1)} custom-call(f32[16,8,8,256]{3,2,1,0:T(8,128)} %fields_ref.3), custom_call_target="tpu_custom_call" | custom-call | flops 1000000 | bytes 2097152 | tf_op jit(solution)/shard_map/pallas_call | solution.py:72
  3.7 19.5 %all-to-all-start = ((bf16[32,16,512]{2,1,0:T(8,128)(2,1)}), bf16[32,16,512]{2,1,0:T(8,128)(2,1)S(1)}, u32[]{:S(2)}, u32[]{:S(2)}) async-start(bf16[32,16,512]{2,1,0:T(8,128)(2,1)} %shard_map.77), calls=%async_computation | async-start | bytes 1048576 | tf_op jit(solution)/shard_map/all_to_all | solution.py:385
  23.2 2.4 %shard_map.78 = (bf16[2,128,256]{2,1,0:T(8,128)(2,1)}, bf16[2,128,256]{2,1,0:T(8,128)(2,1)}) custom-call(f32[16,8,8,256]{3,2,1,0:T(8,128)} %fields_ref.3), custom_call_target="tpu_custom_call" | custom-call | flops 100000 | bytes 2097152 | tf_op jit(solution)/shard_map/pallas_call | solution.py:98
  25.6 3.1 %collective-permute-start = (bf16[2,128,256]{2,1,0:T(8,128)(2,1)}, bf16[2,128,256]{2,1,0:T(8,128)(2,1)S(1)}, u32[]{:S(2)}, u32[]{:S(2)}) collective-permute-start(bf16[2,128,256]{2,1,0:T(8,128)(2,1)} %get-tuple-element.20), channel_id=1, source_target_pairs={{0,1},{1,2},{2,3},{3,4},{4,5},{5,6},{6,7},{7,8},{8,9},{9,10},{10,1... | collective-permute-start | bytes 393224 | tf_op jit(solution)/shard_map/ppermute | solution.py:371
  28.7 2.2 %collective-permute-start.1 = (bf16[2,128,256]{2,1,0:T(8,128)(2,1)}, bf16[2,128,256]{2,1,0:T(8,128)(2,1)S(1)}, u32[]{:S(2)}, u32[]{:S(2)}) collective-permute-start(bf16[2,128,256]{2,1,0:T(8,128)(2,1)} %get-tuple-element.21), channel_id=1, source_target_pairs={{1,0},{2,1},{3,2},{4,3},{5,4},{6,5},{7,6},{8,7},{9,8},{10,9},{11,1... | collective-permute-start | bytes 393224 | tf_op jit(solution)/shard_map/ppermute | solution.py:371
  30.9 1.8 %constant_dynamic-slice_fusion = bf16[1024,1024]{1,0:T(8,128)(2,1)S(1)} fusion(bf16[2048,1024]{1,0:T(8,128)(2,1)} %param.8, s32[]{:T(128)S(6)} %select_n.23), kind=kLoop, calls=%fused_computation.8 | loop fusion | bytes 4194308 | tf_op jit(solution)/shard_map/dynamic_slice | solution.py:392
  32.7 0.1 pad_add_fusion.who_ref
  32.8 0.7 add_convert_fusion.1.edge_ref
  33.4 1.3 %collective-permute-done.y_low_ref.yl_ref = bf16[2,128,256]{2,1,0:T(8,128)(2,1)S(1)} collective-permute-done((bf16[2,128,256]{2,1,0:T(8,128)(2,1)}, bf16[2,128,256]{2,1,0:T(8,128)(2,1)S(1)}, u32[]{:S(2)}, u32[]{:S(2)}) %collective-permute-start) | collective-permute-done | bytes 131104 | tf_op jit(solution)/shard_map/ppermute | solution.py:371
  34.7 3.8 %collective-permute-done.1.y_high_ref.yh_ref = bf16[2,128,256]{2,1,0:T(8,128)(2,1)S(1)} collective-permute-done((bf16[2,128,256]{2,1,0:T(8,128)(2,1)}, bf16[2,128,256]{2,1,0:T(8,128)(2,1)S(1)}, u32[]{:S(2)}, u32[]{:S(2)}) %collective-permute-start.1) | collective-permute-done | bytes 131104 | tf_op jit(solution)/shard_map/ppermute | solution.py:371
  38.5 0.5 all-to-all-done
  39.0 2.0 %shard_map.79 = (f32[32,4,1024]{2,1,0:T(4,128)S(1)}, bf16[32,4,1024]{2,1,0:T(4,128)(2,1)}) custom-call(s32[2]{0:T(128)S(1)} %pad_add_fusion.who_ref, bf16[16,2,16,512]{3,2,1,0:T(8,128)(2,1)S(1)} %bitcast.10, bf16[2,512,1024]{2,1,0:T(8,128)(2,1)S(1)} %bitcast.9), custom_call_target="tpu_custom_call" | custom-call | flops 540000000 | bytes 3145728 | tf_op jit(solution)/shard_map/pallas_call | solution.py:178
  41.0 0.0 copy-start.1
  41.0 0.0 copy-start.2
  41.1 5.0 %collective-permute-start.2 = (bf16[32,4,1024]{2,1,0:T(4,128)(2,1)}, bf16[32,4,1024]{2,1,0:T(4,128)(2,1)S(1)}, u32[]{:S(2)}, u32[]{:S(2)}) collective-permute-start(bf16[32,4,1024]{2,1,0:T(4,128)(2,1)} %get-tuple-element.26), channel_id=1, source_target_pairs={{0,32},{32,0},{1,33},{33,1},{2,34},{34,2},{3,35},{35,3},{4,36},{36... | collective-permute-start | bytes 786440 | tf_op jit(solution)/shard_map/ppermute | solution.py:399
  46.1 1.4 %collective-permute-done.2 = bf16[32,4,1024]{2,1,0:T(4,128)(2,1)S(1)} collective-permute-done((bf16[32,4,1024]{2,1,0:T(4,128)(2,1)}, bf16[32,4,1024]{2,1,0:T(4,128)(2,1)S(1)}, u32[]{:S(2)}, u32[]{:S(2)}) %collective-permute-start.2) | collective-permute-done | bytes 262176 | tf_op jit(solution)/shard_map/ppermute | solution.py:399
  47.4 0.9 add_convert_fusion
  48.3 8.7 %all-to-all-start.1 = ((bf16[32,4,1024]{2,1,0:T(4,128)(2,1)}), bf16[32,4,1024]{2,1,0:T(4,128)(2,1)S(1)}, u32[]{:S(2)}, u32[]{:S(2)}) async-start(bf16[32,4,1024]{2,1,0:T(4,128)(2,1)} %add_convert_fusion), calls=%async_computation.1 | async-start | bytes 524288 | tf_op jit(solution)/shard_map/all_to_all | solution.py:401
  57.1 1.9 %shard_map.80 = (bf16[288,256]{1,0:T(8,128)(2,1)}, bf16[288,256]{1,0:T(8,128)(2,1)}) custom-call(f32[16,8,8,256]{3,2,1,0:T(8,128)} %fields_ref.3, f32[16,8,8,256]{3,2,1,0:T(8,128)} %fields_ref.3, bf16[2,128,256]{2,1,0:T(8,128)(2,1)} %copy-done.3, bf16[2,128,256]{2,1,0:T(8,128)(2,1)} %copy-done.4), custom_call_target="tpu_custom_call" | custom-call | flops 100000 | bytes 1048576 | tf_op jit(solution)/shard_map/pallas_call | solution.py:119
  58.9 1.9 %broadcast_select_fusion.2 = (bf16[288,256]{1,0:T(8,128)(2,1)}, bf16[288,256]{1,0:T(8,128)(2,1)}) fusion(bf16[288,256]{1,0:T(8,128)(2,1)} %get-tuple-element.30, bf16[288,256]{1,0:T(8,128)(2,1)} %get-tuple-element.29, pred[]{:T(512)S(6)} %eq.3), kind=kLoop, calls=%fused_computation.4 | loop fusion | flops 147456 | bytes 589825 | tf_op jit(solution)/shard_map/jit(_where)/select_n | solution.py:408
  60.8 2.8 %collective-permute-start.5 = (bf16[288,256]{1,0:T(8,128)(2,1)}, bf16[288,256]{1,0:T(8,128)(2,1)}, u32[]{:S(2)}, u32[]{:S(2)}) collective-permute-start(bf16[288,256]{1,0:T(8,128)(2,1)} %get-tuple-element.40), channel_id=1, source_target_pairs={{0,32},{32,0},{1,33},{33,1},{2,34},{34,2},{3,35},{35,3},{4,36},{36... | collective-permute-start | bytes 442376 | tf_op jit(solution)/shard_map/ppermute | solution.py:408
  63.6 5.8 %collective-permute-start.4 = (bf16[288,256]{1,0:T(8,128)(2,1)}, bf16[288,256]{1,0:T(8,128)(2,1)}, u32[]{:S(2)}, u32[]{:S(2)}) collective-permute-start(bf16[288,256]{1,0:T(8,128)(2,1)} %get-tuple-element.41), channel_id=1, source_target_pairs={{32,64},{96,128},{160,192},{224,256},{288,320},{352,384},{416,448}... | collective-permute-start | bytes 442376 | tf_op jit(solution)/shard_map/ppermute | solution.py:407
  69.4 0.0 all-to-all-done.1
  69.5 0.1 convert_reduce_fusion
  69.6 3.1 %collective-permute-start.3 = (f32[4,1024]{1,0:T(4,128)S(1)}, f32[4,1024]{1,0:T(4,128)S(1)}, u32[]{:S(2)}, u32[]{:S(2)}) collective-permute-start(f32[4,1024]{1,0:T(4,128)S(1)} %convert_reduce_fusion), channel_id=1, source_target_pairs={{1,1},{2,34},{0,67},{3,96},{5,133},{6,166},{4,199},{7,228},{9,265}... | collective-permute-start | bytes 49160 | tf_op jit(solution)/shard_map/ppermute | solution.py:411
  72.7 6.9 %collective-permute-done.4 = bf16[288,256]{1,0:T(8,128)(2,1)} collective-permute-done((bf16[288,256]{1,0:T(8,128)(2,1)}, bf16[288,256]{1,0:T(8,128)(2,1)}, u32[]{:S(2)}, u32[]{:S(2)}) %collective-permute-start.4) | collective-permute-done | bytes 147488 | tf_op jit(solution)/shard_map/ppermute | solution.py:407
  79.6 1.4 %shard_map.81 = bf16[32,4,1024]{2,1,0:T(4,128)(2,1)} custom-call(s32[2]{0:T(128)S(1)} %pad_add_fusion.who_ref, f32[4,1024]{1,0:T(4,128)S(1)} %collective-permute-done.3.rows_ref, bf16[128,1024]{1,0:T(8,128)(2,1)S(1)} %copy-done.1, f32[1,1024]{1,0:T(1,128)S(1)} %bitcast.11), custom_call_target="tpu_custom_call" | custom-call | flops 100000 | bytes 300000 | tf_op jit(solution)/shard_map/pallas_call | solution.py:206
  80.9 11.8 %all-to-all-start.2 = ((bf16[32,4,1024]{2,1,0:T(4,128)(2,1)}), bf16[32,4,1024]{2,1,0:T(4,128)(2,1)S(1)}, u32[]{:S(2)}, u32[]{:S(2)}) async-start(bf16[32,4,1024]{2,1,0:T(4,128)(2,1)} %shard_map.81), calls=%async_computation.2 | async-start | bytes 524288 | tf_op jit(solution)/shard_map/all_to_all | solution.py:416
  92.8 1.7 %broadcast_select_fusion = (bf16[288,256]{1,0:T(8,128)(2,1)}, bf16[288,256]{1,0:T(8,128)(2,1)}) fusion(bf16[288,256]{1,0:T(8,128)(2,1)} %collective-permute-done.5, bf16[288,256]{1,0:T(8,128)(2,1)} %collective-permute-done.4, pred[]{:T(512)S(6)} %eq.3), kind=kLoop, calls=%fused_computation.2 | loop fusion | flops 147456 | bytes 589825 | tf_op jit(solution)/shard_map/jit(_where)/select_n | solution.py:414
  94.5 6.4 %shard_map.82 = f32[16,8,8,256]{3,2,1,0:T(8,128)} custom-call(f32[4]{0:T(128)} %add_convert_fusion.1.edge_ref, f32[16,8,8,256]{3,2,1,0:T(8,128)} %fields_ref.3, bf16[13,8,8,256]{3,2,1,0:T(8,128)(2,1)} %source_ref.1, bf16[2,128,256]{2,1,0:T(8,128)(2,1)} %copy-done.3, bf16[2,128,256]{2,1,0:T(8,128)(2,1)} %copy-done.4, ...), custom_call_target="tpu_custom_call" | custom-call | flops 100000000 | bytes 4194304 | tf_op jit(solution)/shard_map/pallas_call | solution.py:354
  100.9 3.0 %all-to-all-done.2.normed_ref = bf16[32,4,1024]{2,1,0:T(4,128)(2,1)S(1)} async-done(((bf16[32,4,1024]{2,1,0:T(4,128)(2,1)}), bf16[32,4,1024]{2,1,0:T(4,128)(2,1)S(1)}, u32[]{:S(2)}, u32[]{:S(2)}) %all-to-all-start.2) | async-done | bytes 262176 | tf_op jit(solution)/shard_map/all_to_all | solution.py:416
  103.9 1.9 %shard_map.83 = bf16[128,1408]{1,0:T(8,128)(2,1)} custom-call(s32[2]{0:T(128)S(1)} %pad_add_fusion.who_ref, bf16[32,4,1024]{2,1,0:T(4,128)(2,1)S(1)} %all-to-all-done.2.normed_ref, bf16[1024,1408]{1,0:T(8,128)(2,1)S(1)} %copy-done), custom_call_target="tpu_custom_call" | custom-call | flops 370000000 | bytes 4194304 | tf_op jit(solution)/shard_map/pallas_call | solution.py:247
  (10 shorter events, 0.0 us)
Async XLA Ops:
  3.7 35.3 %all-to-all-start = ((bf16[32,16,512]{2,1,0:T(8,128)(2,1)}), bf16[32,16,512]{2,1,0:T(8,128)(2,1)S(1)}, u32[]{:S(2)}, u32[]{:S(2)}) async-start(bf16[32,16,512]{2,1,0:T(8,128)(2,1)} %shard_map.77), calls=%async_computation | async-start | bytes 1048576 | tf_op jit(solution)/shard_map/all_to_all | solution.py:385
  25.6 9.1 %collective-permute-start = (bf16[2,128,256]{2,1,0:T(8,128)(2,1)}, bf16[2,128,256]{2,1,0:T(8,128)(2,1)S(1)}, u32[]{:S(2)}, u32[]{:S(2)}) collective-permute-start(bf16[2,128,256]{2,1,0:T(8,128)(2,1)} %get-tuple-element.20), channel_id=1, source_target_pairs={{0,1},{1,2},{2,3},{3,4},{4,5},{5,6},{6,7},{7,8},{8,9},{9,10},{10,1... | collective-permute-start | bytes 393224 | tf_op jit(solution)/shard_map/ppermute | solution.py:371
  28.7 9.8 %collective-permute-start.1 = (bf16[2,128,256]{2,1,0:T(8,128)(2,1)}, bf16[2,128,256]{2,1,0:T(8,128)(2,1)S(1)}, u32[]{:S(2)}, u32[]{:S(2)}) collective-permute-start(bf16[2,128,256]{2,1,0:T(8,128)(2,1)} %get-tuple-element.21), channel_id=1, source_target_pairs={{1,0},{2,1},{3,2},{4,3},{5,4},{6,5},{7,6},{8,7},{9,8},{10,9},{11,1... | collective-permute-start | bytes 393224 | tf_op jit(solution)/shard_map/ppermute | solution.py:371
  34.7 22.3 %copy-start.3 = (bf16[2,128,256]{2,1,0:T(8,128)(2,1)}, bf16[2,128,256]{2,1,0:T(8,128)(2,1)S(1)}, u32[]{:S(2)}) copy-start(bf16[2,128,256]{2,1,0:T(8,128)(2,1)S(1)} %collective-permute-done.y_low_ref.yl_ref) | copy-start | bytes 393220
  38.5 18.5 %copy-start.4 = (bf16[2,128,256]{2,1,0:T(8,128)(2,1)}, bf16[2,128,256]{2,1,0:T(8,128)(2,1)S(1)}, u32[]{:S(2)}) copy-start(bf16[2,128,256]{2,1,0:T(8,128)(2,1)S(1)} %collective-permute-done.1.y_high_ref.yh_ref) | copy-start | bytes 393220
  41.0 38.5 %copy-start.1 = (bf16[128,1024]{1,0:T(8,128)(2,1)S(1)}, bf16[128,1024]{1,0:T(8,128)(2,1)}, u32[]{:S(2)}) copy-start(bf16[128,1024]{1,0:T(8,128)(2,1)} %position_ref.1) | copy-start | bytes 786436
  41.0 38.5 %copy-start.2 = (f32[1024]{0:T(1024)S(1)}, f32[1024]{0:T(1024)}, u32[]{:S(2)}) copy-start(f32[1024]{0:T(1024)} %param.10) | copy-start | bytes 12292
  41.1 6.4 %collective-permute-start.2 = (bf16[32,4,1024]{2,1,0:T(4,128)(2,1)}, bf16[32,4,1024]{2,1,0:T(4,128)(2,1)S(1)}, u32[]{:S(2)}, u32[]{:S(2)}) collective-permute-start(bf16[32,4,1024]{2,1,0:T(4,128)(2,1)} %get-tuple-element.26), channel_id=1, source_target_pairs={{0,32},{32,0},{1,33},{33,1},{2,34},{34,2},{3,35},{35,3},{4,36},{36... | collective-permute-start | bytes 786440 | tf_op jit(solution)/shard_map/ppermute | solution.py:399
  48.3 21.2 %all-to-all-start.1 = ((bf16[32,4,1024]{2,1,0:T(4,128)(2,1)}), bf16[32,4,1024]{2,1,0:T(4,128)(2,1)S(1)}, u32[]{:S(2)}, u32[]{:S(2)}) async-start(bf16[32,4,1024]{2,1,0:T(4,128)(2,1)} %add_convert_fusion), calls=%async_computation.1 | async-start | bytes 524288 | tf_op jit(solution)/shard_map/all_to_all | solution.py:401
  58.9 44.9 %copy-start = (bf16[1024,1408]{1,0:T(8,128)(2,1)S(1)}, bf16[1024,1408]{1,0:T(8,128)(2,1)}, u32[]{:S(2)}) copy-start(bf16[1024,1408]{1,0:T(8,128)(2,1)} %weight_ref.1) | copy-start | bytes 8650756
  60.8 11.9 %collective-permute-start.5 = (bf16[288,256]{1,0:T(8,128)(2,1)}, bf16[288,256]{1,0:T(8,128)(2,1)}, u32[]{:S(2)}, u32[]{:S(2)}) collective-permute-start(bf16[288,256]{1,0:T(8,128)(2,1)} %get-tuple-element.40), channel_id=1, source_target_pairs={{0,32},{32,0},{1,33},{33,1},{2,34},{34,2},{3,35},{35,3},{4,36},{36... | collective-permute-start | bytes 442376 | tf_op jit(solution)/shard_map/ppermute | solution.py:408
  63.6 15.9 %collective-permute-start.4 = (bf16[288,256]{1,0:T(8,128)(2,1)}, bf16[288,256]{1,0:T(8,128)(2,1)}, u32[]{:S(2)}, u32[]{:S(2)}) collective-permute-start(bf16[288,256]{1,0:T(8,128)(2,1)} %get-tuple-element.41), channel_id=1, source_target_pairs={{32,64},{96,128},{160,192},{224,256},{288,320},{352,384},{416,448}... | collective-permute-start | bytes 442376 | tf_op jit(solution)/shard_map/ppermute | solution.py:407
  69.6 10.0 %collective-permute-start.3 = (f32[4,1024]{1,0:T(4,128)S(1)}, f32[4,1024]{1,0:T(4,128)S(1)}, u32[]{:S(2)}, u32[]{:S(2)}) collective-permute-start(f32[4,1024]{1,0:T(4,128)S(1)} %convert_reduce_fusion), channel_id=1, source_target_pairs={{1,1},{2,34},{0,67},{3,96},{5,133},{6,166},{4,199},{7,228},{9,265}... | collective-permute-start | bytes 49160 | tf_op jit(solution)/shard_map/ppermute | solution.py:411
  80.9 22.9 %all-to-all-start.2 = ((bf16[32,4,1024]{2,1,0:T(4,128)(2,1)}), bf16[32,4,1024]{2,1,0:T(4,128)(2,1)S(1)}, u32[]{:S(2)}, u32[]{:S(2)}) async-start(bf16[32,4,1024]{2,1,0:T(4,128)(2,1)} %shard_map.81), calls=%async_computation.2 | async-start | bytes 524288 | tf_op jit(solution)/shard_map/all_to_all | solution.py:416
